TPU v7x, 32 devices: a whole 2x2x4 slice. The times are simulated.
32 devices in a mesh: dp: 4 (over x, core), fsdp: 8 (over z, y).
Axes of the slice: x: 2, y: 2, z: 4, core: 2. Of those that a mesh axis runs over, the one named last changes fastest.
Arguments:
- token_ids: int32 [2, 128, 128], P(None, ('dp', 'fsdp')), may hold values from 0 to 30719
- valid_mask: int32 [2, 128, 128], P(None, ('dp', 'fsdp')), may hold values from 0 to 1, as said below
- seq_ids: int32 [2, 128, 128], P(None, ('dp', 'fsdp')), may hold values from 0 to 3, never falling along the last dimension, each value on 1 to 64 neighbouring positions
- mask_pos: int32 [2, 128, 20], P(None, ('dp', 'fsdp')), may hold values from 0 to 127, as said below
- mask_labels: int32 [2, 128, 20], P(None, ('dp', 'fsdp')), may hold values from 0 to 30719
- teacher_in: bfloat16 [2, 128, 128, 768], P(None, ('dp', 'fsdp')), may hold values from -6 to 6
- teacher_flat: bfloat16 [7077888], P(('dp', 'fsdp'))
- teacher_vec: bfloat16 [9984], replicated
- teacher_head: bfloat16 [30720, 768], P('fsdp')
- emb_table: float32 [30720, 312], P(('dp', 'fsdp'))
- emb_first: float32 [30720, 312], P(('dp', 'fsdp')), may hold values from -9.536743e-06 to 9.536743e-06
- emb_second: float32 [30720, 312], P(('dp', 'fsdp')), may hold values from 2.057727e-13 to 8.230908e-13
- pos_table: float32 [128, 312], P(('dp', 'fsdp')), may hold values from -6 to 6
- pos_first: float32 [128, 312], P(('dp', 'fsdp')), may hold values from -9.536743e-06 to 9.536743e-06
- pos_second: float32 [128, 312], P(('dp', 'fsdp')), may hold values from 2.057727e-13 to 8.230908e-13
- layer_flat: float32 [2, 1138176], P(None, ('dp', 'fsdp'))
- layer_first: float32 [2, 1138176], P(None, ('dp', 'fsdp')), may hold values from -9.536743e-06 to 9.536743e-06
- layer_second: float32 [2, 1138176], P(None, ('dp', 'fsdp')), may hold values from 2.057727e-13 to 8.230908e-13
- proj_weight: float32 [312, 768], P(None, ('dp', 'fsdp')), may hold values from -0.3125 to 0.3125
- proj_first: float32 [312, 768], P(None, ('dp', 'fsdp')), may hold values from -9.536743e-06 to 9.536743e-06
- proj_second: float32 [312, 768], P(None, ('dp', 'fsdp')), may hold values from 2.057727e-13 to 8.230908e-13
- layer_vec: float32 [2, 3696], replicated
- vec_first: float32 [2, 3696], replicated, may hold values from -3.8146973e-05 to 3.8146973e-05
- vec_second: float32 [2, 3696], replicated, may hold values from 3.2923631e-12 to 1.31694525e-11
- misc_vec: float32 [1392], replicated
- misc_first: float32 [1392], replicated, may hold values from -3.8146973e-05 to 3.8146973e-05
- misc_second: float32 [1392], replicated, may hold values from 3.2923631e-12 to 1.31694525e-11
Outputs:
- loss: float32 [], replicated
- pair_count: float32 [], replicated
- grad_norm: float32 [], replicated
- emb_first_new: float32 [30720, 312], P(('dp', 'fsdp'))
- emb_second_new: float32 [30720, 312], P(('dp', 'fsdp'))
- emb_new: float32 [30720, 312], P(('dp', 'fsdp'))
- pos_first_new: float32 [128, 312], P(('dp', 'fsdp'))
- pos_second_new: float32 [128, 312], P(('dp', 'fsdp'))
- pos_new: float32 [128, 312], P(('dp', 'fsdp'))
- layer_first_new: float32 [2, 1138176], P(None, ('dp', 'fsdp'))
- layer_second_new: float32 [2, 1138176], P(None, ('dp', 'fsdp'))
- layer_new: float32 [2, 1138176], P(None, ('dp', 'fsdp'))
- proj_first_new: float32 [312, 768], P(None, ('dp', 'fsdp'))
- proj_second_new: float32 [312, 768], P(None, ('dp', 'fsdp'))
- proj_new: float32 [312, 768], P(None, ('dp', 'fsdp'))
- vec_first_new: float32 [2, 3696], replicated
- vec_second_new: float32 [2, 3696], replicated
- vec_new: float32 [2, 3696], replicated
- misc_first_new: float32 [1392], replicated
- misc_second_new: float32 [1392], replicated
- misc_new: float32 [1392], replicated
Inputs may be any that keep to these rules, and one draw needn't show every extreme that they name: `valid_mask`: the ones of each row form a prefix of one position or more. `mask_pos`: each masked position lies among its row's valid positions.
All inputs are finite; a program needn't handle non-finite values.
Results may differ from a plain program's by a relative error of at most 0.00075.
The roundings to bfloat16 on the way count: a program that leaves them out, or rounds other values in their place, can miss the bound.
Values may be sent and summed in bfloat16 or wider, within the bound.
A program may use at most 320 MiB of HBM per device.

v0:
```python
from functools import partial

import jax
import jax.numpy as jnp
from jax import lax
from jax.sharding import PartitionSpec as P

DS = 312
HS = 12
FS = 1200
DT = 768
HT = 12
FT = 3072
STEP = 5


NORM_EPS = 1e-06
CLIP_NORM = 0.05
LEARN_RATE = 0.05
BETA_ONE = 0.9
BETA_TWO = 0.999
ADAM_EPS = 1e-06
WEIGHT_DECAY = 0.01
NEG_LARGE = -1e30


def merged(x, axis, combine):
    everything = jax.tree.map(lambda part: lax.all_gather(part, axis), x)
    leading = jax.tree.map(lambda part: part[0], everything)

    def turn(k, so_far):
        return combine(so_far, jax.tree.map(lambda part: part[k], everything))

    return lax.fori_loop(1, lax.axis_size(axis), turn, leading)


def outer_product(left, right):
    return lax.dot_general(
        left, right, (((0,), (0,)), ((), ())), preferred_element_type=jnp.float32
    )


def back_product(grad, weight):
    return lax.dot_general(
        grad, weight, (((1,), (1,)), ((), ())), preferred_element_type=jnp.float32
    )


def norm_forward(value, gain, bias):
    average = jnp.mean(value, -1, keepdims=True)
    centered = value - average
    inverse = lax.rsqrt(jnp.mean(centered * centered, -1, keepdims=True) + NORM_EPS)
    normed = centered * inverse
    return (normed * gain + bias, normed, inverse)


def norm_backward(grad, normed, inverse, gain):
    d_normed = grad * gain
    d_value = inverse * (
        d_normed
        - jnp.mean(d_normed, -1, keepdims=True)
        - normed * jnp.mean(d_normed * normed, -1, keepdims=True)
    )
    return (d_value, jnp.sum(grad * normed, 0), jnp.sum(grad, 0))


def cut_pieces(vector, sizes):
    pieces = []
    start = 0
    for amount in sizes:
        pieces.append(vector[..., start : start + amount])
        start += amount
    return pieces


def split_flat(flat, width, hidden):
    pieces = cut_pieces(flat, [3 * width * width, width * width, width * hidden, hidden * width])
    return (
        pieces[0].reshape(width, 3 * width),
        pieces[1].reshape(width, width),
        pieces[2].reshape(width, hidden),
        pieces[3].reshape(hidden, width),
    )


def student_vectors(vector):
    bias_q, bias_v, bias_o, gain_one, shift_one, bias_up, bias_down, gain_two, shift_two = (
        cut_pieces(vector, [DS] * 5 + [FS] + [DS] * 3)
    )
    return (
        bias_q,
        jnp.zeros_like(bias_q),
        bias_v,
        bias_o,
        gain_one,
        shift_one,
        bias_up,
        bias_down,
        gain_two,
        shift_two,
    )


def teacher_vectors(vector):
    return tuple(cut_pieces(vector, [DT] * 6 + [FT] + [DT] * 3))


def attention_scores(parts, allowed):
    size = parts.shape[4]
    scores = jnp.einsum(
        "rqhd,rkhd->rhqk", parts[:, :, 0], parts[:, :, 1], preferred_element_type=jnp.float32
    ) * size ** (-0.5)
    return (scores, jnp.where(allowed[:, None], scores, NEG_LARGE))


def layer_forward(hidden, matrices, vectors, allowed, heads):
    w_qkv, w_out, w_up, w_down = matrices
    bias_q, bias_k, bias_v, bias_o, gain_one, shift_one, bias_up, bias_down, gain_two, shift_two = (
        vectors
    )
    tokens, width = hidden.shape
    rows, length = (allowed.shape[0], allowed.shape[1])
    hidden_low = hidden.astype(jnp.bfloat16)
    qkv = jnp.dot(hidden_low, w_qkv, preferred_element_type=jnp.float32) + jnp.concatenate(
        [bias_q, bias_k, bias_v]
    )
    parts = qkv.astype(jnp.bfloat16).reshape(rows, length, 3, heads, width // heads)
    scores, masked = attention_scores(parts, allowed)
    topmost = jnp.max(masked, -1, keepdims=True)
    expo = jnp.exp(masked - topmost)
    summed = jnp.sum(expo, -1, keepdims=True)
    weights = (expo / summed).astype(jnp.bfloat16)
    context = jnp.einsum(
        "rhqk,rkhd->rqhd", weights, parts[:, :, 2], preferred_element_type=jnp.float32
    )
    context = context.reshape(tokens, width).astype(jnp.bfloat16)
    attended = jnp.dot(context, w_out, preferred_element_type=jnp.float32) + bias_o
    middle, normed_one, inverse_one = norm_forward(hidden + attended, gain_one, shift_one)
    middle_low = middle.astype(jnp.bfloat16)
    inner = jnp.dot(middle_low, w_up, preferred_element_type=jnp.float32) + bias_up
    active = jax.nn.gelu(inner, approximate=True).astype(jnp.bfloat16)
    outer = jnp.dot(active, w_down, preferred_element_type=jnp.float32) + bias_down
    result, normed_two, inverse_two = norm_forward(middle + outer, gain_two, shift_two)
    kept = (
        hidden_low,
        parts,
        topmost + jnp.log(summed),
        context,
        normed_one,
        inverse_one,
        middle_low,
        inner,
        active,
        normed_two,
        inverse_two,
    )
    return (result, scores, kept)


def layer_backward(grad, score_grad, matrices, vectors, allowed, kept):
    w_qkv, w_out, w_up, w_down = matrices
    gain_one, gain_two = (vectors[4], vectors[8])
    (
        hidden_low,
        parts,
        log_total,
        context,
        normed_one,
        inverse_one,
        middle_low,
        inner,
        active,
        normed_two,
        inverse_two,
    ) = kept
    tokens, width = grad.shape
    size = parts.shape[4]
    d_sum_two, d_gain_two, d_shift_two = norm_backward(grad, normed_two, inverse_two, gain_two)
    d_outer = d_sum_two.astype(jnp.bfloat16)
    w_down_grad = outer_product(active, d_outer)
    d_active = back_product(d_outer, w_down)
    unused, gelu_pull = jax.vjp(partial(jax.nn.gelu, approximate=True), inner)
    d_inner = gelu_pull(d_active)[0].astype(jnp.bfloat16)
    w_up_grad = outer_product(middle_low, d_inner)
    d_middle = d_sum_two + back_product(d_inner, w_up)
    d_sum_one, d_gain_one, d_shift_one = norm_backward(d_middle, normed_one, inverse_one, gain_one)
    d_attended = d_sum_one.astype(jnp.bfloat16)
    w_out_grad = outer_product(context, d_attended)
    d_context = (
        back_product(d_attended, w_out)
        .astype(jnp.bfloat16)
        .reshape(parts.shape[0], parts.shape[1], parts.shape[3], size)
    )
    scores, masked = attention_scores(parts, allowed)
    weights = jnp.exp(masked - log_total)
    d_value = jnp.einsum(
        "rhqk,rqhd->rkhd",
        weights.astype(jnp.bfloat16),
        d_context,
        preferred_element_type=jnp.float32,
    )
    d_weights = jnp.einsum(
        "rqhd,rkhd->rhqk", d_context, parts[:, :, 2], preferred_element_type=jnp.float32
    )
    d_scores = weights * (d_weights - jnp.sum(weights * d_weights, -1, keepdims=True)) + score_grad
    d_scores = d_scores.astype(jnp.bfloat16)
    d_query = jnp.einsum(
        "rhqk,rkhd->rqhd", d_scores, parts[:, :, 1], preferred_element_type=jnp.float32
    ) * size ** (-0.5)
    d_key = jnp.einsum(
        "rhqk,rqhd->rkhd", d_scores, parts[:, :, 0], preferred_element_type=jnp.float32
    ) * size ** (-0.5)
    d_qkv = jnp.stack([d_query, d_key, d_value], 2).reshape(tokens, 3 * width).astype(jnp.bfloat16)
    w_qkv_grad = outer_product(hidden_low, d_qkv)
    d_hidden = d_sum_one + back_product(d_qkv, w_qkv)
    bias_grad = jnp.sum(d_qkv.astype(jnp.float32), 0)
    vector_grad = jnp.concatenate(
        [
            bias_grad[:width],
            bias_grad[2 * width :],
            jnp.sum(d_attended.astype(jnp.float32), 0),
            d_gain_one,
            d_shift_one,
            jnp.sum(d_inner.astype(jnp.float32), 0),
            jnp.sum(d_outer.astype(jnp.float32), 0),
            d_gain_two,
            d_shift_two,
        ]
    )
    flat_grad = jnp.concatenate(
        [
            w_qkv_grad.reshape(-1),
            w_out_grad.reshape(-1),
            w_up_grad.reshape(-1),
            w_down_grad.reshape(-1),
        ]
    )
    return (d_hidden, flat_grad, vector_grad)


def combine_stats(first_half, second_half):
    s_top = jnp.maximum(first_half[0], second_half[0])
    s_sum = first_half[1] * jnp.exp(first_half[0] - s_top) + second_half[1] * jnp.exp(
        second_half[0] - s_top
    )
    t_top = jnp.maximum(first_half[2], second_half[2])
    scale_one = jnp.exp(first_half[2] - t_top)
    scale_two = jnp.exp(second_half[2] - t_top)
    t_sum = first_half[3] * scale_one + second_half[3] * scale_two
    cross = first_half[4] * scale_one + second_half[4] * scale_two
    return (s_top, s_sum, t_top, t_sum, cross)


def hidden_term(source, target, proj_all, proj_bias, weight, denom):
    source_low = source.astype(jnp.bfloat16)
    mapped = jnp.dot(source_low, proj_all, preferred_element_type=jnp.float32) + proj_bias
    spread = mapped - target
    d_mapped = (2.0 * weight * spread / denom).astype(jnp.bfloat16)
    return (
        jnp.sum(weight * spread * spread) / denom,
        outer_product(source_low, d_mapped),
        jnp.sum(d_mapped.astype(jnp.float32), 0),
        back_product(d_mapped, proj_all),
    )


def adam_update(value, first, second, grad):
    first = BETA_ONE * first + (1.0 - BETA_ONE) * grad
    second = BETA_TWO * second + (1.0 - BETA_TWO) * grad * grad
    ratio = first / (1.0 - BETA_ONE**STEP) / (jnp.sqrt(second / (1.0 - BETA_TWO**STEP)) + ADAM_EPS)
    return (first, second, value - LEARN_RATE * (ratio + WEIGHT_DECAY * value))


def local(
    token_ids,
    valid_mask,
    seq_ids,
    mask_pos,
    mask_labels,
    teacher_in,
    teacher_flat,
    teacher_vec,
    teacher_head,
    emb_table,
    emb_first,
    emb_second,
    pos_table,
    pos_first,
    pos_second,
    layer_flat,
    layer_first,
    layer_second,
    proj_weight,
    proj_first,
    proj_second,
    layer_vec,
    vec_first,
    vec_second,
    misc_vec,
    misc_first,
    misc_second,
):
    micro, rows, length = token_ids.shape
    width = emb_table.shape[1]
    layers = layer_vec.shape[0]
    picks = mask_pos.shape[2]
    tokens = rows * length
    groups = lax.axis_size("fsdp")
    place = lax.axis_index("fsdp")
    devices = lax.axis_size("dp") * groups
    hidden_denom = float(micro * rows * devices * length * DT)
    predict_denom = float(micro * rows * devices * picks)
    usable = valid_mask > 0
    same_doc = seq_ids[..., :, None] == seq_ids[..., None, :]
    pair_mask = same_doc & usable[..., :, None] & usable[..., None, :]
    allowed = pair_mask | jnp.eye(length, dtype=bool)
    count = lax.psum(jnp.sum(pair_mask.astype(jnp.int32)), ("dp", "fsdp")).astype(jnp.float32)
    table_all, places_all, proj_all = (
        lax.all_gather(emb_table.astype(jnp.bfloat16), ("dp", "fsdp"), axis=0, tiled=True),
        lax.all_gather(pos_table.astype(jnp.bfloat16), ("dp", "fsdp"), axis=0, tiled=True),
        lax.all_gather(proj_weight.astype(jnp.bfloat16), ("dp", "fsdp"), axis=1, tiled=True),
    )
    vocab = table_all.shape[0] // groups
    slice_table = lax.dynamic_slice_in_dim(table_all, place * vocab, vocab, 0)
    s_vectors = [student_vectors(layer_vec[layer_index]) for layer_index in range(layers)]
    t_vectors = teacher_vectors(teacher_vec.astype(jnp.float32))
    emb_gain, emb_bias, proj_bias = (misc_vec[:DS], misc_vec[DS : 2 * DS], misc_vec[2 * DS :])
    grad_table = jnp.zeros(table_all.shape, jnp.float32)
    grad_places = jnp.zeros(places_all.shape, jnp.float32)
    grad_proj = jnp.zeros(proj_all.shape, jnp.float32)
    grad_slice = jnp.zeros(slice_table.shape, jnp.float32)
    grad_vec = jnp.zeros(layer_vec.shape, jnp.float32)
    grad_misc = jnp.zeros(misc_vec.shape, jnp.float32)
    layer_acc = jnp.zeros(layer_flat.shape, jnp.float32)
    attention_sum = jnp.float32(0.0)
    hidden_sum = jnp.float32(0.0)
    predict_sum = jnp.float32(0.0)
    own_start = place * rows * picks
    for micro_index in range(micro):
        allowed_now = allowed[micro_index]
        t_matrices = split_flat(
            lax.all_gather(teacher_flat, ("dp", "fsdp"), axis=0, tiled=True), DT, FT
        )
        token_rows = table_all[token_ids[micro_index]].astype(jnp.float32) + places_all[
            None
        ].astype(jnp.float32)
        embedded, normed_zero, inverse_zero = norm_forward(
            token_rows.reshape(tokens, width), emb_gain, emb_bias
        )
        hidden = embedded
        saved = []
        for layer_index in range(layers):
            matrices = split_flat(
                lax.all_gather(
                    layer_flat[layer_index].astype(jnp.bfloat16), ("dp", "fsdp"), axis=0, tiled=True
                ),
                DS,
                FS,
            )
            hidden, scores, kept = layer_forward(
                hidden, matrices, s_vectors[layer_index], allowed_now, HS
            )
            saved.append(kept)
        t_input = teacher_in[micro_index].reshape(tokens, DT).astype(jnp.float32)
        t_out, t_scores, unused = layer_forward(t_input, t_matrices, t_vectors, allowed_now, HT)
        differ = scores - t_scores
        pair_now = pair_mask[micro_index][:, None]
        attention_sum = attention_sum + jnp.sum(jnp.where(pair_now, differ * differ, 0.0)) / count
        score_grad = jnp.where(pair_now, 2.0 * differ / count, 0.0)
        weight = valid_mask[micro_index].reshape(tokens, 1).astype(jnp.float32)
        loss_zero, proj_zero, bias_zero, back_zero = hidden_term(
            embedded, t_input, proj_all, proj_bias, weight, hidden_denom
        )
        loss_last, proj_last, bias_last, back_last = hidden_term(
            hidden, t_out, proj_all, proj_bias, weight, hidden_denom
        )
        hidden_sum = hidden_sum + loss_zero + loss_last
        grad_proj = grad_proj + proj_zero + proj_last
        flat_pick = (
            jnp.arange(rows, dtype=jnp.int32)[:, None] * length + mask_pos[micro_index]
        ).reshape(-1)
        picked = hidden.astype(jnp.bfloat16)[flat_pick]
        t_picked = t_out.astype(jnp.bfloat16)[flat_pick]
        picked_all, t_picked_all = (
            lax.all_gather(picked, "fsdp", axis=0, tiled=True),
            lax.all_gather(t_picked, "fsdp", axis=0, tiled=True),
        )
        s_logits = jnp.einsum(
            "gd,vd->gv", picked_all, slice_table, preferred_element_type=jnp.float32
        )
        t_logits = jnp.einsum(
            "gd,vd->gv", t_picked_all, teacher_head, preferred_element_type=jnp.float32
        )
        s_top = jnp.max(s_logits, -1)
        t_top = jnp.max(t_logits, -1)
        t_exp = jnp.exp(t_logits - t_top[:, None])
        local_stats = (
            s_top,
            jnp.sum(jnp.exp(s_logits - s_top[:, None]), -1),
            t_top,
            jnp.sum(t_exp, -1),
            jnp.sum(t_exp * s_logits, -1),
        )
        s_top, s_sum, t_top, t_sum, cross = merged(local_stats, "fsdp", combine_stats)
        log_total = s_top + jnp.log(s_sum)
        d_logits = (
            2.0 * jnp.exp(s_logits - log_total[:, None])
            - jnp.exp(t_logits - t_top[:, None]) / t_sum[:, None]
        ) / predict_denom
        d_logits = d_logits.astype(jnp.bfloat16)
        grad_slice = grad_slice + outer_product(d_logits, picked_all)
        d_picked = lax.psum_scatter(
            jnp.dot(d_logits, slice_table, preferred_element_type=jnp.float32).astype(jnp.bfloat16),
            "fsdp",
            scatter_dimension=0,
            tiled=True,
        ).astype(jnp.float32)
        labels_flat = mask_labels[micro_index].reshape(-1)
        label_rows = table_all[labels_flat].astype(jnp.float32)
        picked_wide = picked.astype(jnp.float32)
        target_logit = jnp.sum(picked_wide * label_rows, -1)
        own_total = lax.dynamic_slice_in_dim(log_total, own_start, rows * picks, 0)
        own_cross = lax.dynamic_slice_in_dim(cross / t_sum, own_start, rows * picks, 0)
        predict_sum = (
            predict_sum + jnp.sum(2.0 * own_total - own_cross - target_logit) / predict_denom
        )
        d_picked = d_picked - label_rows / predict_denom
        grad_table = grad_table.at[labels_flat].add(-picked_wide / predict_denom)
        d_hidden = jnp.zeros((tokens, width), jnp.float32).at[flat_pick].add(d_picked) + back_last
        for layer_index in reversed(range(layers)):
            matrices = split_flat(
                lax.all_gather(
                    layer_flat[layer_index].astype(jnp.bfloat16), ("dp", "fsdp"), axis=0, tiled=True
                ),
                DS,
                FS,
            )
            extra_grad = score_grad if layer_index == layers - 1 else 0.0
            d_hidden, flat_grad, vector_grad = layer_backward(
                d_hidden,
                extra_grad,
                matrices,
                s_vectors[layer_index],
                allowed_now,
                saved[layer_index],
            )
            layer_acc = layer_acc.at[layer_index].add(
                lax.psum_scatter(flat_grad, ("dp", "fsdp"), scatter_dimension=0, tiled=True)
            )
            grad_vec = grad_vec.at[layer_index].add(vector_grad)
        d_token, d_gain, d_bias = norm_backward(
            d_hidden + back_zero, normed_zero, inverse_zero, emb_gain
        )
        grad_table = grad_table.at[token_ids[micro_index].reshape(-1)].add(d_token)
        grad_places = grad_places + jnp.sum(d_token.reshape(rows, length, width), 0)
        grad_misc = grad_misc + jnp.concatenate([d_gain, d_bias, bias_zero + bias_last])
    current = lax.dynamic_slice_in_dim(grad_table, place * vocab, vocab, 0)
    grad_table = lax.dynamic_update_slice_in_dim(grad_table, current + grad_slice, place * vocab, 0)
    g_table, g_places, g_proj = (
        lax.psum_scatter(grad_table, ("dp", "fsdp"), scatter_dimension=0, tiled=True),
        lax.psum_scatter(grad_places, ("dp", "fsdp"), scatter_dimension=0, tiled=True),
        lax.psum_scatter(grad_proj, ("dp", "fsdp"), scatter_dimension=1, tiled=True),
    )
    loss_parts = jnp.stack([attention_sum, hidden_sum, predict_sum])
    shard_squares = (
        jnp.sum(g_table * g_table)
        + jnp.sum(g_places * g_places)
        + jnp.sum(g_proj * g_proj)
        + jnp.sum(layer_acc * layer_acc)
    )
    g_vec, g_misc, loss_parts = lax.psum((grad_vec, grad_misc, loss_parts), ("dp", "fsdp"))
    shard_squares = lax.psum(shard_squares, ("dp", "fsdp"))
    norm = jnp.sqrt(shard_squares + jnp.sum(g_vec * g_vec) + jnp.sum(g_misc * g_misc))
    factor = CLIP_NORM / jnp.maximum(norm, CLIP_NORM)
    emb_a, emb_b, emb_c = adam_update(emb_table, emb_first, emb_second, g_table * factor)
    pos_a, pos_b, pos_c = adam_update(pos_table, pos_first, pos_second, g_places * factor)
    lay_a, lay_b, lay_c = adam_update(layer_flat, layer_first, layer_second, layer_acc * factor)
    pro_a, pro_b, pro_c = adam_update(proj_weight, proj_first, proj_second, g_proj * factor)
    vec_a, vec_b, vec_c = adam_update(layer_vec, vec_first, vec_second, g_vec * factor)
    mis_a, mis_b, mis_c = adam_update(misc_vec, misc_first, misc_second, g_misc * factor)
    loss = jnp.sum(loss_parts)
    return (
        loss,
        count,
        norm,
        emb_a,
        emb_b,
        emb_c,
        pos_a,
        pos_b,
        pos_c,
        lay_a,
        lay_b,
        lay_c,
        pro_a,
        pro_b,
        pro_c,
        vec_a,
        vec_b,
        vec_c,
        mis_a,
        mis_b,
        mis_c,
    )


def solution(mesh):
    placed = (
        P(None, ("dp", "fsdp"), None),
        P(None, ("dp", "fsdp"), None),
        P(None, ("dp", "fsdp"), None),
        P(None, ("dp", "fsdp"), None),
        P(None, ("dp", "fsdp"), None),
        P(None, ("dp", "fsdp"), None, None),
        P(("dp", "fsdp")),
        P(),
        P("fsdp", None),
        P(("dp", "fsdp"), None),
        P(("dp", "fsdp"), None),
        P(("dp", "fsdp"), None),
        P(("dp", "fsdp"), None),
        P(("dp", "fsdp"), None),
        P(("dp", "fsdp"), None),
        P(None, ("dp", "fsdp")),
        P(None, ("dp", "fsdp")),
        P(None, ("dp", "fsdp")),
        P(None, ("dp", "fsdp")),
        P(None, ("dp", "fsdp")),
        P(None, ("dp", "fsdp")),
        P(),
        P(),
        P(),
        P(),
        P(),
        P(),
    )
    return jax.shard_map(
        local,
        mesh=mesh,
        in_specs=placed,
        out_specs=(
            P(),
            P(),
            P(),
            P(("dp", "fsdp"), None),
            P(("dp", "fsdp"), None),
            P(("dp", "fsdp"), None),
            P(("dp", "fsdp"), None),
            P(("dp", "fsdp"), None),
            P(("dp", "fsdp"), None),
            P(None, ("dp", "fsdp")),
            P(None, ("dp", "fsdp")),
            P(None, ("dp", "fsdp")),
            P(None, ("dp", "fsdp")),
            P(None, ("dp", "fsdp")),
            P(None, ("dp", "fsdp")),
            P(),
            P(),
            P(),
            P(),
            P(),
            P(),
        ),
        check_vma=False,
    )
```

profile of v0, /device:TPU:0, one launch (start us, length us, event | category | flops | bytes accessed | tf_op | source)
XLA Modules:
  0.0 2323.7 jit_solution(6858862127341442484)
XLA Ops:
  21.7 70.9 %all-gather.17 = bf16[32,4,312]{2,1,0:T(4,128)(2,1)S(1)} all-gather(bf16[1,4,312]{2,1,0:T(4,128)(2,1)S(1)} %convert_bitcast_fusion.1), channel_id=1, replica_groups=mesh['dp'=4,'fsdp'=8] {'dp','fsdp'}, dimensions={0}, use_global_device_ids=true | all-gather | bytes 82368 | tf_op jit(solution)/shard_map/all_gather | solution.py:320
  96.0 74.3 %all_gather.102 = bf16[312,768]{0,1:T(8,128)(2,1)} all-gather(bf16[312,24]{0,1:T(8,128)(2,1)S(1)} %convert_element_type.574), channel_id=1, replica_groups=mesh['dp'=4,'fsdp'=8] {'dp','fsdp'}, dimensions={1}, use_global_device_ids=true | all-gather | bytes 494208 | tf_op jit(solution)/shard_map/all_gather | solution.py:321
  173.2 38.6 %psum.35 = s32[]{:T(128)} all-reduce(s32[]{:T(128)} %convert_reduce_fusion.20), channel_id=1, replica_groups=mesh['dp'=4,'fsdp'=8] {'dp','fsdp'}, use_global_device_ids=true, to_apply=%region_10.11 | all-reduce | flops 1 | bytes 8 | tf_op jit(solution)/shard_map/psum | solution.py:317
  563.5 35.5 %all-gather.5 = bf16[640,768]{1,0:T(8,128)(2,1)} all-gather(bf16[80,768]{1,0:T(8,128)(2,1)S(1)} %gather_fusion.3), channel_id=7, replica_groups=mesh['dp'=4,'fsdp'=8] {'fsdp'}, dimensions={0}, use_global_device_ids=true | all-gather | bytes 1105920 | tf_op jit(solution)/shard_map/all_gather | solution.py:386
  600.5 31.2 %all-gather.2 = bf16[640,312]{1,0:T(8,128)(2,1)S(1)} all-gather(bf16[80,312]{1,0:T(8,128)(2,1)S(1)} %gather_fusion.2), channel_id=4, replica_groups=mesh['dp'=4,'fsdp'=8] {'fsdp'}, dimensions={0}, use_global_device_ids=true | all-gather | bytes 449280 | tf_op jit(solution)/shard_map/all_gather | solution.py:385
  650.5 30.4 %all-gather.22 = f32[8,1,640]{2,1,0:T(1,128)S(1)} all-gather(f32[1,1,640]{2,1,0:T(1,128)S(1)} %reshape.1847), channel_id=10, replica_groups=mesh['dp'=4,'fsdp'=8] {'fsdp'}, dimensions={0}, use_global_device_ids=true | all-gather | bytes 23040 | tf_op jit(solution)/shard_map/all_gather | solution.py:28
  680.9 30.2 %all-gather.21 = f32[8,1,640]{2,1,0:T(1,128)S(1)} all-gather(f32[1,1,640]{2,1,0:T(1,128)S(1)} %reshape.1845), channel_id=9, replica_groups=mesh['dp'=4,'fsdp'=8] {'fsdp'}, dimensions={0}, use_global_device_ids=true | all-gather | bytes 23040 | tf_op jit(solution)/shard_map/all_gather | solution.py:28
  741.5 30.2 %all-gather.20 = f32[8,1,640]{2,1,0:T(1,128)S(1)} all-gather(f32[1,1,640]{2,1,0:T(1,128)S(1)} %reshape.1843), channel_id=8, replica_groups=mesh['dp'=4,'fsdp'=8] {'fsdp'}, dimensions={0}, use_global_device_ids=true | all-gather | bytes 23040 | tf_op jit(solution)/shard_map/all_gather | solution.py:28
  771.8 30.2 %all-gather.18 = f32[8,1,640]{2,1,0:T(1,128)S(1)} all-gather(f32[1,1,640]{2,1,0:T(1,128)S(1)} %reshape.1839), channel_id=5, replica_groups=mesh['dp'=4,'fsdp'=8] {'fsdp'}, dimensions={0}, use_global_device_ids=true | all-gather | bytes 23040 | tf_op jit(solution)/shard_map/all_gather | solution.py:28
  808.9 32.5 %all-gather.12 = bf16[640,768]{1,0:T(8,128)(2,1)S(1)} all-gather(bf16[80,768]{1,0:T(8,128)(2,1)S(1)} %gather_fusion.6), channel_id=14, replica_groups=mesh['dp'=4,'fsdp'=8] {'fsdp'}, dimensions={0}, use_global_device_ids=true | all-gather | bytes 1105920 | tf_op jit(solution)/shard_map/all_gather | solution.py:386
  852.6 31.1 %all-gather.9 = bf16[640,312]{1,0:T(8,128)(2,1)S(1)} all-gather(bf16[80,312]{1,0:T(8,128)(2,1)S(1)} %gather_fusion.5), channel_id=11, replica_groups=mesh['dp'=4,'fsdp'=8] {'fsdp'}, dimensions={0}, use_global_device_ids=true | all-gather | bytes 449280 | tf_op jit(solution)/shard_map/all_gather | solution.py:385
  924.4 30.2 %all-gather.26 = f32[8,1,640]{2,1,0:T(1,128)S(1)} all-gather(f32[1,1,640]{2,1,0:T(1,128)S(1)} %reshape.1855), channel_id=16, replica_groups=mesh['dp'=4,'fsdp'=8] {'fsdp'}, dimensions={0}, use_global_device_ids=true | all-gather | bytes 23040 | tf_op jit(solution)/shard_map/all_gather | solution.py:28
  955.3 30.2 %all-gather.24 = f32[8,1,640]{2,1,0:T(1,128)S(1)} all-gather(f32[1,1,640]{2,1,0:T(1,128)S(1)} %reshape.1851), channel_id=13, replica_groups=mesh['dp'=4,'fsdp'=8] {'fsdp'}, dimensions={0}, use_global_device_ids=true | all-gather | bytes 23040 | tf_op jit(solution)/shard_map/all_gather | solution.py:28
  986.1 30.2 %all-gather.25 = f32[8,1,640]{2,1,0:T(1,128)S(1)} all-gather(f32[1,1,640]{2,1,0:T(1,128)S(1)} %reshape.1853), channel_id=15, replica_groups=mesh['dp'=4,'fsdp'=8] {'fsdp'}, dimensions={0}, use_global_device_ids=true | all-gather | bytes 23040 | tf_op jit(solution)/shard_map/all_gather | solution.py:28
  1017.0 30.2 %all-gather.23 = f32[8,1,640]{2,1,0:T(1,128)S(1)} all-gather(f32[1,1,640]{2,1,0:T(1,128)S(1)} %reshape.1849), channel_id=12, replica_groups=mesh['dp'=4,'fsdp'=8] {'fsdp'}, dimensions={0}, use_global_device_ids=true | all-gather | bytes 23040 | tf_op jit(solution)/shard_map/all_gather | solution.py:28
  1167.7 51.3 %reduce-scatter.9.cloned.1.call-done = bf16[80,312]{1,0:T(8,128)(2,1)} async-done(((bf16[640,312]{1,0:T(8,128)(2,1)}), bf16[80,312]{1,0:T(8,128)(2,1)}) %reduce-scatter.9.cloned.1.call-update) | async-done | bytes 49936 | tf_op jit(solution)/shard_map/reduce_scatter | solution.py:412
  1420.8 39.1 %concatenate.107 = f32[1138176]{0:T(1024)} concatenate(f32[292032]{0:T(1024)} %reshape.1652, f32[97344]{0:T(1024)} %reshape.1653, f32[374400]{0:T(1024)} %reshape.1654, f32[374400]{0:T(1024)} %reshape.1655), dimensions={0} | concatenate | bytes 9105408 | tf_op jit(solution)/shard_map/concatenate | solution.py:230
  1489.2 38.9 %concatenate.106 = f32[1138176]{0:T(1024)} concatenate(f32[292032]{0:T(1024)} %reshape.1647, f32[97344]{0:T(1024)} %reshape.1648, f32[374400]{0:T(1024)} %reshape.1649, f32[374400]{0:T(1024)} %reshape.1650), dimensions={0} | concatenate | bytes 9105408 | tf_op jit(solution)/shard_map/concatenate | solution.py:230
  1557.5 36.2 %scatter_fusion = f32[30720,312]{1,0:T(8,128)} fusion(f32[30720,312]{1,0:T(8,128)} %scatter_custom_fusion, s32[512]{0:T(512)S(1)} %bitcast.577, f32[512,312]{1,0:T(8,128)S(1)} %copy.239), kind=kCustom, calls=%fused_computation.10 | custom fusion | flops 159744 | bytes 1918976 | tf_op jit(solution)/shard_map/scatter-add | solution.py:454
  1593.7 32.8 %scatter_custom_fusion.3 = f32[30720,312]{1,0:T(8,128)} fusion(f32[30720,312]{1,0:T(8,128)} %scatter_fusion, s32[80]{0:T(128)} %copy-done.389, bf16[80,312]{1,0:T(8,128)(2,1)S(1)} %copy-done.165, f32[]{:T(128)} %constant.451.clone.1), kind=kCustom, calls=%fused_computation.549 | custom fusion | flops 99840 | bytes 38388992 | tf_op jit(solution)/shard_map/scatter-add | solution.py:428
  1626.5 35.9 %scatter_fusion.1 = f32[30720,312]{1,0:T(8,128)} fusion(f32[30720,312]{1,0:T(8,128)} %scatter_custom_fusion.3, s32[512]{0:T(512)S(1)} %bitcast.576, f32[512,312]{1,0:T(8,128)S(1)} %copy.254), kind=kCustom, calls=%fused_computation.13 | custom fusion | flops 159744 | bytes 1918976 | tf_op jit(solution)/shard_map/scatter-add | solution.py:454
  1714.8 115.5 %all-reduce.14.cloned.1.call-done = (f32[128,312]{1,0:T(8,128)}, f32[1138176]{0:T(1024)}, f32[1138176]{0:T(1024)}, f32[1138176]{0:T(1024)}, f32[1138176]{0:T(1024)}) async-done(((f32[128,312]{1,0:T(8,128)}, f32[1138176]{0:T(1024)}, f32[1138176]{0:T(1024)}, f32[1138176]{0:T(1024)}, f32[1138176]{0:T(1024)}), (f32[128,312]{1,0:T(8,128)}, f32[1138176]{0:T(1024)}, f32[1138176]{0:T(1024)}, f32[1138176]{0:T(1024)}, ...) | async-done | bytes 18370576
  1841.0 405.3 %reduce-scatter.11.cloned.1.call-done = f32[960,312]{1,0:T(8,128)} async-done(((f32[30720,312]{1,0:T(8,128)}), f32[960,312]{1,0:T(8,128)}) %reduce-scatter.11.cloned.1.call-update) | async-done | bytes 1198096 | tf_op jit(solution)/shard_map/reduce_scatter | solution.py:460
  2254.3 40.2 %all-reduce.8 = (f32[3]{0:T(128)S(1)}, f32[]{:T(128)}, f32[2,3696]{1,0:T(2,128)S(1)}, f32[1392]{0:T(1024)S(1)}) all-reduce(f32[3]{0:T(128)S(1)} %copy-done.382, f32[]{:T(128)S(6)} %add.1346, f32[2,3696]{1,0:T(2,128)S(1)} %scatter-add.89, f32[1392]{0:T(1024)S(1)} %add.1353), channel_id=1, replica_groups=mesh['dp'=4,'fsdp'=8] {'dp','fsdp'}, use_global_device_ids=true, to_apply=%region_66.67 | all-reduce | flops 8788 | bytes 70304 | tf_op jit(solution)/shard_map/psum | solution.py:471
  (1426 shorter events, 972.6 us)
Async XLA Ops:
  7.2 207.2 %all-reduce.16.cloned.1.call-start = ((), (), s32[]{:S(2)}) async-start(), calls=%async_computation.11 | async-start | bytes 9109504
  14.1 328.6 %all-gather.31.cloned.1.call-start = ((), (), s32[]{:S(2)}) async-start(), calls=%async_computation.4 | async-start | bytes 14598144 | tf_op jit(solution)/shard_map/all_gather | solution.py:342
  14.8 393.7 %all-gather.33.cloned.1.call-start = ((), (), s32[]{:S(2)}) async-start(), calls=%async_computation.8 | async-start | bytes 21086208 | tf_op jit(solution)/shard_map/all_gather | solution.py:319
  15.8 1149.0 %reduce-scatter.7.cloned.1.call-start = ((), (), s32[]{:S(2)}) async-start(), calls=%async_computation.5 | async-start | bytes 552960 | tf_op jit(solution)/shard_map/reduce_scatter | solution.py:412
  16.6 502.0 %copy-start.235 = (f32[312]{0:T(512)}, f32[312]{0:T(512)S(1)}, u32[]{:S(2)}) copy-start(f32[312]{0:T(512)S(1)} %get-tuple-element.770) | copy-start | bytes 3748
  16.6 513.3 %copy-start.241 = (f32[312]{0:T(512)}, f32[312]{0:T(512)S(1)}, u32[]{:S(2)}) copy-start(f32[312]{0:T(512)S(1)} %get-tuple-element.767) | copy-start | bytes 3748
  16.6 521.5 %copy-start.233 = (f32[312]{0:T(512)}, f32[312]{0:T(512)S(1)}, u32[]{:S(2)}) copy-start(f32[312]{0:T(512)S(1)} %get-tuple-element.762) | copy-start | bytes 3748
  464.2 673.4 %copy-start.10 = (f32[4,128,312]{1,0,2:T(4,128)}, f32[4,128,312]{1,0,2:T(4,128)S(1)}, u32[]{:S(2)}) copy-start(f32[4,128,312]{1,0,2:T(4,128)S(1)} %get-tuple-element.935) | copy-start | bytes 1916932
  530.4 708.7 %copy-start.25 = (f32[512,312]{0,1:T(8,128)}, f32[512,312]{0,1:T(8,128)S(1)}, u32[]{:S(2)}) copy-start(f32[512,312]{0,1:T(8,128)S(1)} %get-tuple-element.1027) | copy-start | bytes 1916932
  645.7 157.0 %copy-start.15 = (bf16[312,768]{0,1:T(8,128)(2,1)S(1)}, bf16[312,768]{0,1:T(8,128)(2,1)}, u32[]{:S(2)}) copy-start(bf16[312,768]{0,1:T(8,128)(2,1)} %all_gather.102) | copy-start | bytes 1437700
  645.7 157.0 %copy-start.49 = (f32[512,768]{1,0:T(8,128)S(1)}, f32[512,768]{1,0:T(8,128)}, u32[]{:S(2)}) copy-start(f32[512,768]{1,0:T(8,128)} %get-tuple-element.1043) | copy-start | bytes 4718596
  645.7 157.0 %copy-start.94 = (bf16[512,312]{0,1:T(8,128)(2,1)S(1)}, bf16[512,312]{0,1:T(8,128)(2,1)}, u32[]{:S(2)}) copy-start(bf16[512,312]{0,1:T(8,128)(2,1)} %copy-done.93) | copy-start | bytes 958468
  645.7 157.0 %copy-start.348 = (f32[512]{0:T(512)S(1)}, f32[512]{0:T(512)}, u32[]{:S(2)}) copy-start(f32[512]{0:T(512)} %copy-done.347) | copy-start | bytes 6148
  645.7 157.0 %copy-start.377 = (f32[768]{0:T(1024)S(1)}, f32[768]{0:T(1024)}, u32[]{:S(2)}) copy-start(f32[768]{0:T(1024)} %slice.666) | copy-start | bytes 9220
  650.5 154.1 %copy-start.48 = (f32[512,768]{1,0:T(8,128)S(1)}, f32[512,768]{1,0:T(8,128)}, u32[]{:S(2)}) copy-start(f32[512,768]{1,0:T(8,128)} %copy-done.46) | copy-start | bytes 4718596
  888.7 159.2 %copy-start.273 = (f32[4,12,128]{2,1,0:T(8,128)S(1)}, f32[4,12,128]{2,1,0:T(8,128)}, u32[]{:S(2)}) copy-start(f32[4,12,128]{2,1,0:T(8,128)} %copy-done.272) | copy-start | bytes 73732
  888.7 159.2 %copy-start.275 = (f32[4,12,128]{2,1,0:T(8,128)S(1)}, f32[4,12,128]{2,1,0:T(8,128)}, u32[]{:S(2)}) copy-start(f32[4,12,128]{2,1,0:T(8,128)} %copy-done.274) | copy-start | bytes 73732
  888.7 159.9 %copy-start.269 = (f32[4,12,128]{2,1,0:T(8,128)S(1)}, f32[4,12,128]{2,1,0:T(8,128)}, u32[]{:S(2)}) copy-start(f32[4,12,128]{2,1,0:T(8,128)} %copy-done.268) | copy-start | bytes 73732
  888.7 159.8 %copy-start.271 = (f32[4,12,128]{2,1,0:T(8,128)S(1)}, f32[4,12,128]{2,1,0:T(8,128)}, u32[]{:S(2)}) copy-start(f32[4,12,128]{2,1,0:T(8,128)} %get-tuple-element.716) | copy-start | bytes 73732
  1072.8 146.2 %reduce-scatter.9.cloned.1.call-start = ((), (), s32[]{:S(2)}) async-start(), calls=%async_computation.6 | async-start | bytes 552960 | tf_op jit(solution)/shard_map/reduce_scatter | solution.py:412
  1158.8 554.6 %reduce-scatter.13.cloned.1.call-start = ((), (), s32[]{:S(2)}) async-start(), calls=%async_computation.9 | async-start | bytes 1216512
  1164.7 665.6 %all-reduce.14.cloned.1.call-start = ((), (), s32[]{:S(2)}) async-start(), calls=%async_computation.10 | async-start | bytes 36831232
  1528.1 718.3 %reduce-scatter.11.cloned.1.call-start = ((), (), s32[]{:S(2)}) async-start(), calls=%async_computation.7 | async-start | bytes 48660480 | tf_op jit(solution)/shard_map/reduce_scatter | solution.py:460
  1836.5 417.8 %copy-start.382 = (f32[3]{0:T(128)S(1)}, f32[3]{0:T(128)}, u32[]{:S(2)}) copy-start(f32[3]{0:T(128)} %pad_maximum_fusion.6) | copy-start | bytes 40
  (401 other events, 4293.1 us)
Sparse Core Ops, SparseCore 0:
  14.1 149.4 all-reduce.15
  166.9 102.9 all-gather.30
  273.7 130.1 all-gather.32
  1072.9 59.9 reduce-scatter.6
  1158.9 60.0 reduce-scatter.8
  1224.7 95.1 reduce-scatter.12
  1528.2 302.0 all-reduce.13
  1837.9 408.3 reduce-scatter.10
where the time goes:
time: 2340 us; the launch traced here: 2320 us
  blocking collectives  657 us (28%)
  local copies, waits for them, and re-layouts  601 us (26%)
  waiting for transfers between devices  573 us (24%)
  other arithmetic  238 us (10%)
  matrix products  221 us (9%)
  between operations  32.1 us (1%)
    reduce_scatter x1, waiting for transfers between devices, local(): lax.psum_scatter(grad_table, ('dp', 'fsdp'), scatter_dimension=0, tiled=T...  405 us
    all_gather x10, blocking collectives, merged(): everything = jax.tree.map(lambda part: lax.all_gather(part, axis), x)  303 us
    concatenate x4, local copies, waits for them, and re-layouts, layer_backward(): jnp.concatenate([w_qkv_grad.reshape(-1), w_out_grad.reshape(-1), w_up_gra...  137 us
    unnamed x11, waiting for transfers between devices  116 us
    unnamed x865, local copies, waits for them, and re-layouts  102 us
    slice x20, local copies, waits for them, and re-layouts, cut_pieces(): pieces.append(vector[..., start:start + amount])  99.2 us
    all_gather x1, blocking collectives, local(): lax.all_gather(proj_weight.astype(jnp.bfloat16), ('dp', 'fsdp'), axis=1,...  74.3 us
    scatter-add x2, other arithmetic, local(): grad_table = grad_table.at[token_ids[micro_index].reshape(-1)].add(d_token)  72.2 us
  transfers between devices with their start and end apart: 8, of which 3 were waited for; matrix products, arithmetic and copies ran while one was open for 34% of the time, Pallas kernels for 0%

commit v1 on v0

v1 whole, which is shorter than its diff:
```python
import math
from functools import partial

import jax
import jax.numpy as jnp
from jax import lax
from jax.experimental import pallas as pl
from jax.experimental.pallas import tpu as pltpu
from jax.sharding import PartitionSpec as P

DS = 312
HS = 12
FS = 1200
DT = 768
HT = 12
FT = 3072
STEP = 5


NORM_EPS = 1e-06
CLIP_NORM = 0.05
LEARN_RATE = 0.05
BETA_ONE = 0.9
BETA_TWO = 0.999
ADAM_EPS = 1e-06
WEIGHT_DECAY = 0.01
NEG_LARGE = -1e30

BOTH = ("dp", "fsdp")
MESH = pl.DeviceIdType.MESH
SLOTS = 48
WIDE = 3 * DS + DS + 2 * FS


def place_of():
    fsdp = lax.axis_size("fsdp")
    return lax.axis_index("dp") * fsdp + lax.axis_index("fsdp")


def member(index, whole):
    fsdp = lax.axis_size("fsdp")
    if whole:
        return (index // fsdp, index % fsdp)
    return (lax.axis_index("dp"), index)


def greet(count, me, whole):
    barrier = pltpu.get_barrier_semaphore()

    def signal(step, carry):
        pl.semaphore_signal(
            barrier, inc=1, device_id=member((me + step) % count, whole), device_id_type=MESH
        )
        return carry

    lax.fori_loop(1, count, signal, 0)
    pl.semaphore_wait(barrier, count - 1)


def exchange_kernel(count, whole, spread, x_ref, o_ref, send, recv, local_sem):
    me = place_of() if whole else lax.axis_index("fsdp")
    own = pltpu.make_async_copy(x_ref if spread else x_ref.at[me], o_ref.at[me], local_sem)
    own.start()
    greet(count, me, whole)

    def copy(step):
        peer = (me + step) % count
        return pltpu.make_async_remote_copy(
            x_ref if spread else x_ref.at[peer],
            o_ref.at[me],
            send.at[step],
            recv.at[step],
            device_id=member(peer, whole),
            device_id_type=MESH,
        )

    def start(step, carry):
        copy(step).start()
        return carry

    def finish(step, carry):
        copy(step).wait()
        return carry

    lax.fori_loop(1, count, start, 0)
    own.wait()
    lax.fori_loop(1, count, finish, 0)


def exchange(x, number, whole=True, spread=False):
    count = lax.axis_size("fsdp") * (lax.axis_size("dp") if whole else 1)
    return pl.pallas_call(
        partial(exchange_kernel, count, whole, spread),
        out_shape=jax.ShapeDtypeStruct(((count,) if spread else ()) + x.shape, x.dtype),
        in_specs=[pl.BlockSpec(memory_space=pl.ANY)],
        out_specs=pl.BlockSpec(memory_space=pl.ANY),
        scratch_shapes=[
            pltpu.SemaphoreType.DMA((count,)),
            pltpu.SemaphoreType.DMA((count,)),
            pltpu.SemaphoreType.DMA,
        ],
        compiler_params=pltpu.CompilerParams(collective_id=number, has_side_effects=True),
    )(x)


class Grid:
    def __init__(self):
        self.fsdp = lax.axis_size("fsdp")
        self.z_size = 4 if self.fsdp % 4 == 0 else 1
        self.side = self.fsdp // self.z_size
        assert lax.axis_size("dp") == 2 * self.side
        dp, fsdp = lax.axis_index("dp"), lax.axis_index("fsdp")
        self.x, self.core = dp // 2, dp % 2
        self.z, self.y = fsdp // self.side, fsdp % self.side
        side, z_size = self.side, self.z_size
        self.keys = [(g, b, a) for g in range(side) for b in range(side) for a in range(z_size)]
        self.rank = {key: index for index, key in enumerate(self.keys)}
        self.count = len(self.keys)

    def at(self, third, second, z, other=0):
        core = (self.core + other) % 2
        x = (self.x + third * (1 - core) + second * core) % self.side
        y = (self.y + second * (1 - core) + third * core) % self.side
        return (x * 2 + core, ((self.z + z) % self.z_size) * self.side + y)

    def index(self, third, second, z, other=0):
        dp, fsdp = self.at(third, second, z, other)
        return dp * self.fsdp + fsdp

    def neighbours(self):
        return (
            [(0, 0, a, 0) for a in range(1, self.z_size)]
            + [(0, b, 0, 0) for b in range(1, self.side)]
            + [(g, 0, 0, 0) for g in range(1, self.side)]
            + [(0, 0, 0, 1)]
        )

    def greet(self):
        barrier = pltpu.get_barrier_semaphore()
        around = self.neighbours()
        for where in around:
            pl.semaphore_signal(barrier, inc=1, device_id=self.at(*where), device_id_type=MESH)
        pl.semaphore_wait(barrier, len(around))


class Spread:
    def __init__(self, grid, x_ref, o_ref, send, recv, local_sem):
        self.grid, self.x_ref, self.o_ref = grid, x_ref, o_ref
        self.send, self.recv = send, recv
        self.started = []
        self.own = pltpu.make_async_copy(x_ref, o_ref.at[self.slot((0, 0, 0))], local_sem)
        self.own.start()

    def slot(self, key, other=0):
        grid = self.grid
        third, second, z = key
        return grid.index(grid.side - third, grid.side - second, grid.z_size - z, other)

    def push(self, key, name, where):
        grid = self.grid
        index = grid.rank[name] + (grid.count if where[3] else 0)
        copy = pltpu.make_async_remote_copy(
            self.x_ref if key == (0, 0, 0) else self.o_ref.at[self.slot(key)],
            self.o_ref.at[self.slot(key)],
            self.send.at[index],
            self.recv.at[index],
            device_id=grid.at(*where),
            device_id_type=MESH,
        )
        copy.start()
        self.started.append(copy)

    def forward(self, key):
        grid = self.grid
        third, second, z = key
        if key == (0, 0, 0):
            for step in range(1, grid.z_size):
                self.push(key, (0, 0, step), (0, 0, step, 0))
        if third == 0 and second == 0:
            for step in range(1, grid.side):
                self.push(key, (0, step, z), (0, step, 0, 0))
        if third == 0:
            for step in range(1, grid.side):
                self.push(key, (step, second, z), (step, 0, 0, 0))
        self.push(key, key, (0, 0, 0, 1))

    def arrived(self, key, other=0):
        grid = self.grid
        index = grid.rank[key] + (grid.count if other else 0)
        pltpu.make_async_remote_copy(
            self.o_ref.at[self.slot(key, other)],
            self.o_ref.at[self.slot(key, other)],
            self.send.at[index],
            self.recv.at[index],
            device_id=grid.at(0, 0, 0, 1),
            device_id_type=MESH,
        ).wait_recv()

    def start(self):
        self.forward((0, 0, 0))

    def middle(self):
        for key in self.grid.keys[1:]:
            self.arrived(key)
            self.forward(key)

    def finish(self):
        for key in self.grid.keys:
            self.arrived(key, 1)
        self.own.wait()
        for copy in self.started:
            copy.wait_send()


def entry_kernel(
    ask_ref, w_ref, table_ref, got_ref, all_ref, rows_ref, sent, asks, *sems
):
    ask_send, ask_recv, ask_local, w_send, w_recv, w_local, row_send, row_recv, row_local, out_sem = sems
    grid = Grid()
    count = 2 * grid.count
    me = place_of()
    own = pltpu.make_async_copy(ask_ref.at[me], asks.at[me], ask_local)
    own.start()
    greet(count, me, True)

    def ask_copy(step):
        peer = (me + step) % count
        return pltpu.make_async_remote_copy(
            ask_ref.at[peer],
            asks.at[me],
            ask_send.at[step],
            ask_recv.at[step],
            device_id=member(peer, True),
            device_id_type=MESH,
        )

    def row_copy(step):
        peer = (me + step) % count
        return pltpu.make_async_remote_copy(
            sent.at[peer],
            rows_ref.at[me],
            row_send.at[step],
            row_recv.at[step],
            device_id=member(peer, True),
            device_id_type=MESH,
        )

    def each(first, action):
        def body(step, carry):
            action(step)
            return carry

        lax.fori_loop(first, count, body, 0)

    each(1, lambda step: ask_copy(step).start())
    spread = Spread(grid, w_ref, all_ref, w_send, w_recv, w_local)
    spread.start()
    own.wait()
    table = table_ref[...]
    line = lax.broadcasted_iota(jnp.int32, (table.shape[0], 128), 0)

    def answer(source):
        marks = jnp.where(line == asks[source], 1.0, 0.0).astype(jnp.bfloat16)
        sent[source] = outer_product(marks, table)[:SLOTS].astype(jnp.bfloat16)

    answer(me)
    mine = pltpu.make_async_copy(sent.at[me], rows_ref.at[me], row_local)
    mine.start()

    def serve(step):
        ask_copy(step).wait_recv()
        answer((me + count - step) % count)

    each(1, serve)
    each(1, lambda step: row_copy(step).start())
    keep = pltpu.make_async_copy(asks, got_ref, out_sem)
    keep.start()
    spread.middle()
    spread.finish()
    mine.wait()
    keep.wait()
    each(1, lambda step: row_copy(step).wait())
    each(1, lambda step: ask_copy(step).wait_send())


def entry(asked, weights, table_low, number):
    count = asked.shape[0]
    width = table_low.shape[1]
    anywhere = pl.BlockSpec(memory_space=pl.ANY)
    dma = pltpu.SemaphoreType.DMA
    return pl.pallas_call(
        entry_kernel,
        out_shape=(
            jax.ShapeDtypeStruct(asked.shape, asked.dtype),
            jax.ShapeDtypeStruct((count,) + weights.shape, weights.dtype),
            jax.ShapeDtypeStruct((count, SLOTS, width), table_low.dtype),
        ),
        in_specs=[anywhere, anywhere, pl.BlockSpec(memory_space=pltpu.VMEM)],
        out_specs=(anywhere, anywhere, anywhere),
        scratch_shapes=[
            pltpu.VMEM((count, SLOTS, width), table_low.dtype),
            pltpu.VMEM(asked.shape, asked.dtype),
            *[dma((count,)), dma((count,)), dma] * 3,
            dma,
        ],
        compiler_params=pltpu.CompilerParams(
            collective_id=number, has_side_effects=True, vmem_limit_bytes=32 * 1024 * 1024
        ),
    )(asked, weights, table_low)


def reduce_kernel(plan, sources, *refs):
    ins, rest = refs[:sources], refs[sources:]
    row_ref, o_ref, got_ref = rest[:3]
    if plan:
        x_ref, rest = rest[3], rest[1:]
    else:
        x_ref = ins[0]
    held, third_in, second_in, z_in, send, recv, row_send, row_recv, row_local = rest[3:]
    grid = Grid()
    side, z_size, count, rank = grid.side, grid.z_size, grid.count, grid.rank
    order = sorted(grid.keys, key=lambda key: (key[0] == 0, key[1] == 0, key[2] == 0))
    devices = 2 * count
    me = place_of()
    own = pltpu.make_async_copy(row_ref.at[me], got_ref.at[me], row_local)
    own.start()
    greet(devices, me, True)

    def row_copy(step):
        peer = (me + step) % devices
        return pltpu.make_async_remote_copy(
            row_ref.at[peer],
            got_ref.at[me],
            row_send.at[step],
            row_recv.at[step],
            device_id=member(peer, True),
            device_id_type=MESH,
        )

    def row_start(step, carry):
        row_copy(step).start()
        return carry

    def row_finish(step, carry):
        row_copy(step).wait()
        return carry

    started = []

    def push(source, target, index, where):
        copy = pltpu.make_async_remote_copy(
            source,
            target,
            send.at[index],
            recv.at[index],
            device_id=grid.at(*where),
            device_id_type=MESH,
        )
        copy.start()
        started.append(copy)

    def arrived(target, index):
        pltpu.make_async_remote_copy(
            target,
            target,
            send.at[index],
            recv.at[index],
            device_id=grid.at(0, 0, 0, 1),
            device_id_type=MESH,
        ).wait_recv()

    for source, at, rows, block, line in plan:
        value = jnp.zeros((rows, x_ref.shape[2]), x_ref.dtype)
        if source >= 0:
            value = ins[source][at : at + rows, :]
        x_ref[block, line : line + rows, :] = value
    for key in order:
        push(x_ref.at[grid.index(*key, 1)], held.at[rank[key]], rank[key], (0, 0, 0, 1))
    from_third = {}
    from_second = {}
    from_z = {}
    index = count
    for step in range(1, side):
        for second in range(side):
            for z in range(z_size):
                from_third[step, second, z] = (
                    third_in.at[((step - 1) * side + second) * z_size + z],
                    index,
                )
                index += 1
    for step in range(1, side):
        for z in range(z_size):
            from_second[step, z] = (second_in.at[(step - 1) * z_size + z], index)
            index += 1
    for z in range(1, z_size):
        from_z[z] = (z_in.at[z - 1], index)
        index += 1
    for number, key in enumerate(order):
        third, second, z = key
        arrived(held.at[rank[key]], rank[key])
        total = held[rank[key]] + x_ref[grid.index(*key)]
        if third == 0:
            for step in range(1, side):
                arrived(*from_third[step, second, z])
                total = total + from_third[step, second, z][0][...]
        if third == 0 and second == 0:
            for step in range(1, side):
                arrived(*from_second[step, z])
                total = total + from_second[step, z][0][...]
        if key == (0, 0, 0):
            for step in range(1, z_size):
                arrived(*from_z[step])
                total = total + from_z[step][0][...]
            o_ref[...] = total
            continue
        held[rank[key]] = total
        if third:
            target, where = from_third[third, second, z], (third, 0, 0, 0)
        elif second:
            target, where = from_second[second, z], (0, second, 0, 0)
        else:
            target, where = from_z[z], (0, 0, z, 0)
        push(held.at[rank[key]], target[0], target[1], where)
        if number == 0:
            lax.fori_loop(1, devices, row_start, 0)
    for copy in started:
        copy.wait_send()
    own.wait()
    lax.fori_loop(1, devices, row_finish, 0)


def reduce(parts, plan, block, rows, number):
    count = lax.axis_size("dp") * lax.axis_size("fsdp")
    side = lax.axis_size("dp") // 2
    z_size = count // 2 // side // side
    kind = parts[0].dtype
    vmem, anywhere = pl.BlockSpec(memory_space=pltpu.VMEM), pl.BlockSpec(memory_space=pl.ANY)
    dma = pltpu.SemaphoreType.DMA
    return pl.pallas_call(
        partial(reduce_kernel, plan, len(parts)),
        out_shape=(
            jax.ShapeDtypeStruct(block, kind),
            jax.ShapeDtypeStruct(rows.shape, rows.dtype),
        ),
        in_specs=[vmem] * len(parts) + [anywhere],
        out_specs=(vmem, anywhere),
        scratch_shapes=[
            *([pltpu.VMEM((count,) + block, kind)] if plan else []),
            pltpu.VMEM((count // 2,) + block, kind),
            pltpu.VMEM(((side - 1) * side * z_size,) + block, kind),
            pltpu.VMEM(((side - 1) * z_size,) + block, kind),
            pltpu.VMEM((z_size - 1,) + block, kind),
            *[dma((count,))] * 4,
            dma,
        ],
        compiler_params=pltpu.CompilerParams(
            collective_id=number, has_side_effects=True, vmem_limit_bytes=58 * 1024 * 1024
        ),
    )(*parts, rows)


def woven(block, weave):
    chunk = block.shape[0]
    me = place_of()
    made = block
    for index in range(-(-3 * DS // chunk)):
        amount = min(chunk, 3 * DS - index * chunk)
        head = block[:amount].reshape((3, amount // 3, DS) if weave else (amount // 3, 3, DS))
        head = head.transpose(1, 0, 2).reshape(amount, DS)
        if index == 0:
            made = jnp.where(me < 3 * DS // chunk, head, made)
        elif amount < chunk:
            made = jnp.where(me == index, jnp.concatenate([head, block[amount:]]), made)
    return made


def block_plan(devices, chunk, layers, others):
    plan = []
    for block in range(devices):
        for layer in range(layers):
            base = 6 * layer
            row, end, line = block * chunk, (block + 1) * chunk, layer * chunk
            first = row
            if row < 3 * DS:
                stop = min(end, 3 * DS)
                amount = (stop - row) // 3
                for part in range(3):
                    plan.append((base + part, row // 3, amount, block, line + part * amount))
                row = stop
            for part, start, size in ((3, 3 * DS, DS), (4, 4 * DS, FS), (5, 4 * DS + FS, FS)):
                stop = min(end, start + size)
                if row < stop:
                    where = line + row - first
                    plan.append((base + part, row - start, stop - row, block, where))
                    row = stop
        line = layers * chunk
        for index, amount in enumerate(others):
            plan.append((6 * layers + index, block * amount, amount, block, line))
            line += amount
        spare = -line % 8
        if spare:
            plan.append((-1, 0, spare, block, line))
    return tuple(plan)


def pack(parts, width, rows):
    count = parts[0].shape[0]
    if all(part.ndim == 3 for part in parts):
        joined = jnp.concatenate(parts, 1)
        return jnp.pad(joined, ((0, 0), (0, rows - joined.shape[1]), (0, 0)))
    joined = jnp.concatenate([part.reshape(count, -1) for part in parts], 1)
    joined = jnp.pad(joined, ((0, 0), (0, rows * width - joined.shape[1])))
    return joined.reshape(count, rows, width)


def outer_product(left, right):
    return lax.dot_general(
        left, right, (((0,), (0,)), ((), ())), preferred_element_type=jnp.float32
    )


def back_product(grad, weight):
    return lax.dot_general(
        grad, weight, (((1,), (1,)), ((), ())), preferred_element_type=jnp.float32
    )


def norm_forward(value, gain, bias):
    average = jnp.mean(value, -1, keepdims=True)
    centered = value - average
    inverse = lax.rsqrt(jnp.mean(centered * centered, -1, keepdims=True) + NORM_EPS)
    normed = centered * inverse
    return (normed * gain + bias, normed, inverse)


def norm_backward(grad, normed, inverse, gain):
    d_normed = grad * gain
    d_value = inverse * (
        d_normed
        - jnp.mean(d_normed, -1, keepdims=True)
        - normed * jnp.mean(d_normed * normed, -1, keepdims=True)
    )
    return (d_value, jnp.sum(grad * normed, 0), jnp.sum(grad, 0))


def cut_pieces(vector, sizes):
    pieces = []
    start = 0
    for amount in sizes:
        pieces.append(vector[..., start : start + amount])
        start += amount
    return pieces


def split_rows(wide, width, hidden):
    first, second, third = 3 * width, 4 * width, 4 * width + hidden
    return (
        wide[:first].reshape(width, 3 * width),
        wide[first:second],
        wide[second:third].reshape(width, hidden),
        wide[third:],
    )


def combine_stats(first_half, second_half):
    s_top = jnp.maximum(first_half[0], second_half[0])
    s_sum = first_half[1] * jnp.exp(first_half[0] - s_top) + second_half[1] * jnp.exp(
        second_half[0] - s_top
    )
    t_top = jnp.maximum(first_half[2], second_half[2])
    scale_one = jnp.exp(first_half[2] - t_top)
    scale_two = jnp.exp(second_half[2] - t_top)
    t_sum = first_half[3] * scale_one + second_half[3] * scale_two
    cross = first_half[4] * scale_one + second_half[4] * scale_two
    return (s_top, s_sum, t_top, t_sum, cross)


def hidden_term(source, target, proj_turned, proj_bias, weight, denom):
    source_low = source.astype(jnp.bfloat16)
    mapped = back_product(source_low, proj_turned) + proj_bias
    spread = mapped - target
    d_mapped = (2.0 * weight * spread / denom).astype(jnp.bfloat16)
    return (
        jnp.sum(weight * spread * spread) / denom,
        outer_product(d_mapped, source_low),
        jnp.sum(d_mapped.astype(jnp.float32), 0),
        jnp.dot(d_mapped, proj_turned, preferred_element_type=jnp.float32),
    )


def sum_cores(value):
    first = lax.axis_index("dp") % 2 == 0
    parts = value.reshape(2, 2, -1, value.shape[1])
    given = jnp.where(first, parts[:, 1], parts[:, 0])
    kept = jnp.where(first, parts[:, 0], parts[:, 1])
    return kept + lax.ppermute(given, "dp", [(0, 1), (1, 0), (2, 3), (3, 2)])


def sum_along_x(parts):
    first = lax.axis_index("dp") // 2 == 0
    given = jnp.where(first, parts[1], parts[0])
    kept = jnp.where(first, parts[0], parts[1])
    return kept + lax.ppermute(given, "dp", [(0, 2), (2, 0), (1, 3), (3, 1)])


def adam_update(value, first, second, grad):
    first = BETA_ONE * first + (1.0 - BETA_ONE) * grad
    second = BETA_TWO * second + (1.0 - BETA_TWO) * grad * grad
    ratio = first / (1.0 - BETA_ONE**STEP) / (jnp.sqrt(second / (1.0 - BETA_TWO**STEP)) + ADAM_EPS)
    return (first, second, value - LEARN_RATE * (ratio + WEIGHT_DECAY * value))


def gelu(value):
    return 0.5 * value * (1.0 + jnp.tanh(0.7978845608028654 * (value + 0.044715 * value * value * value)))


def regroup(weights, group):
    amount = weights.shape[0]
    made = lax.broadcasted_iota(jnp.int32, (amount, amount), 0)
    taken = lax.broadcasted_iota(jnp.int32, (amount, amount), 1)
    inner = amount // group
    marks = jnp.where((made % inner) * group + made // inner == taken, 1.0, 0.0)
    return jnp.dot(
        marks.astype(jnp.bfloat16), weights, preferred_element_type=jnp.float32
    ).astype(jnp.bfloat16)


def softmax_low(scores, mask):
    masked = jnp.where(mask > 0.0, scores, NEG_LARGE)
    expo = jnp.exp(masked - jnp.max(masked, -1, keepdims=True))
    return (expo * (1.0 / jnp.sum(expo, -1, keepdims=True))).astype(jnp.bfloat16)


TILE = 256
CHUNK = 96


def teacher_kernel(x_ref, w_ref, vec_ref, mask_ref, y_ref, s_ref, qkv_ref, up_ref, context_ref):
    size = DT // HT
    for index in range(3 * DT // CHUNK):
        made = regroup(w_ref[index], 3)
        for part in range(3):
            rows = CHUNK // 3
            qkv_ref[part, index * rows : (index + 1) * rows, :] = made[part * rows : (part + 1) * rows]
    first_up, first_down = 4 * DT // CHUNK, (4 * DT + FT) // CHUNK
    many = FT // DT
    for index in range(FT // CHUNK // 2):
        at = first_up + 2 * index
        made = regroup(w_ref[at : at + 2].reshape(2 * CHUNK, DT), many)
        rows = 2 * CHUNK // many
        for part in range(many):
            up_ref[part, index * rows : (index + 1) * rows, :] = made[part * rows : (part + 1) * rows]
    line = lax.broadcasted_iota(jnp.int32, (1, 2 * size), 1)
    low_half = line < size
    length = mask_ref.shape[1]

    def vector(index, amount=1):
        return vec_ref[:, index * DT : (index + amount) * DT]

    def tile(step, carry):
        at = pl.ds(pl.multiple_of(step * TILE, TILE), TILE)
        x_low = x_ref[at, :]
        q, k, v = (
            (
                jnp.dot(x_low, qkv_ref[part], preferred_element_type=jnp.float32) + vector(part)
            ).astype(jnp.bfloat16)
            for part in range(3)
        )
        nothing = jnp.zeros((length, 2 * size), jnp.bfloat16)
        for row in range(TILE // length):
            span = slice(row * length, (row + 1) * length)
            here = pl.ds(pl.multiple_of(step * TILE + row * length, length), length)
            mask = mask_ref[here, :]
            for pair in range(HT // 2):
                lanes = slice(pair * 2 * size, (pair + 1) * 2 * size)
                k_pair, v_pair = k[span, lanes], v[span, lanes]
                k_both = jnp.concatenate(
                    [jnp.where(low_half, k_pair, nothing), jnp.where(low_half, nothing, k_pair)]
                )
                v_both = jnp.concatenate(
                    [jnp.where(low_half, v_pair, nothing), jnp.where(low_half, nothing, v_pair)]
                )
                scores = back_product(q[span, lanes], k_both) * size ** (-0.5)
                s_ref[here, pair * 2 * length : (pair + 1) * 2 * length] = scores
                weights = jnp.concatenate(
                    [softmax_low(scores[:, :length], mask), softmax_low(scores[:, length:], mask)], 1
                )
                context_ref[span, lanes] = jnp.dot(
                    weights, v_both, preferred_element_type=jnp.float32
                ).astype(jnp.bfloat16)
        w_out = w_ref[3 * DT // CHUNK : first_up].reshape(DT, DT)
        attended = jnp.dot(context_ref[...], w_out, preferred_element_type=jnp.float32) + vector(3)
        middle = norm_forward(x_low.astype(jnp.float32) + attended, vector(4), vector(5))[0]
        middle_low = middle.astype(jnp.bfloat16)
        outer = jnp.zeros((TILE, DT), jnp.float32)
        for part in range(many):
            inner = jnp.dot(middle_low, up_ref[part], preferred_element_type=jnp.float32) + vector(
                6 + part
            )
            begin = first_down + part * (DT // CHUNK)
            w_down = w_ref[begin : begin + DT // CHUNK].reshape(DT, DT)
            outer = outer + jnp.dot(
                gelu(inner).astype(jnp.bfloat16), w_down, preferred_element_type=jnp.float32
            )
        y_ref[at, :] = norm_forward(
            middle + outer + vector(6 + many), vector(7 + many), vector(8 + many)
        )[0]
        return carry

    lax.fori_loop(0, x_ref.shape[0] // TILE, tile, 0)


def teacher_forward(x_low, blocks, vectors, mask):
    tokens, length = mask.shape
    vmem = pl.BlockSpec(memory_space=pltpu.VMEM)
    return pl.pallas_call(
        teacher_kernel,
        out_shape=(
            jax.ShapeDtypeStruct((tokens, DT), jnp.float32),
            jax.ShapeDtypeStruct((tokens, HT * length), jnp.float32),
        ),
        in_specs=[vmem] * 4,
        out_specs=(vmem, vmem),
        scratch_shapes=[
            pltpu.VMEM((3, DT, DT), jnp.bfloat16),
            pltpu.VMEM((FT // DT, DT, DT), jnp.bfloat16),
            pltpu.VMEM((TILE, DT), jnp.bfloat16),
        ],
        compiler_params=pltpu.CompilerParams(vmem_limit_bytes=58 * 1024 * 1024),
        cost_estimate=pl.CostEstimate(
            flops=20 * 10**9, bytes_accessed=25 * 10**6, transcendentals=5 * 10**6
        ),
    )(x_low, blocks, vectors, mask)


WIDER = -(-FS // 128) * 128
VMEM_SPEC = pl.BlockSpec(memory_space=pltpu.VMEM)


def refold(source, target, source_width, target_width):
    period = math.lcm(source_width, target_width)
    groups = source.shape[1] * source_width // period
    step_in, step_out = period // source_width, period // target_width
    lane = lax.broadcasted_iota(jnp.int32, (groups, 128), 1)
    for row in range(step_out):
        for tile in range(-(-target_width // 128)):
            begin = row * target_width + 128 * tile
            amount = min(128, target_width - 128 * tile)
            made, at = jnp.zeros((groups, 128), source.dtype), 0
            while at < amount:
                line, column = divmod(begin + at, source_width)
                where, lanes = divmod(column, 128)
                piece = source[where, pl.ds(line, groups, stride=step_in), :]
                if (at - lanes) % 128:
                    piece = pltpu.roll(piece, (at - lanes) % 128, 1)
                length = min(128 - lanes, source_width - column, amount - at)
                made = jnp.where((lane >= at) & (lane < at + length), piece, made)
                at += length
            target[tile, pl.ds(row, groups, stride=step_out), :] = made


def unpack_kernel(plan, layers, w_ref, qkv_ref, out_ref, up_ref, down_ref, place_ref, proj_ref, *scratch):
    square, wide, folded, unfolded, small = scratch
    for layer in range(layers):
        for matrix, at, rows, block, line in plan:
            part = matrix - 6 * layer
            if not 0 <= part < 6:
                continue
            value = w_ref[block].astype(jnp.float32)[line : line + rows]
            if part < 4:
                square[part, at : at + rows, :] = value
            elif part == 4:
                for tile in range(-(-DS // 128)):
                    lanes = min(128, DS - 128 * tile)
                    folded[tile, at : at + rows, :lanes] = value[:, 128 * tile : 128 * tile + lanes]
            else:
                wide[at : at + rows, :] = value
        for part in range(3):
            qkv_ref[layer, part] = square[part].astype(jnp.bfloat16)
        out_ref[layer] = square[3].astype(jnp.bfloat16)
        refold(folded, unfolded, DS, FS)
        for tile in range(WIDER // 128):
            up_ref[layer, :, 128 * tile : 128 * tile + 128] = unfolded[tile].astype(jnp.bfloat16)
        down_ref[layer, :FS, :] = wide[...].astype(jnp.bfloat16)
        down_ref[layer, FS:, :] = jnp.zeros((WIDER - FS, DS), jnp.bfloat16)
    for matrix, at, rows, block, line in plan:
        if matrix >= 6 * layers:
            value = w_ref[block].astype(jnp.float32)[line : line + rows]
            small[matrix - 6 * layers, at : at + rows, :] = value
    place_ref[...] = small[0, : place_ref.shape[0]].astype(jnp.bfloat16)
    proj_ref[...] = small[1].astype(jnp.bfloat16)


def unpack(blocks, plan, layers, length):
    low = partial(jax.ShapeDtypeStruct, dtype=jnp.bfloat16)
    full = jnp.float32
    return pl.pallas_call(
        partial(unpack_kernel, plan, layers),
        out_shape=(
            low((layers, 3, DS, DS)),
            low((layers, DS, DS)),
            low((layers, DS, WIDER)),
            low((layers, WIDER, DS)),
            low((length, DS)),
            low((DT, DS)),
        ),
        in_specs=[VMEM_SPEC],
        out_specs=(VMEM_SPEC,) * 6,
        scratch_shapes=[
            pltpu.VMEM((4, DS, DS), full),
            pltpu.VMEM((FS, DS), full),
            pltpu.VMEM((-(-DS // 128), FS, 128), full),
            pltpu.VMEM((WIDER // 128, DS, 128), full),
            pltpu.VMEM((2, DT, DS), full),
        ],
        compiler_params=pltpu.CompilerParams(vmem_limit_bytes=50 * 1024 * 1024),
        cost_estimate=pl.CostEstimate(flops=0, bytes_accessed=20 * 10**6, transcendentals=0),
    )(blocks)


def by_heads(value, heads):
    width = value.shape[1]
    size = width // heads
    lane = lax.broadcasted_iota(jnp.int32, (1, width), 1)
    nothing = jnp.zeros_like(value)
    return jnp.concatenate(
        [
            jnp.where((lane >= head * size) & (lane < (head + 1) * size), value, nothing)
            for head in range(heads)
        ]
    )


def student_kernel(
    layers, token_ref, place_ref, evec_ref, vec_ref, bias_ref, mask_ref,
    qkv_w, out_w, up_w, down_w,
    emb_ref, zero_ref, zero_inv, last_ref, low_ref, qkv_ref, context_ref, one_ref, one_inv, two_ref, two_inv,
):
    length = mask_ref.shape[1]
    size = DS // HS

    def tile(step, carry):
        at = pl.ds(pl.multiple_of(step * TILE, TILE), TILE)
        places = jnp.concatenate([place_ref[...].astype(jnp.float32)] * (TILE // length))
        hidden, normed, inverse = norm_forward(
            token_ref[at, :] + places, evec_ref[0:1, :], evec_ref[1:2, :]
        )
        emb_ref[at, :] = hidden
        zero_ref[at, :] = normed
        zero_inv[at, :] = inverse
        for layer in range(layers):
            def vector(index):
                return vec_ref[layer, index : index + 1, :]

            low = hidden.astype(jnp.bfloat16)
            low_ref[layer, at, :] = low
            parts = []
            for part in range(3):
                made = jnp.dot(low, qkv_w[layer, part], preferred_element_type=jnp.float32)
                if part != 1:
                    made = made + vector(part // 2)
                parts.append(made.astype(jnp.bfloat16))
                qkv_ref[layer, part, at, :] = parts[part]
            contexts = []
            for row in range(TILE // length):
                span = slice(row * length, (row + 1) * length)
                here = pl.ds(pl.multiple_of(step * TILE + row * length, length), length)
                mask = mask_ref[here, :]
                q, k, v = (part[span] for part in parts)
                scores = back_product(q, by_heads(k, HS)) * size ** (-0.5)
                weights = jnp.concatenate(
                    [
                        softmax_low(scores[:, head * length : (head + 1) * length], mask)
                        for head in range(HS)
                    ],
                    1,
                )
                contexts.append(
                    jnp.dot(weights, by_heads(v, HS), preferred_element_type=jnp.float32)
                )
            context = jnp.concatenate(contexts).astype(jnp.bfloat16)
            context_ref[layer, at, :] = context
            attended = jnp.dot(context, out_w[layer], preferred_element_type=jnp.float32) + vector(2)
            middle, normed, inverse = norm_forward(hidden + attended, vector(3), vector(4))
            one_ref[layer, at, :] = normed
            one_inv[layer, at, :] = inverse
            inner = jnp.dot(
                middle.astype(jnp.bfloat16), up_w[layer], preferred_element_type=jnp.float32
            ) + bias_ref[layer]
            outer = jnp.dot(
                gelu(inner).astype(jnp.bfloat16), down_w[layer], preferred_element_type=jnp.float32
            ) + vector(5)
            hidden, normed, inverse = norm_forward(middle + outer, vector(6), vector(7))
            two_ref[layer, at, :] = normed
            two_inv[layer, at, :] = inverse
        last_ref[at, :] = hidden
        return carry

    lax.fori_loop(0, token_ref.shape[0] // TILE, tile, 0)


def student_forward(token_rows, places, evec, vectors, biases, mask, matrices):
    tokens = token_rows.shape[0]
    layers = vectors.shape[0]
    full = partial(jax.ShapeDtypeStruct, dtype=jnp.float32)
    low = partial(jax.ShapeDtypeStruct, dtype=jnp.bfloat16)
    made = (
        full((tokens, DS)),
        full((tokens, DS)),
        full((tokens, 1)),
        full((tokens, DS)),
        low((layers, tokens, DS)),
        low((layers, 3, tokens, DS)),
        low((layers, tokens, DS)),
        full((layers, tokens, DS)),
        full((layers, tokens, 1)),
        full((layers, tokens, DS)),
        full((layers, tokens, 1)),
    )
    return pl.pallas_call(
        partial(student_kernel, layers),
        out_shape=made,
        in_specs=[VMEM_SPEC] * 10,
        out_specs=(VMEM_SPEC,) * len(made),
        compiler_params=pltpu.CompilerParams(vmem_limit_bytes=58 * 1024 * 1024),
        cost_estimate=pl.CostEstimate(
            flops=8 * 10**9, bytes_accessed=40 * 10**6, transcendentals=6 * 10**6
        ),
    )(token_rows, places, evec, vectors, biases, mask, *matrices)


def back_kernel(
    last, grad_ref, vec_ref, bias_ref, mask_ref, qkv_w, out_w, up_w, down_w,
    low_ref, qkv_ref, context_ref, one_ref, one_inv, two_ref, two_inv, *refs,
):
    if last:
        score_ref, count_ref, refs = refs[0], refs[1], refs[2:]
    hidden_ref, *weight_refs, vec_out, bias_out, refs = (*refs[:9], refs[9:])
    dq_ref, dk_ref, dv_ref, do_ref, du_ref, dd_ref = weight_refs
    if last:
        loss_ref, refs = refs[0], refs[1:]
        loss_ref[...] = jnp.zeros_like(loss_ref)
    outer_s, attended_s, q_s, k_s, v_s, middle_s, active_s, inner_s, unfolded, folded = refs
    length = mask_ref.shape[1]
    size = DS // HS
    vec_out[...] = jnp.zeros_like(vec_out)
    bias_out[...] = jnp.zeros_like(bias_out)
    many = 256

    def vector(index):
        return vec_ref[index : index + 1, :]

    def note(index, value):
        vec_out[index : index + 1, :] += jnp.sum(value.astype(jnp.float32), 0, keepdims=True)

    def norm_back(grad, normed, inverse, gain, index):
        d_normed = grad * gain
        note(index, grad * normed)
        note(index + 1, grad)
        return inverse * (
            d_normed
            - jnp.mean(d_normed, -1, keepdims=True)
            - normed * jnp.mean(d_normed * normed, -1, keepdims=True)
        )

    def tile(step, carry):
        at = pl.ds(pl.multiple_of(step * TILE, TILE), TILE)
        d_sum = norm_back(grad_ref[at, :], two_ref[at, :], two_inv[at, :], vector(6), 6)
        d_outer = d_sum.astype(jnp.bfloat16)
        outer_s[at, :] = d_outer
        note(5, d_outer)
        middle = (one_ref[at, :] * vector(3) + vector(4)).astype(jnp.bfloat16)
        middle_s[at, :] = middle
        d_middle = d_sum
        for first in range(0, WIDER, many):
            lanes = slice(first, first + many)
            inner = jnp.dot(
                middle, up_w[:, lanes], preferred_element_type=jnp.float32
            ) + bias_ref[:, lanes]
            squared = inner * inner
            bent = jnp.tanh(0.7978845608028654 * (inner + 0.044715 * squared * inner))
            active_s[at, lanes] = (0.5 * inner * (1.0 + bent)).astype(jnp.bfloat16)
            slope = 0.5 * (1.0 + bent) + 0.5 * inner * (1.0 - bent * bent) * (
                0.7978845608028654 * (1.0 + 3.0 * 0.044715 * squared)
            )
            d_inner = (back_product(d_outer, down_w[lanes, :]) * slope).astype(jnp.bfloat16)
            inner_s[at, lanes] = d_inner
            bias_out[:, lanes] += jnp.sum(d_inner.astype(jnp.float32), 0, keepdims=True)
            d_middle = d_middle + back_product(d_inner, up_w[:, lanes])
        d_one = norm_back(d_middle, one_ref[at, :], one_inv[at, :], vector(3), 3)
        d_attended = d_one.astype(jnp.bfloat16)
        attended_s[at, :] = d_attended
        note(2, d_attended)
        d_context = back_product(d_attended, out_w[...]).astype(jnp.bfloat16)
        for row in range(TILE // length):
            here = pl.ds(pl.multiple_of(step * TILE + row * length, length), length)
            mask = mask_ref[here, :]
            d_row = d_context[row * length : (row + 1) * length]
            q, k, v = (qkv_ref[part, here, :] for part in range(3))
            keys = by_heads(k, HS)
            scores = back_product(q, keys) * size ** (-0.5)
            d_weights = back_product(d_row, by_heads(v, HS))
            low_weights, d_scores = [], []
            for head in range(HS):
                lanes = slice(head * length, (head + 1) * length)
                masked = jnp.where(mask > 0.0, scores[:, lanes], NEG_LARGE)
                expo = jnp.exp(masked - jnp.max(masked, -1, keepdims=True))
                weights = expo * (1.0 / jnp.sum(expo, -1, keepdims=True))
                low_weights.append(weights.astype(jnp.bfloat16))
                turned = weights * d_weights[:, lanes]
                made = turned - weights * jnp.sum(turned, -1, keepdims=True)
                if last:
                    differ = jnp.where(mask > 1.0, scores[:, lanes] - score_ref[here, lanes], 0.0)
                    loss_ref[...] += jnp.sum(differ * differ, 0, keepdims=True)
                    made = made + differ * (2.0 / count_ref[...])
                d_scores.append(made.astype(jnp.bfloat16))
            scale = size ** (-0.5)
            q_s[here, :] = (
                jnp.dot(jnp.concatenate(d_scores, 1), keys, preferred_element_type=jnp.float32)
                * scale
            ).astype(jnp.bfloat16)
            k_s[here, :] = (
                outer_product(jnp.concatenate(d_scores), by_heads(q, HS)) * scale
            ).astype(jnp.bfloat16)
            v_s[here, :] = outer_product(
                jnp.concatenate(low_weights), by_heads(d_row, HS)
            ).astype(jnp.bfloat16)
        d_hidden = d_one
        for part, held in enumerate((q_s, k_s, v_s)):
            d_part = held[at, :]
            if part != 1:
                note(part // 2, d_part)
            d_hidden = d_hidden + back_product(d_part, qkv_w[part])
        hidden_ref[at, :] = d_hidden
        return carry

    lax.fori_loop(0, grad_ref.shape[0] // TILE, tile, 0)
    low = low_ref[...]
    dq_ref[...] = outer_product(low, q_s[...])
    dk_ref[...] = outer_product(low, k_s[...])
    dv_ref[...] = outer_product(low, v_s[...])
    do_ref[...] = outer_product(context_ref[...], attended_s[...])
    for first in range(0, WIDER, many):
        lanes = slice(first, first + many)
        stop = min(first + many, FS)
        dd_ref[first:stop, :] = outer_product(active_s[:, lanes], outer_s[...])[: stop - first]
        made = outer_product(middle_s[...], inner_s[:, lanes])
        for tile_at in range(many // 128):
            unfolded[first // 128 + tile_at] = made[:, 128 * tile_at : 128 * tile_at + 128]
    refold(unfolded, folded, FS, DS)
    for tile_at in range(-(-DS // 128)):
        lanes = min(128, DS - 128 * tile_at)
        du_ref[:, 128 * tile_at : 128 * tile_at + lanes] = folded[tile_at, :, :lanes]


def student_backward(grad, vectors, biases, mask, matrices, saved, last):
    tokens, length = mask.shape
    full = partial(jax.ShapeDtypeStruct, dtype=jnp.float32)
    made = [
        full((tokens, DS)),
        *[full((DS, DS))] * 4,
        full((FS, DS)),
        full((FS, DS)),
        full((8, DS)),
        full((1, WIDER)),
    ]
    given = [grad, vectors, biases, mask, *matrices, *saved]
    if last:
        given += last
        made.append(full((1, length)))
    low = partial(pltpu.VMEM, dtype=jnp.bfloat16)
    return pl.pallas_call(
        partial(back_kernel, bool(last)),
        out_shape=tuple(made),
        in_specs=[VMEM_SPEC] * len(given),
        out_specs=(VMEM_SPEC,) * len(made),
        scratch_shapes=[
            *[low((tokens, DS))] * 6,
            *[low((tokens, WIDER))] * 2,
            pltpu.VMEM((WIDER // 128, DS, 128), jnp.float32),
            pltpu.VMEM((-(-DS // 128), FS, 128), jnp.float32),
        ],
        compiler_params=pltpu.CompilerParams(vmem_limit_bytes=58 * 1024 * 1024),
        cost_estimate=pl.CostEstimate(
            flops=10**9, bytes_accessed=4 * 10**6, transcendentals=3 * 10**5
        ),
    )(*given)


def three_parts(value):
    high = lax.reduce_precision(value, 8, 7)
    rest = value - high
    middle = lax.reduce_precision(rest, 8, 7)
    low = rest - middle
    return jnp.concatenate([high, middle, low], -1).astype(jnp.bfloat16)


def pick_exact(marks, value, turned=False):
    width = value.shape[1]
    terms = three_parts(value)
    made = outer_product(marks, terms) if turned else jnp.dot(
        marks, terms, preferred_element_type=jnp.float32
    )
    return made[:, :width] + made[:, width : 2 * width] + made[:, 2 * width :]


def plan_requests(ids, local_rows):
    order = lax.broadcasted_iota(jnp.int32, (ids.shape[0],), 0)
    same = ids[:, None] == ids[None, :]
    leader = jnp.min(jnp.where(same, order[None, :], ids.shape[0]), 1)
    leads = leader == order
    owner = ids // local_rows
    before = (
        (owner[:, None] == owner[None, :]) & leads[None, :] & (order[None, :] < leader[:, None])
    )
    rank = jnp.sum(before.astype(jnp.int32), 1)
    return (leads, owner, ids - owner * local_rows, rank)


def round_marks(plan, turn, devices):
    leads, owner, local_id, rank = plan
    inside = (rank >= turn * SLOTS) & (rank < (turn + 1) * SLOTS)
    slot = jnp.where(inside, owner * SLOTS + rank - turn * SLOTS, -1)
    line = lax.broadcasted_iota(jnp.int32, (devices * SLOTS, 1), 0)
    hit = line == slot[None, :]
    asked = jnp.max(jnp.where(hit & leads[None, :], local_id[None, :], -1), 1)
    return (hit.astype(jnp.bfloat16), asked.reshape(devices, 1, SLOTS))


def question(plan, turn, devices, extra):
    marks, asked = round_marks(plan, turn, devices)
    fill = jnp.full((devices, 1, 128 - SLOTS - extra.shape[0]), -1, jnp.int32)
    note = jnp.broadcast_to(extra[None, None, :], (devices, 1, extra.shape[0]))
    return (marks, jnp.concatenate([asked, note, fill], 2))


def ask(plan, turn, devices, extra):
    marks, asked = question(plan, turn, devices, extra)
    return (marks, exchange(asked, 0)[:, 0, :SLOTS].reshape(-1))


def wanted_marks(wanted, local_rows):
    return (wanted[:, None] == lax.broadcasted_iota(jnp.int32, (1, local_rows), 1)).astype(
        jnp.bfloat16
    )


def fetch(marks, wanted, table_low, devices):
    rows = jnp.dot(
        wanted_marks(wanted, table_low.shape[0]), table_low, preferred_element_type=jnp.float32
    ).astype(jnp.bfloat16)
    got = exchange(rows.reshape(devices, SLOTS, -1), 1)
    return outer_product(marks, got.reshape(devices * SLOTS, -1))


def give_back(marks, wanted, grads, local_rows, devices):
    sent = pick_exact(marks, grads)
    got = exchange(sent.reshape(devices, SLOTS, -1), 2)
    return pick_exact(wanted_marks(wanted, local_rows), got.reshape(devices * SLOTS, -1), True)


def local(
    token_ids,
    valid_mask,
    seq_ids,
    mask_pos,
    mask_labels,
    teacher_in,
    teacher_flat,
    teacher_vec,
    teacher_head,
    emb_table,
    emb_first,
    emb_second,
    pos_table,
    pos_first,
    pos_second,
    layer_flat,
    layer_first,
    layer_second,
    proj_weight,
    proj_first,
    proj_second,
    layer_vec,
    vec_first,
    vec_second,
    misc_vec,
    misc_first,
    misc_second,
):
    micro, micro_rows, length = token_ids.shape
    rows = micro * micro_rows
    local_rows, width = emb_table.shape
    layers = layer_vec.shape[0]
    picks = mask_pos.shape[2]
    tokens = rows * length
    n_dp, groups = lax.axis_size("dp"), lax.axis_size("fsdp")
    place = lax.axis_index("fsdp")
    devices = n_dp * groups
    hidden_denom = float(rows * devices * length * DT)
    predict_denom = float(rows * devices * picks)
    flat_local = layer_flat.shape[1]
    by_rows = flat_local % DS == 0

    usable = valid_mask.reshape(rows, length) > 0
    docs = seq_ids.reshape(rows, length)
    same_doc = docs[:, :, None] == docs[:, None, :]
    pair_mask = same_doc & usable[:, :, None] & usable[:, None, :]
    allowed = pair_mask | jnp.eye(length, dtype=bool)
    table_low = emb_table.astype(jnp.bfloat16)
    ids = jnp.concatenate([token_ids.reshape(-1), mask_labels.reshape(-1)])
    plan = plan_requests(ids, local_rows)
    extra = jnp.stack([-1 - jnp.sum(pair_mask.astype(jnp.int32)), -1 - jnp.max(plan[3])])
    teacher_lines = teacher_flat.reshape(-1, DT)
    teacher_all = lax.all_gather(teacher_lines, BOTH, axis=0, tiled=True).reshape(-1, CHUNK, DT)
    own_parts = [
        layer_flat.astype(jnp.bfloat16),
        pos_table.astype(jnp.bfloat16),
        proj_weight.astype(jnp.bfloat16).T,
    ]
    if by_rows:
        chunk = flat_local // DS
        own_layers = [woven(part.reshape(-1, DS), False) for part in own_parts[0]]
        own_parts = [part.reshape(1, -1, DS) for part in own_layers + own_parts[1:]]
        line, lines = DS, sum(part.shape[1] for part in own_parts)
    else:
        own_parts = [part.reshape(1, -1) for part in own_parts]
        line, lines = 128, -(-sum(part.shape[1] for part in own_parts) // 128)
    block_rows = -(-lines // 16) * 16
    marks, asked = question(plan, 0, devices, extra)
    got, weights_all, token_blocks = entry(asked, pack(own_parts, line, block_rows)[0], table_low, 3)
    wanted = got[:, 0, :SLOTS].reshape(-1)
    notes = got[:, 0, SLOTS : SLOTS + 2]
    count = jnp.sum(-1 - notes[:, 0]).astype(jnp.float32)
    rounds = jnp.max(-1 - notes[:, 1]) // SLOTS + 1
    all_rows = outer_product(marks, token_blocks.reshape(devices * SLOTS, width))

    def more_rows(state):
        turn, so_far = state
        marks_now, wanted_now = ask(plan, turn, devices, extra)
        return (turn + 1, so_far + fetch(marks_now, wanted_now, table_low, devices))

    all_rows = lax.while_loop(lambda state: state[0] < rounds, more_rows, (1, all_rows))[1]
    token_rows, label_rows = (all_rows[:tokens], all_rows[tokens:])
    pos_local, proj_local = pos_table.shape[0], proj_weight.shape[1]
    if by_rows:
        where = block_plan(devices, chunk, layers, (pos_local, proj_local))
        *matrices, places_all, proj_all = unpack(weights_all, where, layers, length)
    else:
        flat_all = weights_all.reshape(devices, -1)
        split = []
        for index in range(layers):
            wide = flat_all[:, index * flat_local : (index + 1) * flat_local].reshape(WIDE, DS)
            qkv, out, up, down = split_rows(wide, DS, FS)
            split.append(
                (
                    qkv.reshape(DS, 3, DS).transpose(1, 0, 2),
                    out,
                    jnp.pad(up, ((0, 0), (0, WIDER - FS))),
                    jnp.pad(down, ((0, WIDER - FS), (0, 0))),
                )
            )
        matrices = [jnp.stack(group) for group in zip(*split)]
        start = layers * flat_local
        places_all = flat_all[:, start : start + pos_local * DS].reshape(length, DS)
        start += pos_local * DS
        proj_all = flat_all[:, start : start + proj_local * DS].reshape(DT, DS)

    to_owner = [
        (d * groups + f, f * n_dp + d) for d in range(n_dp) for f in range(groups)
    ]
    from_owner = [(owner, holder) for holder, owner in to_owner]
    table_then = lax.optimization_barrier((table_low, teacher_all))[0]
    slice_part = lax.ppermute(table_then, BOTH, from_owner)
    slice_table = lax.all_gather(slice_part, "dp", axis=0, tiled=True)

    proj_bias = misc_vec[2 * DS :]
    evec = misc_vec[: 2 * DS].reshape(2, DS)
    cut = 5 * DS
    vectors = jnp.concatenate([layer_vec[:, :cut], layer_vec[:, cut + FS :]], 1).reshape(
        layers, 8, DS
    )
    biases = jnp.pad(layer_vec[:, cut : cut + FS], ((0, 0), (0, WIDER - FS)))[:, None]

    mask = jnp.where(pair_mask, 2.0, jnp.where(allowed, 1.0, 0.0)).reshape(tokens, length)
    embedded, normed_zero, inverse_zero, hidden, *saved = student_forward(
        token_rows, places_all, evec, vectors, biases, mask, matrices
    )
    t_input = teacher_in.reshape(tokens, DT).astype(jnp.float32)
    t_out, t_scores = teacher_forward(
        teacher_in.reshape(tokens, DT), teacher_all, teacher_vec.astype(jnp.float32)[None], mask
    )
    weight = valid_mask.reshape(tokens, 1).astype(jnp.float32)
    loss_zero, proj_zero, bias_zero, back_zero = hidden_term(
        embedded, t_input, proj_all, proj_bias, weight, hidden_denom
    )
    loss_last, proj_last, bias_last, back_last = hidden_term(
        hidden, t_out, proj_all, proj_bias, weight, hidden_denom
    )
    hidden_sum = loss_zero + loss_last
    grad_proj = proj_zero + proj_last

    flat_pick = (
        jnp.arange(rows, dtype=jnp.int32)[:, None] * length + mask_pos.reshape(rows, picks)
    ).reshape(-1)
    pick_marks = (flat_pick[:, None] == lax.broadcasted_iota(jnp.int32, (1, tokens), 1)).astype(
        jnp.bfloat16
    )
    both_low = jnp.concatenate([hidden.astype(jnp.bfloat16), t_out.astype(jnp.bfloat16)], 1)
    both_picked = jnp.dot(pick_marks, both_low, preferred_element_type=jnp.float32).astype(
        jnp.bfloat16
    )
    picked = both_picked[:, :width]
    both_all = exchange(both_picked, 4, whole=False, spread=True).reshape(-1, width + DT)
    picked_all, t_picked_all = both_all[:, :width], both_all[:, width:]
    s_logits = jnp.einsum("gd,vd->gv", picked_all, slice_table, preferred_element_type=jnp.float32)
    t_logits = jnp.einsum(
        "gd,vd->gv", t_picked_all, teacher_head, preferred_element_type=jnp.float32
    )
    s_top = jnp.max(s_logits, -1)
    t_top = jnp.max(t_logits, -1)
    t_exp = jnp.exp(t_logits - t_top[:, None])
    local_stats = jnp.stack(
        [
            s_top,
            jnp.sum(jnp.exp(s_logits - s_top[:, None]), -1),
            t_top,
            jnp.sum(t_exp, -1),
            jnp.sum(t_exp * s_logits, -1),
        ]
    )
    stats_all = exchange(local_stats, 5, whole=False, spread=True)
    stats = tuple(stats_all[0])
    for other in range(1, groups):
        stats = combine_stats(stats, tuple(stats_all[other]))
    s_top, s_sum, t_top, t_sum, cross = stats
    log_total = s_top + jnp.log(s_sum)
    d_logits = (
        2.0 * jnp.exp(s_logits - log_total[:, None])
        - jnp.exp(t_logits - t_top[:, None]) / t_sum[:, None]
    ) / predict_denom
    d_logits = d_logits.astype(jnp.bfloat16)
    grad_slice = outer_product(d_logits, picked_all)
    d_logits, grad_slice = lax.optimization_barrier((d_logits, grad_slice))
    if n_dp == 4:
        to_send = [sum_cores, sum_along_x, lambda part: lax.ppermute(part, BOTH, to_owner)]
    else:
        to_send = [
            lambda value: lax.psum_scatter(value, "dp", scatter_dimension=0, tiled=True),
            lambda part: lax.ppermute(part, BOTH, to_owner),
        ]
    d_logits, head_grad = lax.optimization_barrier((d_logits, to_send.pop(0)(grad_slice)))
    if len(to_send) > 1:
        head_grad = to_send.pop(0)(head_grad)
    d_picked_all = jnp.dot(d_logits, slice_table, preferred_element_type=jnp.float32)
    d_picked = jnp.sum(
        exchange(
            d_picked_all.astype(jnp.bfloat16).reshape(groups, rows * picks, width), 6, whole=False
        ).astype(jnp.float32),
        0,
    )
    picked_wide = picked.astype(jnp.float32)
    target_logit = jnp.sum(picked_wide * label_rows, -1)
    own_start = place * rows * picks
    own_total = lax.dynamic_slice_in_dim(log_total, own_start, rows * picks, 0)
    own_cross = lax.dynamic_slice_in_dim(cross / t_sum, own_start, rows * picks, 0)
    predict_sum = jnp.sum(2.0 * own_total - own_cross - target_logit) / predict_denom
    d_picked = d_picked - label_rows / predict_denom
    d_hidden = pick_exact(pick_marks, d_picked, True) + back_last

    matrix_grads = [None] * layers
    vector_grads = [None] * layers
    attention_sum = jnp.float32(0.0)
    d_hidden, head_grad = lax.optimization_barrier((d_hidden, head_grad))
    head_grad = to_send.pop(0)(head_grad)
    for layer_index in reversed(range(layers)):
        d_hidden, *others = student_backward(
            d_hidden,
            vectors[layer_index],
            biases[layer_index],
            mask,
            [matrix[layer_index] for matrix in matrices],
            [kept[layer_index] for kept in saved],
            [t_scores, count.reshape(1, 1)] if layer_index == layers - 1 else [],
        )
        matrix_grads[layer_index] = others[:6]
        d_vectors, d_bias_up, square = others[6], others[7], others[8:]
        d_vectors = d_vectors.reshape(-1)
        vector_grads[layer_index] = jnp.concatenate(
            [d_vectors[:cut], d_bias_up[0, :FS], d_vectors[cut:]]
        )
        if square:
            attention_sum = jnp.sum(square[0]) / count
    d_hidden, head_grad = lax.optimization_barrier((d_hidden, head_grad))
    d_token, d_gain, d_bias = norm_backward(
        d_hidden + back_zero, normed_zero, inverse_zero, misc_vec[:DS]
    )
    grad_places = jnp.sum(d_token.reshape(rows, length, width), 0)

    row_grads = jnp.concatenate([d_token, -picked_wide / predict_denom])
    def more_grads(state):
        turn, so_far = state
        marks_now, wanted_now = ask(plan, turn, devices, extra)
        return (
            turn + 1,
            so_far + give_back(marks_now, wanted_now, row_grads, local_rows, devices),
        )

    grad_small = jnp.concatenate(vector_grads + [d_gain, d_bias, bias_zero + bias_last])
    small_local = -(-grad_small.shape[0] // devices)
    small_local = -(-small_local // DS) * DS
    small_padded = jnp.pad(grad_small, (0, devices * small_local - grad_small.shape[0]))
    rest = [grad_places, grad_proj, small_padded.reshape(-1, DS)]
    sizes = [flat_local] * layers + [part.size // devices for part in rest]
    lines = -(-sum(sizes) // line)
    block = (-(-lines // 8) * 8, line)
    sent = pick_exact(marks, row_grads).reshape(devices, SLOTS, width)
    if by_rows:
        amounts = [size // DS for size in sizes[layers:]]
        grad_parts = sum(matrix_grads, []) + rest
        block_rows_of = block_plan(devices, chunk, layers, amounts)
    else:
        wides = []
        for grads in matrix_grads:
            first = jnp.stack(grads[:3], 1).reshape(-1, width)
            wides.append(jnp.concatenate([first, *grads[3:]]))
        grad_parts = [pack([part.reshape(devices, -1) for part in wides + rest], *block[::-1])]
        block_rows_of = ()
    reduced, row_blocks = reduce(grad_parts, block_rows_of, block, sent, 7)
    g_table = pick_exact(
        wanted_marks(wanted, local_rows), row_blocks.reshape(devices * SLOTS, width), True
    )
    g_table = lax.while_loop(lambda state: state[0] < rounds, more_grads, (1, g_table))[1]
    g_table = g_table + head_grad
    if by_rows:
        pieces = []
        start = 0
        for size in sizes:
            pieces.append(reduced[start : start + size // DS])
            start += size // DS
    else:
        pieces = cut_pieces(reduced.reshape(-1), sizes)
    if by_rows:
        pieces[:layers] = [woven(piece, True) for piece in pieces[:layers]]
    layer_acc = jnp.stack([piece.reshape(-1) for piece in pieces[:layers]])
    g_places = pieces[layers].reshape(pos_local, DS)
    g_proj = pieces[layers + 1].reshape(proj_local, DS).T
    small_part = pieces[layers + 2].reshape(-1)
    squares = (
        jnp.sum(g_table * g_table)
        + jnp.sum(g_places * g_places)
        + jnp.sum(g_proj * g_proj)
        + jnp.sum(layer_acc * layer_acc)
        + jnp.sum(small_part * small_part)
    )
    note = jnp.concatenate(
        [small_part, jnp.stack([attention_sum + hidden_sum + predict_sum, squares])]
    )
    note = jnp.pad(note, (0, -(-note.shape[0] // 128) * 128 - note.shape[0])).reshape(1, -1)
    notes_all = exchange(note, 8, spread=True)[:, 0]
    small = notes_all[:, :small_local].reshape(-1)
    loss = jnp.sum(notes_all[:, small_local])
    norm = jnp.sqrt(jnp.sum(notes_all[:, small_local + 1]))
    g_vec = small[: layer_vec.size].reshape(layer_vec.shape)
    g_misc = small[layer_vec.size : layer_vec.size + misc_vec.shape[0]]
    factor = CLIP_NORM / jnp.maximum(norm, CLIP_NORM)
    return (
        loss,
        count,
        norm,
        *adam_update(emb_table, emb_first, emb_second, g_table * factor),
        *adam_update(pos_table, pos_first, pos_second, g_places * factor),
        *adam_update(layer_flat, layer_first, layer_second, layer_acc * factor),
        *adam_update(proj_weight, proj_first, proj_second, g_proj * factor),
        *adam_update(layer_vec, vec_first, vec_second, g_vec * factor),
        *adam_update(misc_vec, misc_first, misc_second, g_misc * factor),
    )


def solution(mesh):
    rows, lines, flat, tail, every = (
        P(None, BOTH),
        P(BOTH, None),
        P(BOTH),
        P(None, BOTH),
        P(),
    )
    placed = (
        *[rows] * 6,
        flat,
        every,
        P("fsdp", None),
        *[lines] * 6,
        *[tail] * 6,
        *[every] * 6,
    )
    return jax.shard_map(
        local,
        mesh=mesh,
        in_specs=placed,
        out_specs=(*[every] * 3, *[lines] * 6, *[tail] * 6, *[every] * 6),
        check_vma=False,
    )
```

time: 2340 us -> 805 us (0.34)
  blocking collectives: 657 us -> 0 us
  waiting for transfers between devices: 573 us -> 0.06 us
  local copies, waits for them, and re-layouts: 601 us -> 105 us
  Pallas kernels: 0 us -> 491 us
  matrix products: 221 us -> 62.2 us
  other arithmetic: 238 us -> 90.6 us
    all_gather x16 -> x0, blocking collectives: 578 us -> none  [the longest x10 303 us: merged(): everything = jax.tree.map(lambda part: lax.all_gather(part, axis), x)]
    pallas_call x0 -> x11, Pallas kernels: none -> 491 us  [the longest x4 139 us: exchange(): pl.pallas_call(partial(exchange_kernel, count, whole, spread), out_shape=...]
    reduce_scatter x3 -> x0, waiting for transfers between devices: 457 us -> none  [the longest x1 405 us: local(): lax.psum_scatter(grad_table, ('dp', 'fsdp'), scatter_dimension=0, tiled=T...]
    concatenate x29 -> x6, local copies, waits for them, and re-layouts: 139 us -> 0.65 us  [the longest x2 0.33 us: woven(): made = jnp.where(me == index, jnp.concatenate([head, block[amount:]]), made)]
    scatter-add x8 -> x0, other arithmetic: 132 us -> none  [the longest x2 72.2 us: local(): grad_table = grad_table.at[token_ids[micro_index].reshape(-1)].add(d_token)]
    unnamed x11 -> x2, waiting for transfers between devices: 116 us -> 0.03 us
    slice x52 -> x25, local copies, waits for them, and re-layouts: 111 us -> 22.7 us  [the longest x1 10.8 us: sum_cores(): kept = jnp.where(first, parts[:, 0], parts[:, 1])]
    dot_general x54 -> x4, matrix products: 95.6 us -> 10.4 us  [the longest x2 4.36 us: hidden_term(): jnp.dot(d_mapped, proj_turned, preferred_element_type=jnp.float32)]
  transfers between devices with their start and end apart: 8 -> 6, of which waited for: 3 -> 0; matrix products, arithmetic and copies ran while one was open for 34% -> 13% of each run, Pallas kernels for 0% -> 43%
where the time goes in v1:
time: 805 us; the launch traced here: 794 us
  Pallas kernels  491 us (61%)
  local copies, waits for them, and re-layouts  105 us (13%)
  other arithmetic  90.6 us (11%)
  matrix products  62.2 us (8%)
  between operations  28.6 us (4%)
  starting transfers between devices  15.6 us (2%)
    pallas_call x4, Pallas kernels, exchange(): pl.pallas_call(partial(exchange_kernel, count, whole, spread), out_shape=...  139 us
    pallas_call x1, Pallas kernels, reduce(): pl.pallas_call(partial(reduce_kernel, plan, len(parts)), out_shape=(jax.S...  113 us
    pallas_call x2, Pallas kernels, student_backward(): pl.pallas_call(partial(back_kernel, bool(last)), out_shape=tuple(made), i...  74.6 us
    pallas_call x1, Pallas kernels, entry(): pl.pallas_call(entry_kernel, out_shape=(jax.ShapeDtypeStruct(asked.shape,...  72.8 us
    pallas_call x1, Pallas kernels, student_forward(): pl.pallas_call(partial(student_kernel, layers), out_shape=made, in_specs=...  50.6 us
    pallas_call x1, Pallas kernels, teacher_forward(): pl.pallas_call(teacher_kernel, out_shape=(jax.ShapeDtypeStruct((tokens, D...  33.5 us
    unnamed x169, local copies, waits for them, and re-layouts  24 us
    dot_general x6, matrix products, outer_product(): lax.dot_general(left, right, (((0,), (0,)), ((), ())), preferred_element_...  17.5 us
  transfers between devices with their start and end apart: 6, of which 0 were waited for; matrix products, arithmetic and copies ran while one was open for 13% of the time, Pallas kernels for 43%

profile of v1, /device:TPU:0, one launch (start us, length us, event | category | flops | bytes accessed | tf_op | source)
XLA Modules:
  0.0 793.6 jit_solution(2663271124996564540)
XLA Ops:
  25.8 72.8 %shard_map.418 = (s32[32,1,128]{2,1,0:T(1,128)S(1)}, bf16[32,256,312]{2,1,0:T(8,128)(2,1)S(1)}, bf16[32,48,312]{2,1,0:T(8,128)(2,1)S(1)}) custom-call(s32[32,1,128]{2,1,0:T(1,128)S(1)} %add_add_fusion.2.ask_ref, bf16[256,312]{1,0:T(8,128)(2,1)S(1)} %maximum_bitcast_fusion.w_ref, bf16[960,312]{1,0:T(8,128)(2,1)S(1)} %copy.189.table_ref), custom_call_target="tpu_custom_call" | custom-call | tf_op jit(solution)/shard_map/pallas_call | solution.py:291
  114.3 8.0 %shard_map.419 = (bf16[2,3,312,312]{3,2,1,0:T(8,128)(2,1)S(1)}, bf16[2,312,312]{2,1,0:T(8,128)(2,1)S(1)}, bf16[2,312,1280]{2,1,0:T(8,128)(2,1)}, bf16[2,1280,312...) custom-call(bf16[32,256,312]{2,1,0:T(8,128)(2,1)} %copy-done), custom_call_target="tpu_custom_call" | custom-call | bytes 20000000 | tf_op jit(solution)/shard_map/pallas_call | solution.py:797
  125.4 50.6 %shard_map.420 = (f32[1024,312]{1,0:T(8,128)}, f32[1024,312]{1,0:T(8,128)}, f32[1024,1]{1,0:T(8,128)}, f32[1024,312]{1,0:T(8,128)}, bf16[2,1024,312]{2,1,0:T(8,1...) custom-call(f32[1024,312]{1,0:T(8,128)} %slice.484.token_ref, ...), custom_call_target="tpu_custom_call" | custom-call | flops 8000000000 | bytes 40000000 | tf_op jit(solution)/shard_map/pallas_call | solution.py:920
  196.2 5.1 slice_bitcast_fusion
  206.9 33.5 %shard_map.421 = (f32[1024,768]{1,0:T(8,128)}, f32[1024,1536]{1,0:T(8,128)}) custom-call(bf16[1024,768]{1,0:T(8,128)(2,1)} %bitcast.228, bf16[96,96,768]{2,1,0:T(8,128)(2,1)} %bitcast.227, f32[1,9984]{1,0:T(1,128)} %reshape.1026.vec_ref, f32[1024,128]{1,0:T(8,128)} %select_select_fusion.mask_ref), custom_call_target="tpu_custom_call" | custom-call | flops 20000000000 | bytes 25000000 | tf_op jit(solution)/shard_map/pallas_call | solution.py:716
  244.2 76.7 %shard_map.422 = bf16[8,160,1080]{2,1,0:T(8,128)(2,1)} custom-call(bf16[160,1080]{1,0:T(8,128)(2,1)} %convolution_convert_fusion.1.x_ref), custom_call_target="tpu_custom_call" | custom-call | tf_op jit(solution)/shard_map/pallas_call | solution.py:92
  320.9 15.0 %fusion.108 = (f32[1280]{0:T(1024)S(1)}, f32[1280,3840]{1,0:T(8,128)}) fusion(bf16[3840,768]{1,0:T(8,128)(2,1)} %param.39, bf16[1280,1080]{1,0:T(8,128)(2,1)} %bitcast.197), kind=kOutput, calls=%fused_computation.352 | convolution fusion | flops 7554661376 | bytes 27530240 | tf_op jit(solution)/shard_map/gd,vd->gv/dot_general | solution.py:1317
  339.7 4.6 reshape.1028
  344.3 7.4 fusion.107
  351.7 17.1 %multiply_reduce_fusion = (f32[1280]{0:T(1024)S(1)}, f32[1280]{0:T(1024)S(1)}, f32[1280]{0:T(1024)S(1)}) fusion(f32[1280,3840]{1,0:T(8,128)S(1)} %get-tuple-element.480, f32[1280,3840]{1,0:T(8,128)} %get-tuple-element.482, f32[1280]{0:T(1024)S(1)} %get-tuple-element.481, f32[1280]{0:T(1024)S(1)} %get-tuple-element.479), kind=kLoop, calls=%fused_computation.41 | loop fusion | flops 29487360 | bytes 39347200 | tf_op jit(solution)/shard_map/reduce_sum | solution.py:1329
  369.5 26.4 %shard_map.423 = f32[8,5,1280]{2,1,0:T(8,128)} custom-call(f32[5,1280]{1,0:T(8,128)} %stack.44.x_ref), custom_call_target="tpu_custom_call" | custom-call | tf_op jit(solution)/shard_map/pallas_call | solution.py:92
  402.2 15.7 %multiply_convert_fusion = bf16[1280,3840]{1,0:T(8,128)(2,1)S(1)} fusion(f32[1280,3840]{1,0:T(8,128)} %get-tuple-element.482, f32[1280,3840]{1,0:T(8,128)} %copy-done.5, f32[1280]{0:T(1024)S(1)} %get-tuple-element.416, f32[1280]{0:T(1024)S(1)} %get-tuple-element.421, f32[1280]{0:T(1024)S(1)} %log_add_fusion), kind=kLoop, calls=%fused_computation.40 | loop fusion | flops 34406400 | bytes 49167360 | tf_op jit(solution)/shard_map/convert_element_type | solution.py:1342
  421.6 7.1 fusion.45
  428.7 7.9 reshape.1008
  436.6 10.8 %fusion.104 = (f32[2,1,960,312]{2,1,0,3:T(1,128)S(1)}, f32[2,1,960,312]{2,1,0,3:T(1,128)}) fusion(f32[2,2,960,312]{2,1,0,3:T(2,128)} %reshape.1008), kind=kLoop, calls=%fused_computation.348 | loop fusion | bytes 9584640 | tf_op jit(solution)/shard_map/slice | solution.py:595
  455.3 5.0 fusion.29
  469.5 4.2 convolution_convert_fusion
  475.9 22.3 %shard_map.424 = bf16[8,160,312]{2,1,0:T(8,128)(2,1)} custom-call(bf16[8,160,312]{2,1,0:T(8,128)(2,1)} %bitcast.200), custom_call_target="tpu_custom_call" | custom-call | tf_op jit(solution)/shard_map/pallas_call | solution.py:92
  506.4 11.2 %collective-permute-start.3 = (f32[960,312]{0,1:T(8,128)}, f32[960,312]{0,1:T(8,128)}, u32[]{:S(2)}, u32[]{:S(2)}) collective-permute-start(f32[960,312]{0,1:T(8,128)} %bitcast_add_fusion.1), channel_id=1, source_target_pairs={{0,0},{1,4},{2,8},{3,12},{4,16},{5,20},{6,24},{7,28},{8,1},{9,5},{... | collective-permute-start | bytes 3594248 | tf_op jit(solution)/shard_map/ppermute | solution.py:1346
  526.0 38.7 %shard_map.425 = (f32[1024,312]{1,0:T(8,128)}, f32[312,312]{1,0:T(8,128)}, f32[312,312]{1,0:T(8,128)}, f32[312,312]{1,0:T(8,128)}, f32[312,312]{1,0:T(8,128)}, /...) custom-call(f32[1024,312]{1,0:T(8,128)} %fusion.43.grad_ref, ...), custom_call_target="tpu_custom_call" | custom-call | flops 1000000000 | bytes 4000000 | tf_op jit(solution)/shard_map/pallas_call | solution.py:1072
  566.7 35.9 %shard_map.426 = (f32[1024,312]{1,0:T(8,128)}, f32[312,312]{1,0:T(8,128)}, f32[312,312]{1,0:T(8,128)}, f32[312,312]{1,0:T(8,128)}, f32[312,312]{1,0:T(8,128)}, /...) custom-call(f32[1024,312]{1,0:T(8,128)} %get-tuple-element.260.grad_ref, ...), custom_call_target="tpu_custom_call" | custom-call | flops 1000000000 | bytes 4000000 | tf_op jit(solution)/shard_map/pallas_call | solution.py:1072
  613.4 4.3 fusion.21
  620.4 112.7 %shard_map.427 = (f32[264,312]{1,0:T(8,128)}, f32[32,48,312]{2,1,0:T(8,128)}) custom-call(f32[312,312]{1,0:T(8,128)} %get-tuple-element.261.refs_0_, f32[312,312]{1,0:T(8,128)} %get-tuple-element.262.refs_1_, f32[312,312]{1,0:T(8,128)} %get-tuple-element.263.refs_2_, f32[312,312]{1,0:T(8,128)} %get-tuple-element.264.refs_3_, ...), custom_call_target="tpu_custom_call" | custom-call | tf_op jit(solution)/shard_map/pallas_call | solution.py:439
  755.7 13.3 %shard_map.428 = f32[32,1,384]{2,1,0:T(1,128)} custom-call(f32[1,384]{1,0:T(1,128)} %reshape.1024.x_ref), custom_call_target="tpu_custom_call" | custom-call | tf_op jit(solution)/shard_map/pallas_call | solution.py:92
  (360 shorter events, 158.8 us)
Async XLA Ops:
  7.2 185.6 %all-gather.4.cloned.1.call-start = ((), (), s32[]{:S(2)}) async-start(), calls=%async_computation | async-start | bytes 14598144 | tf_op jit(solution)/shard_map/all_gather | solution.py:1215
  9.5 15.7 %copy-start.16 = (f32[960,312]{0,1:T(8,128)S(1)}, f32[960,312]{0,1:T(8,128)}, u32[]{:S(2)}) copy-start(f32[960,312]{0,1:T(8,128)} %param.40) | copy-start | bytes 3594244
  9.5 326.5 %all-gather.6.cloned.1.call-start = ((), (), s32[]{:S(2)}) async-start(), calls=%async_computation.1 | async-start | bytes 3194880 | tf_op jit(solution)/shard_map/all_gather | solution.py:1275
  20.4 85.9 %copy-start.69 = (s32[1184]{0:T(1024)}, s32[1184]{0:T(1024)S(1)}, u32[]{:S(2)}) copy-start(s32[1184]{0:T(1024)S(1)} %get-tuple-element.475) | copy-start | bytes 14212
  25.2 79.1 %slice-start.3 = ((f32[1392]{0:T(1024)}), f32[624]{0:T(1024)S(1)}, s32[]{:S(2)}) async-start(f32[1392]{0:T(1024)} %param.55), calls=%async_computation.5 | async-start | bytes 8192 | tf_op jit(solution)/shard_map/slice | solution.py:1278
  193.9 7.4 collective-permute-start
  206.7 35.8 %copy-start.25 = (bf16[1024,312]{1,0:T(8,128)(2,1)}, bf16[1024,312]{1,0:T(8,128)(2,1)S(1)}, u32[]{:S(2)}) copy-start(bf16[1024,312]{1,0:T(8,128)(2,1)S(1)} %convert_element_type.107) | copy-start | bytes 1916932
  351.7 17.1 %copy-start.5 = (f32[1280,3840]{1,0:T(8,128)}, f32[1280,3840]{1,0:T(8,128)S(1)}, u32[]{:S(2)}) copy-start(f32[1280,3840]{1,0:T(8,128)S(1)} %get-tuple-element.480) | copy-start | bytes 58982404
  450.8 12.4 %collective-permute-start.1 = (f32[2,960,312]{1,2,0:T(8,128)S(1)}, f32[2,960,312]{1,2,0:T(8,128)S(1)}, u32[]{:S(2)}, u32[]{:S(2)}) collective-permute-start(f32[2,960,312]{1,2,0:T(8,128)S(1)} %select_bitcast_fusion), channel_id=1, source_target_pairs={{0,8},{8,0},{16,24},{24,16},{1,9},{9,1},{17,25},{25,17},{2,10},{10... | collective-permute-start | bytes 7188488 | tf_op jit(solution)/shard_map/ppermute | solution.py:596
  466.9 38.0 %collective-permute-start.2 = (f32[960,312]{0,1:T(8,128)S(1)}, f32[960,312]{0,1:T(8,128)S(1)}, u32[]{:S(2)}, u32[]{:S(2)}) collective-permute-start(f32[960,312]{0,1:T(8,128)S(1)} %select_bitcast_fusion.1), channel_id=1, source_target_pairs={{0,16},{16,0},{8,24},{24,8},{1,17},{17,1},{9,25},{25,9},{2,18},{18... | collective-permute-start | bytes 3594248 | tf_op jit(solution)/shard_map/ppermute | solution.py:603
  475.9 23.7 %copy-start.46 = (bf16[160,1080]{1,0:T(8,128)(2,1)S(1)}, bf16[160,1080]{1,0:T(8,128)(2,1)}, u32[]{:S(2)}) copy-start(bf16[160,1080]{1,0:T(8,128)(2,1)} %convolution_convert_fusion.1.x_ref) | copy-start | bytes 1036804
  506.4 98.7 %collective-permute-start.3 = (f32[960,312]{0,1:T(8,128)}, f32[960,312]{0,1:T(8,128)}, u32[]{:S(2)}, u32[]{:S(2)}) collective-permute-start(f32[960,312]{0,1:T(8,128)} %bitcast_add_fusion.1), channel_id=1, source_target_pairs={{0,0},{1,4},{2,8},{3,12},{4,16},{5,20},{6,24},{7,28},{8,1},{9,5},{... | collective-permute-start | bytes 3594248 | tf_op jit(solution)/shard_map/ppermute | solution.py:1346
  566.6 36.8 %copy-start.56 = (f32[8,312]{1,0:T(8,128)S(1)}, f32[8,312]{1,0:T(8,128)}, u32[]{:S(2)}) copy-start(f32[8,312]{1,0:T(8,128)} %get-tuple-element.281) | copy-start | bytes 29956
  566.6 38.4 %copy-start.72 = (f32[1,1280]{1,0:T(1,128)S(1)}, f32[1,1280]{1,0:T(1,128)}, u32[]{:S(2)}) copy-start(f32[1,1280]{1,0:T(1,128)} %get-tuple-element.282) | copy-start | bytes 15364
  566.6 38.5 %copy-start.13 = (f32[1024,312]{1,0:T(8,128)S(1)}, f32[1024,312]{1,0:T(8,128)}, u32[]{:S(2)}) copy-start(f32[1024,312]{1,0:T(8,128)} %get-tuple-element.278) | copy-start | bytes 3833860
  566.7 38.5 %copy-start.38 = (f32[1024,312]{1,0:T(8,128)S(1)}, f32[1024,312]{1,0:T(8,128)}, u32[]{:S(2)}) copy-start(f32[1024,312]{1,0:T(8,128)} %fusion.109) | copy-start | bytes 3833860
  749.4 22.7 %copy-start.58 = (f32[4,312]{1,0:T(4,128)S(1)}, f32[4,312]{1,0:T(4,128)}, u32[]{:S(2)}) copy-start(f32[4,312]{1,0:T(4,128)} %param.43) | copy-start | bytes 14980
  749.4 22.7 %copy-start.71 = (f32[4,312]{1,0:T(4,128)S(1)}, f32[4,312]{1,0:T(4,128)}, u32[]{:S(2)}) copy-start(f32[4,312]{1,0:T(4,128)} %param.45) | copy-start | bytes 14980
  749.4 25.6 %copy-start.55 = (f32[1392]{0:T(1024)S(1)}, f32[1392]{0:T(1024)}, u32[]{:S(2)}) copy-start(f32[1392]{0:T(1024)} %param.55) | copy-start | bytes 16708
  749.4 25.6 %copy-start.62 = (f32[1392]{0:T(1024)S(1)}, f32[1392]{0:T(1024)}, u32[]{:S(2)}) copy-start(f32[1392]{0:T(1024)} %param.57) | copy-start | bytes 16708
  749.4 25.6 %copy-start.63 = (f32[1392]{0:T(1024)S(1)}, f32[1392]{0:T(1024)}, u32[]{:S(2)}) copy-start(f32[1392]{0:T(1024)} %param.56) | copy-start | bytes 16708
  749.4 26.3 %copy-start.44 = (f32[2,35568]{1,0:T(2,128)S(1)}, f32[2,35568]{1,0:T(2,128)}, u32[]{:S(2)}) copy-start(f32[2,35568]{1,0:T(2,128)} %param.46) | copy-start | bytes 853636
  749.4 26.3 %copy-start.50 = (f32[2,35568]{1,0:T(2,128)S(1)}, f32[2,35568]{1,0:T(2,128)}, u32[]{:S(2)}) copy-start(f32[2,35568]{1,0:T(2,128)} %param.48) | copy-start | bytes 853636
  751.8 28.4 %copy-start.17 = (f32[960,312]{0,1:T(8,128)S(1)}, f32[960,312]{0,1:T(8,128)}, u32[]{:S(2)}) copy-start(f32[960,312]{0,1:T(8,128)} %param.40) | copy-start | bytes 3594244
  (66 other events, 289.1 us)
Sparse Core Ops, SparseCore 0:
  11.0 135.9 all-gather.3
  202.3 50.4 all-gather.5

commit v2 on v1

--- a/solution.py
+++ b/solution.py
@@ -30,6 +30,10 @@
 MESH = pl.DeviceIdType.MESH
 SLOTS = 48
 WIDE = 3 * DS + DS + 2 * FS
+
+
+def z_size_of(fsdp):
+    return 4 if fsdp % 4 == 0 else 1
 
 
 def place_of():
@@ -106,7 +110,7 @@
 class Grid:
     def __init__(self):
         self.fsdp = lax.axis_size("fsdp")
-        self.z_size = 4 if self.fsdp % 4 == 0 else 1
+        self.z_size = z_size_of(self.fsdp)
         self.side = self.fsdp // self.z_size
         assert lax.axis_size("dp") == 2 * self.side
         dp, fsdp = lax.axis_index("dp"), lax.axis_index("fsdp")
@@ -392,10 +396,12 @@
         for z in range(z_size):
             from_second[step, z] = (second_in.at[(step - 1) * z_size + z], index)
             index += 1
-    for z in range(1, z_size):
-        from_z[z] = (z_in.at[z - 1], index)
-        index += 1
-    for number, key in enumerate(order):
+    for way in (1, -1):
+        for distance in range(z_size - 1):
+            from_z[way, distance] = (z_in.at[len(from_z)], index)
+            index += 1
+
+    def gathered(key):
         third, second, z = key
         arrived(held.at[rank[key]], rank[key])
         total = held[rank[key]] + x_ref[grid.index(*key)]
@@ -407,22 +413,65 @@
             for step in range(1, side):
                 arrived(*from_second[step, z])
                 total = total + from_second[step, z][0][...]
-        if key == (0, 0, 0):
-            for step in range(1, z_size):
-                arrived(*from_z[step])
-                total = total + from_z[step][0][...]
-            o_ref[...] = total
+        return total
+
+    for number, key in enumerate(order):
+        third, second, z = key
+        if third == 0 and second == 0:
             continue
-        held[rank[key]] = total
+        held[rank[key]] = gathered(key)
         if third:
             target, where = from_third[third, second, z], (third, 0, 0, 0)
-        elif second:
+        else:
             target, where = from_second[second, z], (0, second, 0, 0)
-        else:
-            target, where = from_z[z], (0, 0, z, 0)
         push(held.at[rank[key]], target[0], target[1], where)
         if number == 0:
             lax.fori_loop(1, devices, row_start, 0)
+
+    def behind(way):
+        return (grid.z > 0) if way > 0 else (grid.z < z_size - 1)
+
+    def hop(way, distance):
+        target = from_z[way, distance - 1]
+        return pltpu.make_async_remote_copy(
+            held.at[rank[0, 0, way * distance % z_size]],
+            target[0],
+            send.at[target[1]],
+            recv.at[target[1]],
+            device_id=grid.at(0, 0, way % z_size),
+            device_id_type=MESH,
+        )
+
+    def reaches(way, distance):
+        return (grid.z + way * distance >= 0) & (grid.z + way * distance < z_size)
+
+    for distance in range(z_size - 1, 0, -1):
+        for way in (1, -1):
+
+            @pl.when(reaches(way, distance))
+            def _(way=way, distance=distance):
+                key = (0, 0, way * distance % z_size)
+                held[rank[key]] = gathered(key)
+                if distance < z_size - 1:
+
+                    @pl.when(behind(way))
+                    def _():
+                        arrived(*from_z[way, distance])
+                        held[rank[key]] += from_z[way, distance][0][...]
+
+                hop(way, distance).start()
+
+    o_ref[...] = gathered((0, 0, 0))
+    for way in (1, -1):
+
+        @pl.when(behind(way))
+        def _(way=way):
+            arrived(*from_z[way, 0])
+            o_ref[...] += from_z[way, 0][0][...]
+
+    for distance in range(z_size - 1, 0, -1):
+        for way in (1, -1):
+            pl.when(reaches(way, distance))(hop(way, distance).wait_send)
     for copy in started:
         copy.wait_send()
     own.wait()
@@ -449,8 +498,9 @@
             pltpu.VMEM((count // 2,) + block, kind),
             pltpu.VMEM(((side - 1) * side * z_size,) + block, kind),
             pltpu.VMEM(((side - 1) * z_size,) + block, kind),
-            pltpu.VMEM((z_size - 1,) + block, kind),
-            *[dma((count,))] * 4,
+            pltpu.VMEM((2 * (z_size - 1),) + block, kind),
+            *[dma((count + z_size,))] * 2,
+            *[dma((count,))] * 2,
             dma,
         ],
         compiler_params=pltpu.CompilerParams(
@@ -562,19 +612,6 @@
     )
 
 
-def combine_stats(first_half, second_half):
-    s_top = jnp.maximum(first_half[0], second_half[0])
-    s_sum = first_half[1] * jnp.exp(first_half[0] - s_top) + second_half[1] * jnp.exp(
-        second_half[0] - s_top
-    )
-    t_top = jnp.maximum(first_half[2], second_half[2])
-    scale_one = jnp.exp(first_half[2] - t_top)
-    scale_two = jnp.exp(second_half[2] - t_top)
-    t_sum = first_half[3] * scale_one + second_half[3] * scale_two
-    cross = first_half[4] * scale_one + second_half[4] * scale_two
-    return (s_top, s_sum, t_top, t_sum, cross)
-
-
 def hidden_term(source, target, proj_turned, proj_bias, weight, denom):
     source_low = source.astype(jnp.bfloat16)
     mapped = back_product(source_low, proj_turned) + proj_bias
@@ -588,12 +625,9 @@
     )
 
 
-def sum_cores(value):
-    first = lax.axis_index("dp") % 2 == 0
+def own_parts_of(value):
     parts = value.reshape(2, 2, -1, value.shape[1])
-    given = jnp.where(first, parts[:, 1], parts[:, 0])
-    kept = jnp.where(first, parts[:, 0], parts[:, 1])
-    return kept + lax.ppermute(given, "dp", [(0, 1), (1, 0), (2, 3), (3, 2)])
+    return jnp.where(lax.axis_index("dp") % 2 == 0, parts[:, 0], parts[:, 1])
 
 
 def sum_along_x(parts):
@@ -759,9 +793,10 @@
             target[tile, pl.ds(row, groups, stride=step_out), :] = made
 
 
-def unpack_kernel(plan, layers, w_ref, qkv_ref, out_ref, up_ref, down_ref, place_ref, proj_ref, *scratch):
-    square, wide, folded, unfolded, small = scratch
+def unpack_kernel(plan, layers, w_ref, *refs):
+    place_ref, proj_ref, square, wide, folded, unfolded, small = refs[4 * layers :]
     for layer in range(layers):
+        qkv_ref, out_ref, up_ref, down_ref = refs[4 * layer : 4 * layer + 4]
         for matrix, at, rows, block, line in plan:
             part = matrix - 6 * layer
             if not 0 <= part < 6:
@@ -776,13 +811,13 @@
             else:
                 wide[at : at + rows, :] = value
         for part in range(3):
-            qkv_ref[layer, part] = square[part].astype(jnp.bfloat16)
-        out_ref[layer] = square[3].astype(jnp.bfloat16)
+            qkv_ref[part] = square[part].astype(jnp.bfloat16)
+        out_ref[...] = square[3].astype(jnp.bfloat16)
         refold(folded, unfolded, DS, FS)
         for tile in range(WIDER // 128):
-            up_ref[layer, :, 128 * tile : 128 * tile + 128] = unfolded[tile].astype(jnp.bfloat16)
-        down_ref[layer, :FS, :] = wide[...].astype(jnp.bfloat16)
-        down_ref[layer, FS:, :] = jnp.zeros((WIDER - FS, DS), jnp.bfloat16)
+            up_ref[:, 128 * tile : 128 * tile + 128] = unfolded[tile].astype(jnp.bfloat16)
+        down_ref[:FS, :] = wide[...].astype(jnp.bfloat16)
+        down_ref[FS:, :] = jnp.zeros((WIDER - FS, DS), jnp.bfloat16)
     for matrix, at, rows, block, line in plan:
         if matrix >= 6 * layers:
             value = w_ref[block].astype(jnp.float32)[line : line + rows]
@@ -797,15 +832,12 @@
     return pl.pallas_call(
         partial(unpack_kernel, plan, layers),
         out_shape=(
-            low((layers, 3, DS, DS)),
-            low((layers, DS, DS)),
-            low((layers, DS, WIDER)),
-            low((layers, WIDER, DS)),
+            *[low((3, DS, DS)), low((DS, DS)), low((DS, WIDER)), low((WIDER, DS))] * layers,
             low((length, DS)),
             low((DT, DS)),
         ),
         in_specs=[VMEM_SPEC],
-        out_specs=(VMEM_SPEC,) * 6,
+        out_specs=(VMEM_SPEC,) * (4 * layers + 2),
         scratch_shapes=[
             pltpu.VMEM((4, DS, DS), full),
             pltpu.VMEM((FS, DS), full),
@@ -833,9 +865,10 @@
 
 def student_kernel(
     layers, token_ref, place_ref, evec_ref, vec_ref, bias_ref, mask_ref,
-    qkv_w, out_w, up_w, down_w,
-    emb_ref, zero_ref, zero_inv, last_ref, low_ref, qkv_ref, context_ref, one_ref, one_inv, two_ref, two_inv,
+    *refs,
 ):
+    matrices, refs = refs[: 4 * layers], refs[4 * layers :]
+    emb_ref, zero_ref, zero_inv, last_ref = refs[:4]
     length = mask_ref.shape[1]
     size = DS // HS
 
@@ -849,18 +882,23 @@
         zero_ref[at, :] = normed
         zero_inv[at, :] = inverse
         for layer in range(layers):
-            def vector(index):
+            qkv_w, out_w, up_w, down_w = matrices[4 * layer : 4 * layer + 4]
+            low_ref, qkv_ref, context_ref, one_ref, one_inv, two_ref, two_inv = refs[
+                4 + 7 * layer : 11 + 7 * layer
+            ]
+
+            def vector(index, layer=layer):
                 return vec_ref[layer, index : index + 1, :]
 
             low = hidden.astype(jnp.bfloat16)
-            low_ref[layer, at, :] = low
+            low_ref[at, :] = low
             parts = []
             for part in range(3):
-                made = jnp.dot(low, qkv_w[layer, part], preferred_element_type=jnp.float32)
+                made = jnp.dot(low, qkv_w[part], preferred_element_type=jnp.float32)
                 if part != 1:
                     made = made + vector(part // 2)
                 parts.append(made.astype(jnp.bfloat16))
-                qkv_ref[layer, part, at, :] = parts[part]
+                qkv_ref[part, at, :] = parts[part]
             contexts = []
             for row in range(TILE // length):
                 span = slice(row * length, (row + 1) * length)
@@ -879,20 +917,20 @@
                     jnp.dot(weights, by_heads(v, HS), preferred_element_type=jnp.float32)
                 )
             context = jnp.concatenate(contexts).astype(jnp.bfloat16)
-            context_ref[layer, at, :] = context
-            attended = jnp.dot(context, out_w[layer], preferred_element_type=jnp.float32) + vector(2)
+            context_ref[at, :] = context
+            attended = jnp.dot(context, out_w[...], preferred_element_type=jnp.float32) + vector(2)
             middle, normed, inverse = norm_forward(hidden + attended, vector(3), vector(4))
-            one_ref[layer, at, :] = normed
-            one_inv[layer, at, :] = inverse
+            one_ref[at, :] = normed
+            one_inv[at, :] = inverse
             inner = jnp.dot(
-                middle.astype(jnp.bfloat16), up_w[layer], preferred_element_type=jnp.float32
+                middle.astype(jnp.bfloat16), up_w[...], preferred_element_type=jnp.float32
             ) + bias_ref[layer]
             outer = jnp.dot(
-                gelu(inner).astype(jnp.bfloat16), down_w[layer], preferred_element_type=jnp.float32
+                gelu(inner).astype(jnp.bfloat16), down_w[...], preferred_element_type=jnp.float32
             ) + vector(5)
             hidden, normed, inverse = norm_forward(middle + outer, vector(6), vector(7))
-            two_ref[layer, at, :] = normed
-            two_inv[layer, at, :] = inverse
+            two_ref[at, :] = normed
+            two_inv[at, :] = inverse
         last_ref[at, :] = hidden
         return carry
 
@@ -909,18 +947,21 @@
         full((tokens, DS)),
         full((tokens, 1)),
         full((tokens, DS)),
-        low((layers, tokens, DS)),
-        low((layers, 3, tokens, DS)),
-        low((layers, tokens, DS)),
-        full((layers, tokens, DS)),
-        full((layers, tokens, 1)),
-        full((layers, tokens, DS)),
-        full((layers, tokens, 1)),
+        *[
+            low((tokens, DS)),
+            low((3, tokens, DS)),
+            low((tokens, DS)),
+            full((tokens, DS)),
+            full((tokens, 1)),
+            full((tokens, DS)),
+            full((tokens, 1)),
+        ]
+        * layers,
     )
     return pl.pallas_call(
         partial(student_kernel, layers),
         out_shape=made,
-        in_specs=[VMEM_SPEC] * 10,
+        in_specs=[VMEM_SPEC] * (6 + len(matrices)),
         out_specs=(VMEM_SPEC,) * len(made),
         compiler_params=pltpu.CompilerParams(vmem_limit_bytes=58 * 1024 * 1024),
         cost_estimate=pl.CostEstimate(
@@ -1087,6 +1128,306 @@
     )(*given)
 
 
+def d_all_width(width):
+    return -(-width // 128) * 128
+
+
+def head_kernel(
+    groups, pair, denom, p_ref, t_ref, table_ref, head_ref, d_ref, own_ref, w_ref, *refs
+):
+    inbox_ref, refs = (refs[0], refs[1:]) if pair else (None, refs)
+    (
+        p_all, t_all, p_turned, t_turned, s_logits, t_logits, stats, rows_of, low_grads, tiles, total,
+        send, recv, stat_send, stat_recv, d_send, d_recv, tile_sem, pair_send, pair_recv,
+    ) = refs
+    amount, width = p_ref.shape
+    vocab = table_ref.shape[0]
+    z_size = z_size_of(groups)
+    side = groups // z_size
+    across = z_size * amount
+    half = d_all_width(width)
+    dp, me = lax.axis_index("dp"), lax.axis_index("fsdp")
+    z, y = me // side, me % side
+    sibling = (dp // 2 * 2 + 1 - dp % 2, me)
+    barrier = pltpu.get_barrier_semaphore()
+    for step in range(1, groups):
+        pl.semaphore_signal(
+            barrier, inc=1, device_id=(dp, (me + step) % groups), device_id_type=MESH
+        )
+    if pair:
+        pl.semaphore_signal(barrier, inc=1, device_id=sibling, device_id_type=MESH)
+    pl.semaphore_wait(barrier, groups - 1 + (1 if pair else 0))
+
+    def both(at, rank, target, own=False):
+        return [
+            pltpu.make_async_remote_copy(
+                given if own else held.at[at],
+                held.at[at],
+                send.at[2 * rank + index],
+                recv.at[2 * rank + index],
+                device_id=(dp, target),
+                device_id_type=MESH,
+            )
+            for index, (given, held) in enumerate(((p_ref, p_all), (t_ref, t_all)))
+        ]
+
+    def begin(copies):
+        for copy in copies:
+            copy.start()
+
+    def received(copies):
+        for copy in copies:
+            copy.wait_recv()
+
+    def sent(copies):
+        for copy in copies:
+            copy.wait_send()
+
+    def line(step):
+        return z + step, (z + step >= 0) & (z + step < z_size)
+
+    def inside(position):
+        return jnp.minimum(jnp.maximum(position, 0), z_size - 1) * side
+
+    def z_copies(step, way, arriving):
+        origin, known = line(-way * (step + (1 if arriving else 0)))
+        target, there = line(way)
+        rank = 2 * step + (1 if way > 0 else 0)
+        made = both(inside(origin) + y, rank, inside(target) + y, own=step == 0 and not arriving)
+        return made, known if arriving else known & there
+
+    def y_copies(back, step, at, own=False):
+        return both(
+            at, 2 * z_size + (back - 1) * z_size + step, z * side + (y + back) % side, own
+        )
+
+    wide = next(size for size in (384, 320, 128) if vocab % size == 0)
+
+    def measure(back):
+        at_y = (y + side - back) % side
+        slots = [line * side + at_y for line in range(z_size)]
+        t_turned[...] = jnp.concatenate([t_all[at] for at in slots]).astype(jnp.float32).T.astype(
+            jnp.bfloat16
+        )
+        p_turned[...] = jnp.concatenate([p_all[at] for at in slots]).astype(jnp.float32).T.astype(
+            jnp.bfloat16
+        )
+
+        def step(index, carry):
+            s_top, s_sum, t_top, t_sum, cross = carry
+            lines = pl.ds(pl.multiple_of(index * wide, 64), wide)
+            t_now = jnp.dot(head_ref[lines, :], t_turned[...], preferred_element_type=jnp.float32)
+            s_now = jnp.dot(table_ref[lines, :], p_turned[...], preferred_element_type=jnp.float32)
+            t_logits[back, lines, :] = t_now
+            s_logits[back, lines, :] = s_now
+            s_next = jnp.maximum(s_top, jnp.max(s_now, 0, keepdims=True))
+            t_next = jnp.maximum(t_top, jnp.max(t_now, 0, keepdims=True))
+            t_exp = jnp.exp(t_now - t_next)
+            scale = jnp.exp(t_top - t_next)
+            s_sum = s_sum * jnp.exp(s_top - s_next) + jnp.sum(
+                jnp.exp(s_now - s_next), 0, keepdims=True
+            )
+            t_sum = t_sum * scale + jnp.sum(t_exp, 0, keepdims=True)
+            cross = cross * scale + jnp.sum(t_exp * s_now, 0, keepdims=True)
+            return (s_next, s_sum, t_next, t_sum, cross)
+
+        lowest = jnp.full((1, across), -jnp.inf, jnp.float32)
+        zero = jnp.zeros((1, across), jnp.float32)
+        made = lax.fori_loop(0, vocab // wide, step, (lowest, zero, lowest, zero, zero))
+        for index, value in enumerate(made):
+            stats[me, at_y, index : index + 1, :] = value
+
+    p_all[me] = p_ref[...]
+    t_all[me] = t_ref[...]
+    for way in (1, -1):
+        made, wanted = z_copies(0, way, False)
+        pl.when(wanted)(partial(begin, made))
+    for back in range(1, side):
+        begin(y_copies(back, z, me, own=True))
+    for step in range(z_size - 1):
+        for way in (1, -1):
+            made, wanted = z_copies(step, way, True)
+            onward, further = z_copies(step + 1, way, False) if step + 2 < z_size else (None, None)
+
+            @pl.when(wanted)
+            def _(made=made, onward=onward, further=further, step=step, way=way):
+                received(made)
+                if onward is not None:
+                    pl.when(further)(partial(begin, onward))
+                origin = z - way * (step + 1)
+                for back in range(1, side):
+                    begin(y_copies(back, origin, origin * side + y))
+
+    for back in range(side):
+        if back:
+            for step in range(z_size):
+                received(y_copies(back, step, step * side + (y + side - back) % side))
+        measure(back)
+    for step in range(z_size - 1):
+        for way in (1, -1):
+            made, wanted = z_copies(step, way, False)
+            pl.when(wanted)(partial(sent, made))
+    for back in range(1, side):
+        for step in range(z_size):
+            sent(y_copies(back, step, step * side + y))
+
+    def stat_copy(step):
+        return pltpu.make_async_remote_copy(
+            stats.at[me],
+            stats.at[me],
+            stat_send.at[step],
+            stat_recv.at[step],
+            device_id=(dp, (me + step) % groups),
+            device_id_type=MESH,
+        )
+
+    for step in range(1, groups):
+        stat_copy(step).start()
+    for step in range(1, groups):
+        stat_copy(step).wait_recv()
+    for back in range(side):
+        at_y = (y + side - back) % side
+        parts = [stats[other, at_y] for other in range(groups)]
+        s_top, t_top = parts[0][0:1], parts[0][2:3]
+        for part in parts[1:]:
+            s_top = jnp.maximum(s_top, part[0:1])
+            t_top = jnp.maximum(t_top, part[2:3])
+        s_sum, t_sum, cross = (jnp.zeros_like(s_top) for unused in range(3))
+        for part in parts:
+            s_sum = s_sum + part[1:2] * jnp.exp(part[0:1] - s_top)
+            scale = jnp.exp(part[2:3] - t_top)
+            t_sum = t_sum + part[3:4] * scale
+            cross = cross + part[4:5] * scale
+        rows_of[back, 0:1, :] = s_top + jnp.log(s_sum)
+        rows_of[back, 1:2, :] = t_top
+        rows_of[back, 2:3, :] = 1.0 / t_sum
+        rows_of[back, 3:4, :] = cross / t_sum
+        total[back] = jnp.zeros((half, across), jnp.float32)
+    own_ref[...] = rows_of[0]
+    narrow = next(size for size in (384, 320, 128) if vocab % size == 0)
+    outs = []
+    for index in range(vocab // narrow):
+        lines = slice(index * narrow, (index + 1) * narrow)
+        table = table_ref[lines, :]
+
+        def differ(back, carry, lines=lines, table=table):
+            row = rows_of[back]
+            made = 2.0 * jnp.exp(s_logits[back, lines, :] - row[0:1])
+            made = made - jnp.exp(t_logits[back, lines, :] - row[1:2]) * row[2:3]
+            low = (made * (1.0 / denom)).astype(jnp.bfloat16)
+            low_grads[back] = low
+            total[back, :width, :] += outer_product(table, low)
+            return carry
+
+        lax.fori_loop(0, side, differ, 0)
+        if index >= 2:
+            outs[index - 2].wait()
+        made = jnp.zeros((narrow, width), jnp.float32)
+        for back in range(side):
+            at_y = (y + side - back) % side
+            states = jnp.concatenate([p_all[line * side + at_y] for line in range(z_size)])
+            made = made + jnp.dot(low_grads[back], states, preferred_element_type=jnp.float32)
+        tiles[index % 2] = made
+        outs.append(
+            pltpu.make_async_copy(tiles.at[index % 2], w_ref.at[lines, :], tile_sem.at[index % 2])
+        )
+        outs[-1].start()
+    for back in range(side):
+        turned = total[back].T.astype(jnp.bfloat16)
+        for line in range(z_size):
+            at = line * side + (y + side - back) % side
+            t_all[at, :, half : 2 * half] = turned[line * amount : (line + 1) * amount]
+
+    def d_copy(step):
+        peer = (me + step) % groups
+        return pltpu.make_async_remote_copy(
+            t_all.at[peer, :, half : 2 * half],
+            t_all.at[me, :, 0:half],
+            d_send.at[step],
+            d_recv.at[step],
+            device_id=(dp, peer),
+            device_id_type=MESH,
+        )
+
+    for step in range(1, groups):
+        d_copy(step).start()
+    for out in outs[-2:]:
+        out.wait()
+    given = []
+    if pair:
+        part = vocab // 4
+        for index in range(2):
+            start = pl.multiple_of((2 * index + 1 - dp % 2) * part, 8)
+            given.append(
+                pltpu.make_async_remote_copy(
+                    w_ref.at[pl.ds(start, part), :],
+                    inbox_ref.at[index],
+                    pair_send.at[index],
+                    pair_recv.at[index],
+                    device_id=sibling,
+                    device_id_type=MESH,
+                )
+            )
+            given[-1].start()
+    made = t_all[me, :, half : 2 * half].astype(jnp.float32)
+    for step in range(1, groups):
+        d_copy(step).wait_recv()
+        made = made + t_all[(me + groups - step) % groups, :, 0:half].astype(jnp.float32)
+    d_ref[...] = made
+    for step in range(1, groups):
+        stat_copy(step).wait_send()
+        d_copy(step).wait_send()
+    for copy in given:
+        copy.wait()
+
+
+def head(picked, t_picked, table, teacher_head, denom, number):
+    groups, n_dp = lax.axis_size("fsdp"), lax.axis_size("dp")
+    pair = n_dp == 4
+    amount, width = picked.shape
+    vocab = table.shape[0]
+    z_size = z_size_of(groups)
+    side, across = groups // z_size, z_size * amount
+    half = d_all_width(width)
+    assert 2 * half <= DT
+    narrow = next(size for size in (384, 320, 128) if vocab % size == 0)
+    full, low = jnp.float32, jnp.bfloat16
+    anywhere = pl.BlockSpec(memory_space=pl.ANY)
+    dma = pltpu.SemaphoreType.DMA
+    made = [
+        jax.ShapeDtypeStruct((amount, half), full),
+        jax.ShapeDtypeStruct((8, across), full),
+        jax.ShapeDtypeStruct((vocab, width), full),
+    ]
+    if pair:
+        made.append(jax.ShapeDtypeStruct((2, vocab // 4, width), full))
+    return pl.pallas_call(
+        partial(head_kernel, groups, pair, denom),
+        out_shape=tuple(made),
+        in_specs=[VMEM_SPEC] * 4,
+        out_specs=(VMEM_SPEC, VMEM_SPEC) + (anywhere,) * (len(made) - 2),
+        scratch_shapes=[
+            pltpu.VMEM((groups, amount, width), low),
+            pltpu.VMEM((groups, amount, DT), low),
+            pltpu.VMEM((width, across), low),
+            pltpu.VMEM((DT, across), low),
+            pltpu.VMEM((side, vocab, across), full),
+            pltpu.VMEM((side, vocab, across), full),
+            pltpu.VMEM((groups, side, 8, across), full),
+            pltpu.VMEM((side, 8, across), full),
+            pltpu.VMEM((side, narrow, across), low),
+            pltpu.VMEM((2, narrow, width), full),
+            pltpu.VMEM((side, half, across), full),
+            *[dma((2 * (2 * z_size + (side - 1) * z_size),))] * 2,
+            *[dma((groups,))] * 4,
+            *[dma((2,))] * 3,
+        ],
+        compiler_params=pltpu.CompilerParams(
+            collective_id=number, has_side_effects=True, vmem_limit_bytes=60 * 1024 * 1024
+        ),
+    )(picked, t_picked, table, teacher_head)
+
+
 def three_parts(value):
     high = lax.reduce_precision(value, 8, 7)
     rest = value - high
@@ -1202,12 +1543,17 @@
     flat_local = layer_flat.shape[1]
     by_rows = flat_local % DS == 0
 
+    to_owner = [
+        (d * groups + f, f * n_dp + d) for d in range(n_dp) for f in range(groups)
+    ]
+    from_owner = [(owner, holder) for holder, owner in to_owner]
+    table_low = emb_table.astype(jnp.bfloat16)
+
     usable = valid_mask.reshape(rows, length) > 0
     docs = seq_ids.reshape(rows, length)
     same_doc = docs[:, :, None] == docs[:, None, :]
     pair_mask = same_doc & usable[:, :, None] & usable[:, None, :]
     allowed = pair_mask | jnp.eye(length, dtype=bool)
-    table_low = emb_table.astype(jnp.bfloat16)
     ids = jnp.concatenate([token_ids.reshape(-1), mask_labels.reshape(-1)])
     plan = plan_requests(ids, local_rows)
     extra = jnp.stack([-1 - jnp.sum(pair_mask.astype(jnp.int32)), -1 - jnp.max(plan[3])])
@@ -1229,6 +1575,8 @@
     block_rows = -(-lines // 16) * 16
     marks, asked = question(plan, 0, devices, extra)
     got, weights_all, token_blocks = entry(asked, pack(own_parts, line, block_rows)[0], table_low, 3)
+    table_then = lax.optimization_barrier((table_low, got))[0]
+    slice_part = lax.ppermute(table_then, BOTH, from_owner)
     wanted = got[:, 0, :SLOTS].reshape(-1)
     notes = got[:, 0, SLOTS : SLOTS + 2]
     count = jnp.sum(-1 - notes[:, 0]).astype(jnp.float32)
@@ -1260,18 +1608,13 @@
                     jnp.pad(down, ((0, WIDER - FS), (0, 0))),
                 )
             )
-        matrices = [jnp.stack(group) for group in zip(*split)]
+        matrices = sum(map(list, split), [])
         start = layers * flat_local
         places_all = flat_all[:, start : start + pos_local * DS].reshape(length, DS)
         start += pos_local * DS
         proj_all = flat_all[:, start : start + proj_local * DS].reshape(DT, DS)
 
-    to_owner = [
-        (d * groups + f, f * n_dp + d) for d in range(n_dp) for f in range(groups)
-    ]
-    from_owner = [(owner, holder) for holder, owner in to_owner]
-    table_then = lax.optimization_barrier((table_low, teacher_all))[0]
-    slice_part = lax.ppermute(table_then, BOTH, from_owner)
+    slice_part = lax.optimization_barrier((slice_part, teacher_all))[0]
     slice_table = lax.all_gather(slice_part, "dp", axis=0, tiled=True)
 
     proj_bias = misc_vec[2 * DS :]
@@ -1306,81 +1649,42 @@
     pick_marks = (flat_pick[:, None] == lax.broadcasted_iota(jnp.int32, (1, tokens), 1)).astype(
         jnp.bfloat16
     )
-    both_low = jnp.concatenate([hidden.astype(jnp.bfloat16), t_out.astype(jnp.bfloat16)], 1)
-    both_picked = jnp.dot(pick_marks, both_low, preferred_element_type=jnp.float32).astype(
-        jnp.bfloat16
-    )
-    picked = both_picked[:, :width]
-    both_all = exchange(both_picked, 4, whole=False, spread=True).reshape(-1, width + DT)
-    picked_all, t_picked_all = both_all[:, :width], both_all[:, width:]
-    s_logits = jnp.einsum("gd,vd->gv", picked_all, slice_table, preferred_element_type=jnp.float32)
-    t_logits = jnp.einsum(
-        "gd,vd->gv", t_picked_all, teacher_head, preferred_element_type=jnp.float32
-    )
-    s_top = jnp.max(s_logits, -1)
-    t_top = jnp.max(t_logits, -1)
-    t_exp = jnp.exp(t_logits - t_top[:, None])
-    local_stats = jnp.stack(
-        [
-            s_top,
-            jnp.sum(jnp.exp(s_logits - s_top[:, None]), -1),
-            t_top,
-            jnp.sum(t_exp, -1),
-            jnp.sum(t_exp * s_logits, -1),
-        ]
-    )
-    stats_all = exchange(local_stats, 5, whole=False, spread=True)
-    stats = tuple(stats_all[0])
-    for other in range(1, groups):
-        stats = combine_stats(stats, tuple(stats_all[other]))
-    s_top, s_sum, t_top, t_sum, cross = stats
-    log_total = s_top + jnp.log(s_sum)
-    d_logits = (
-        2.0 * jnp.exp(s_logits - log_total[:, None])
-        - jnp.exp(t_logits - t_top[:, None]) / t_sum[:, None]
-    ) / predict_denom
-    d_logits = d_logits.astype(jnp.bfloat16)
-    grad_slice = outer_product(d_logits, picked_all)
-    d_logits, grad_slice = lax.optimization_barrier((d_logits, grad_slice))
-    if n_dp == 4:
-        to_send = [sum_cores, sum_along_x, lambda part: lax.ppermute(part, BOTH, to_owner)]
-    else:
-        to_send = [
-            lambda value: lax.psum_scatter(value, "dp", scatter_dimension=0, tiled=True),
-            lambda part: lax.ppermute(part, BOTH, to_owner),
-        ]
-    d_logits, head_grad = lax.optimization_barrier((d_logits, to_send.pop(0)(grad_slice)))
-    if len(to_send) > 1:
-        head_grad = to_send.pop(0)(head_grad)
-    d_picked_all = jnp.dot(d_logits, slice_table, preferred_element_type=jnp.float32)
-    d_picked = jnp.sum(
-        exchange(
-            d_picked_all.astype(jnp.bfloat16).reshape(groups, rows * picks, width), 6, whole=False
-        ).astype(jnp.float32),
-        0,
-    )
+    picked = jnp.dot(
+        pick_marks, hidden.astype(jnp.bfloat16), preferred_element_type=jnp.float32
+    ).astype(jnp.bfloat16)
+    t_picked = jnp.dot(
+        pick_marks, t_out.astype(jnp.bfloat16), preferred_element_type=jnp.float32
+    ).astype(jnp.bfloat16)
+    d_picked, own_stats, head_grad, *inbox = head(
+        picked, t_picked, slice_table, teacher_head, predict_denom, 4
+    )
+    own_z = place // (groups // z_size_of(groups))
+    own_stats = lax.dynamic_slice_in_dim(own_stats, own_z * rows * picks, rows * picks, 1)
     picked_wide = picked.astype(jnp.float32)
     target_logit = jnp.sum(picked_wide * label_rows, -1)
-    own_start = place * rows * picks
-    own_total = lax.dynamic_slice_in_dim(log_total, own_start, rows * picks, 0)
-    own_cross = lax.dynamic_slice_in_dim(cross / t_sum, own_start, rows * picks, 0)
-    predict_sum = jnp.sum(2.0 * own_total - own_cross - target_logit) / predict_denom
-    d_picked = d_picked - label_rows / predict_denom
+    predict_sum = (
+        jnp.sum(2.0 * own_stats[0] - own_stats[3] - target_logit) / predict_denom
+    )
+    d_picked = d_picked[:, :width] - label_rows / predict_denom
     d_hidden = pick_exact(pick_marks, d_picked, True) + back_last
+
+    if inbox:
+        head_grad = sum_along_x(own_parts_of(head_grad) + inbox[0])
+    else:
+        head_grad = lax.psum_scatter(head_grad, "dp", scatter_dimension=0, tiled=True)
 
     matrix_grads = [None] * layers
     vector_grads = [None] * layers
     attention_sum = jnp.float32(0.0)
-    d_hidden, head_grad = lax.optimization_barrier((d_hidden, head_grad))
-    head_grad = to_send.pop(0)(head_grad)
+    head_grad = lax.ppermute(head_grad, BOTH, to_owner)
     for layer_index in reversed(range(layers)):
         d_hidden, *others = student_backward(
             d_hidden,
             vectors[layer_index],
             biases[layer_index],
             mask,
-            [matrix[layer_index] for matrix in matrices],
-            [kept[layer_index] for kept in saved],
+            matrices[4 * layer_index : 4 * layer_index + 4],
+            saved[7 * layer_index : 7 * layer_index + 7],
             [t_scores, count.reshape(1, 1)] if layer_index == layers - 1 else [],
         )
         matrix_grads[layer_index] = others[:6]

time: 805 us -> 678 us (0.84)
  local copies, waits for them, and re-layouts: 105 us -> 55.2 us
  Pallas kernels: 491 us -> 457 us
  other arithmetic: 90.6 us -> 56.9 us
  matrix products: 62.2 us -> 37.9 us
  waiting for transfers between devices: 0.06 us -> 10.8 us
    pallas_call x4 -> x1, Pallas kernels: 139 us -> 9.88 us  [exchange(): pl.pallas_call(partial(exchange_kernel, count, whole, spread), out_shape=...]
    pallas_call x1 -> x2, Pallas kernels: 8 us -> 107 us  [the longest x1 98.9 us: head(): pl.pallas_call(partial(head_kernel, groups, pair, denom), out_shape=tuple...]
    dot_general x4 -> x2, matrix products: 28.3 us -> 5.85 us  [the longest x1 3.22 us: local(): jnp.dot(pick_marks, t_out.astype(jnp.bfloat16), preferred_element_type=jn...]
    squeeze x11 -> x0, local copies, waits for them, and re-layouts: 19.8 us -> none  [the longest x7 14.9 us: local(): kept[layer_index]]
    reduce_sum x3 -> x1, other arithmetic: 19.9 us -> 0.6 us  [local(): jnp.sum(2.0 * own_stats[0] - own_stats[3] - target_logit) / predict_denom]
    convert_element_type x3 -> x0, other arithmetic: 17.8 us -> none  [the longest x1 15.7 us: local(): d_logits = d_logits.astype(jnp.bfloat16)]
    unnamed x169 -> x132, local copies, waits for them, and re-layouts: 24 us -> 10.4 us
    pallas_call x1, Pallas kernels: 50.6 us -> 38.9 us  [student_forward(): pl.pallas_call(partial(student_kernel, layers), out_shape=made, in_specs=...]
  transfers between devices with their start and end apart: 6 -> 5, of which waited for: 0 -> 1; matrix products, arithmetic and copies ran while one was open for 13% -> 10% of each run, Pallas kernels for 43% -> 34%
where the time goes in v2:
time: 678 us; the launch traced here: 668 us
  Pallas kernels  457 us (67%)
  other arithmetic  56.9 us (8%)
  local copies, waits for them, and re-layouts  55.2 us (8%)
  matrix products  37.9 us (6%)
  between operations  28.4 us (4%)
  starting transfers between devices  21.2 us (3%)
  waiting for transfers between devices  10.8 us (2%)
    pallas_call x1, Pallas kernels, reduce(): pl.pallas_call(partial(reduce_kernel, plan, len(parts)), out_shape=(jax.S...  118 us
    pallas_call x1, Pallas kernels, head(): pl.pallas_call(partial(head_kernel, groups, pair, denom), out_shape=tuple...  98.9 us
    pallas_call x1, Pallas kernels, entry(): pl.pallas_call(entry_kernel, out_shape=(jax.ShapeDtypeStruct(asked.shape,...  75 us
    pallas_call x2, Pallas kernels, student_backward(): pl.pallas_call(partial(back_kernel, bool(last)), out_shape=tuple(made), i...  74.6 us
    pallas_call x1, Pallas kernels, student_forward(): pl.pallas_call(partial(student_kernel, layers), out_shape=made, in_specs=...  38.9 us
    pallas_call x1, Pallas kernels, teacher_forward(): pl.pallas_call(teacher_kernel, out_shape=(jax.ShapeDtypeStruct((tokens, D...  33.7 us
  transfers between devices with their start and end apart: 5, of which 1 were waited for; matrix products, arithmetic and copies ran while one was open for 10% of the time, Pallas kernels for 34%

profile of v2, /device:TPU:0, one launch (start us, length us, event | category | flops | bytes accessed | tf_op | source)
XLA Modules:
  0.0 667.6 jit_solution(14440827006977046784)
XLA Ops:
  23.5 75.0 %shard_map.418 = (s32[32,1,128]{2,1,0:T(1,128)S(1)}, bf16[32,256,312]{2,1,0:T(8,128)(2,1)S(1)}, bf16[32,48,312]{2,1,0:T(8,128)(2,1)S(1)}) custom-call(s32[32,1,128]{2,1,0:T(1,128)S(1)} %add_add_fusion.2.ask_ref, bf16[256,312]{1,0:T(8,128)(2,1)S(1)} %maximum_bitcast_fusion.w_ref, bf16[960,312]{1,0:T(8,128)(2,1)S(1)} %copy.181.table_ref), custom_call_target="tpu_custom_call" | custom-call | tf_op jit(solution)/shard_map/pallas_call | solution.py:295
  98.4 3.9 copy-done
  103.4 6.7 %collective-permute-start = (bf16[960,312]{0,1:T(8,128)(2,1)}, bf16[960,312]{0,1:T(8,128)(2,1)}, u32[]{:S(2)}, u32[]{:S(2)}) collective-permute-start(bf16[960,312]{0,1:T(8,128)(2,1)} %copy.185), channel_id=1, source_target_pairs={{0,0},{4,1},{8,2},{12,3},{16,4},{20,5},{24,6},{28,7},{1,8},{5,9},{... | collective-permute-start | bytes 1797128 | tf_op jit(solution)/shard_map/ppermute | solution.py:1579
  115.2 3.0 fusion.21
  122.1 7.7 %shard_map.419 = (bf16[3,312,312]{2,1,0:T(8,128)(2,1)S(1)}, bf16[312,312]{1,0:T(8,128)(2,1)S(1)}, bf16[312,1280]{1,0:T(8,128)(2,1)S(1)}, bf16[1280,312]{1,0:T(8,...) custom-call(bf16[32,256,312]{2,1,0:T(8,128)(2,1)} %copy-done), custom_call_target="tpu_custom_call" | custom-call | bytes 20000000 | tf_op jit(solution)/shard_map/pallas_call | solution.py:832
  135.7 38.9 %shard_map.420 = (f32[1024,312]{1,0:T(8,128)}, f32[1024,312]{1,0:T(8,128)}, f32[1024,1]{1,0:T(8,128)}, f32[1024,312]{1,0:T(8,128)}, bf16[1024,312]{1,0:T(8,128)(...) custom-call(f32[1024,312]{1,0:T(8,128)} %slice.306.token_ref, ...), custom_call_target="tpu_custom_call" | custom-call | flops 8000000000 | bytes 40000000 | tf_op jit(solution)/shard_map/pallas_call | solution.py:961
  186.1 33.7 %shard_map.421 = (f32[1024,768]{1,0:T(8,128)}, f32[1024,1536]{1,0:T(8,128)}) custom-call(bf16[1024,768]{1,0:T(8,128)(2,1)} %bitcast.182, bf16[96,96,768]{2,1,0:T(8,128)(2,1)} %bitcast.181, f32[1,9984]{1,0:T(1,128)} %reshape.623.vec_ref, f32[1024,128]{1,0:T(8,128)} %select_select_fusion.mask_ref), custom_call_target="tpu_custom_call" | custom-call | flops 20000000000 | bytes 25000000 | tf_op jit(solution)/shard_map/pallas_call | solution.py:750
  219.8 3.2 fusion.44.t_ref
  223.0 6.7 fusion.28
  229.7 4.7 copy.186
  234.4 98.9 %shard_map.422 = (f32[160,384]{1,0:T(8,128)}, f32[8,640]{1,0:T(8,128)}, f32[3840,312]{1,0:T(8,128)}, f32[2,960,312]{2,1,0:T(8,128)}) custom-call(bf16[160,312]{1,0:T(8,128)(2,1)} %get-tuple-element.461.p_ref, bf16[160,768]{1,0:T(8,128)(2,1)} %fusion.44.t_ref, bf16[3840,312]{1,0:T(8,128)(2,1)} %bitcast.152, bf16[3840,768]{1,0:T(8,128)(2,1)} %head_ref.1), custom_call_target="tpu_custom_call" | custom-call | tf_op jit(solution)/shard_map/pallas_call | solution.py:1404
  333.4 4.0 fusion.37
  341.5 3.2 collective-permute-start.1
  354.5 3.6 fusion.90
  360.3 10.7 %collective-permute-done.1 = f32[960,312]{0,1:T(8,128)} collective-permute-done((f32[960,312]{0,1:T(8,128)}, f32[960,312]{0,1:T(8,128)}, u32[]{:S(2)}, u32[]{:S(2)}) %collective-permute-start.1) | collective-permute-done | bytes 1198112 | tf_op jit(solution)/shard_map/ppermute | solution.py:637
  379.7 11.2 %collective-permute-start.2 = (f32[960,312]{0,1:T(8,128)}, f32[960,312]{0,1:T(8,128)}, u32[]{:S(2)}, u32[]{:S(2)}) collective-permute-start(f32[960,312]{0,1:T(8,128)} %copy.197), channel_id=1, source_target_pairs={{0,0},{1,4},{2,8},{3,12},{4,16},{5,20},{6,24},{7,28},{8,1},{9,5},{... | collective-permute-start | bytes 3594248 | tf_op jit(solution)/shard_map/ppermute | solution.py:1679
  394.6 38.7 %shard_map.423 = (f32[1024,312]{1,0:T(8,128)}, f32[312,312]{1,0:T(8,128)}, f32[312,312]{1,0:T(8,128)}, f32[312,312]{1,0:T(8,128)}, f32[312,312]{1,0:T(8,128)}, /...) custom-call(f32[1024,312]{1,0:T(8,128)} %fusion.40.grad_ref, ...), custom_call_target="tpu_custom_call" | custom-call | flops 1000000000 | bytes 4000000 | tf_op jit(solution)/shard_map/pallas_call | solution.py:1113
  435.2 35.9 %shard_map.424 = (f32[1024,312]{1,0:T(8,128)}, f32[312,312]{1,0:T(8,128)}, f32[312,312]{1,0:T(8,128)}, f32[312,312]{1,0:T(8,128)}, f32[312,312]{1,0:T(8,128)}, /...) custom-call(f32[1024,312]{1,0:T(8,128)} %get-tuple-element.271.grad_ref, ...), custom_call_target="tpu_custom_call" | custom-call | flops 1000000000 | bytes 4000000 | tf_op jit(solution)/shard_map/pallas_call | solution.py:1113
  475.8 3.0 multiply_reduce_fusion
  484.1 4.3 fusion.20
  491.1 118.1 %shard_map.425 = (f32[264,312]{1,0:T(8,128)}, f32[32,48,312]{2,1,0:T(8,128)}) custom-call(f32[312,312]{1,0:T(8,128)} %get-tuple-element.279.refs_0_, f32[312,312]{1,0:T(8,128)} %get-tuple-element.280.refs_1_, f32[312,312]{1,0:T(8,128)} %get-tuple-element.281.refs_2_, f32[312,312]{1,0:T(8,128)} %get-tuple-element.282.refs_3_, ...), custom_call_target="tpu_custom_call" | custom-call | tf_op jit(solution)/shard_map/pallas_call | solution.py:488
  620.9 4.2 fusion.23
  633.2 9.9 %shard_map.426 = f32[32,1,384]{2,1,0:T(1,128)} custom-call(f32[1,384]{1,0:T(1,128)} %reshape.621.x_ref), custom_call_target="tpu_custom_call" | custom-call | tf_op jit(solution)/shard_map/pallas_call | solution.py:96
  654.2 3.9 multiply_subtract_fusion
  (285 shorter events, 106.2 us)
Async XLA Ops:
  7.2 167.4 %all-gather.4.cloned.1.call-start = ((), (), s32[]{:S(2)}) async-start(), calls=%async_computation | async-start | bytes 14598144 | tf_op jit(solution)/shard_map/all_gather | solution.py:1561
  9.5 220.2 %all-gather.6.cloned.1.call-start = ((), (), s32[]{:S(2)}) async-start(), calls=%async_computation.1 | async-start | bytes 3194880 | tf_op jit(solution)/shard_map/all_gather | solution.py:1618
  18.1 97.1 %copy-start.58 = (s32[1184]{0:T(1024)}, s32[1184]{0:T(1024)S(1)}, u32[]{:S(2)}) copy-start(s32[1184]{0:T(1024)S(1)} %get-tuple-element.456) | copy-start | bytes 14212
  23.3 86.9 %copy-start.32 = (f32[2,3696]{1,0:T(2,128)S(1)}, f32[2,3696]{1,0:T(2,128)}, u32[]{:S(2)}) copy-start(f32[2,3696]{1,0:T(2,128)} %param.52) | copy-start | bytes 88708
  23.4 89.7 %slice-start = ((f32[1392]{0:T(1024)}), f32[624]{0:T(1024)S(1)}, s32[]{:S(2)}) async-start(f32[1392]{0:T(1024)} %param.55), calls=%async_computation.2 | async-start | bytes 8192 | tf_op jit(solution)/shard_map/slice | solution.py:1621
  103.4 71.1 %collective-permute-start = (bf16[960,312]{0,1:T(8,128)(2,1)}, bf16[960,312]{0,1:T(8,128)(2,1)}, u32[]{:S(2)}, u32[]{:S(2)}) collective-permute-start(bf16[960,312]{0,1:T(8,128)(2,1)} %copy.185), channel_id=1, source_target_pairs={{0,0},{4,1},{8,2},{12,3},{16,4},{20,5},{24,6},{28,7},{1,8},{5,9},{... | collective-permute-start | bytes 1797128 | tf_op jit(solution)/shard_map/ppermute | solution.py:1579
  135.7 39.0 %copy-start.36 = (f32[1392]{0:T(1024)S(1)}, f32[1392]{0:T(1024)}, u32[]{:S(2)}) copy-start(f32[1392]{0:T(1024)} %param.55) | copy-start | bytes 16708
  135.7 39.6 %copy-start.63 = (s32[2,4,20]{2,1,0:T(4,128)S(1)}, s32[2,4,20]{2,1,0:T(4,128)}, u32[]{:S(2)}) copy-start(s32[2,4,20]{2,1,0:T(4,128)} %param.34) | copy-start | bytes 1924
  135.7 41.4 %copy-start.43 = (bf16[9984]{0:T(1024)(128)(2,1)S(1)}, bf16[9984]{0:T(1024)(128)(2,1)}, u32[]{:S(2)}) copy-start(bf16[9984]{0:T(1024)(128)(2,1)} %param.38) | copy-start | bytes 59908
  179.0 40.8 %copy-start.47 = (s32[160]{0:T(256)}, s32[160]{0:T(256)S(1)}, u32[]{:S(2)}) copy-start(s32[160]{0:T(256)S(1)} %add.281) | copy-start | bytes 1924
  341.5 29.6 %collective-permute-start.1 = (f32[960,312]{0,1:T(8,128)}, f32[960,312]{0,1:T(8,128)}, u32[]{:S(2)}, u32[]{:S(2)}) collective-permute-start(f32[960,312]{0,1:T(8,128)} %copy.195), channel_id=1, source_target_pairs={{0,16},{16,0},{8,24},{24,8},{1,17},{17,1},{9,25},{25,9},{2,18},{18... | collective-permute-start | bytes 3594248 | tf_op jit(solution)/shard_map/ppermute | solution.py:637
  379.7 96.1 %collective-permute-start.2 = (f32[960,312]{0,1:T(8,128)}, f32[960,312]{0,1:T(8,128)}, u32[]{:S(2)}, u32[]{:S(2)}) collective-permute-start(f32[960,312]{0,1:T(8,128)} %copy.197), channel_id=1, source_target_pairs={{0,0},{1,4},{2,8},{3,12},{4,16},{5,20},{6,24},{7,28},{8,1},{9,5},{... | collective-permute-start | bytes 3594248 | tf_op jit(solution)/shard_map/ppermute | solution.py:1679
  435.2 36.8 %copy-start.40 = (f32[8,312]{1,0:T(8,128)S(1)}, f32[8,312]{1,0:T(8,128)}, u32[]{:S(2)}) copy-start(f32[8,312]{1,0:T(8,128)} %get-tuple-element.300) | copy-start | bytes 29956
  435.2 38.6 %copy-start.61 = (f32[160]{0:T(256)S(1)}, f32[160]{0:T(256)}, u32[]{:S(2)}) copy-start(f32[160]{0:T(256)} %get-tuple-element.442) | copy-start | bytes 1924
  435.2 40.5 %copy-start.60 = (f32[1,1280]{1,0:T(1,128)S(1)}, f32[1,1280]{1,0:T(1,128)}, u32[]{:S(2)}) copy-start(f32[1,1280]{1,0:T(1,128)} %get-tuple-element.301) | copy-start | bytes 15364
  435.2 40.6 %copy-start.8 = (f32[1024,312]{1,0:T(8,128)S(1)}, f32[1024,312]{1,0:T(8,128)}, u32[]{:S(2)}) copy-start(f32[1024,312]{1,0:T(8,128)} %get-tuple-element.297) | copy-start | bytes 3833860
  435.2 40.6 %copy-start.21 = (f32[1024,312]{1,0:T(8,128)S(1)}, f32[1024,312]{1,0:T(8,128)}, u32[]{:S(2)}) copy-start(f32[1024,312]{1,0:T(8,128)} %fusion.90) | copy-start | bytes 3833860
  435.2 40.6 %copy-start.44 = (f32[312]{0:T(512)S(1)}, f32[312]{0:T(512)}, u32[]{:S(2)}) copy-start(f32[312]{0:T(512)} %slice.262) | copy-start | bytes 3748
  626.8 19.3 %copy-start.42 = (f32[4,312]{1,0:T(4,128)S(1)}, f32[4,312]{1,0:T(4,128)}, u32[]{:S(2)}) copy-start(f32[4,312]{1,0:T(4,128)} %param.43) | copy-start | bytes 14980
  626.8 22.3 %copy-start.37 = (f32[1392]{0:T(1024)S(1)}, f32[1392]{0:T(1024)}, u32[]{:S(2)}) copy-start(f32[1392]{0:T(1024)} %param.55) | copy-start | bytes 16708
  626.8 23.7 %copy-start.23 = (f32[2,35568]{1,0:T(2,128)S(1)}, f32[2,35568]{1,0:T(2,128)}, u32[]{:S(2)}) copy-start(f32[2,35568]{1,0:T(2,128)} %param.46) | copy-start | bytes 853636
  626.8 23.7 %copy-start.29 = (f32[2,35568]{1,0:T(2,128)S(1)}, f32[2,35568]{1,0:T(2,128)}, u32[]{:S(2)}) copy-start(f32[2,35568]{1,0:T(2,128)} %param.48) | copy-start | bytes 853636
  629.2 24.3 %copy-start.33 = (f32[2,3696]{1,0:T(2,128)S(1)}, f32[2,3696]{1,0:T(2,128)}, u32[]{:S(2)}) copy-start(f32[2,3696]{1,0:T(2,128)} %param.52) | copy-start | bytes 88708
  629.2 25.0 %copy-start.13 = (f32[960,312]{0,1:T(8,128)S(1)}, f32[960,312]{0,1:T(8,128)}, u32[]{:S(2)}) copy-start(f32[960,312]{0,1:T(8,128)} %param.40) | copy-start | bytes 3594244
  (47 other events, 214.0 us)
Sparse Core Ops, SparseCore 0:
  11.0 159.3 all-gather.3
  174.8 24.6 all-gather.5

commit v3 on v2

--- a/solution.py
+++ b/solution.py
@@ -107,6 +107,9 @@
     )(x)
 
 
+VMEM_SPEC = pl.BlockSpec(memory_space=pltpu.VMEM)
+
+
 class Grid:
     def __init__(self):
         self.fsdp = lax.axis_size("fsdp")
@@ -300,7 +303,7 @@
             jax.ShapeDtypeStruct((count, SLOTS, width), table_low.dtype),
         ),
         in_specs=[anywhere, anywhere, pl.BlockSpec(memory_space=pltpu.VMEM)],
-        out_specs=(anywhere, anywhere, anywhere),
+        out_specs=(anywhere, VMEM_SPEC, VMEM_SPEC),
         scratch_shapes=[
             pltpu.VMEM((count, SLOTS, width), table_low.dtype),
             pltpu.VMEM(asked.shape, asked.dtype),
@@ -583,16 +586,6 @@
     return (normed * gain + bias, normed, inverse)
 
 
-def norm_backward(grad, normed, inverse, gain):
-    d_normed = grad * gain
-    d_value = inverse * (
-        d_normed
-        - jnp.mean(d_normed, -1, keepdims=True)
-        - normed * jnp.mean(d_normed * normed, -1, keepdims=True)
-    )
-    return (d_value, jnp.sum(grad * normed, 0), jnp.sum(grad, 0))
-
-
 def cut_pieces(vector, sizes):
     pieces = []
     start = 0
@@ -610,31 +603,6 @@
         wide[second:third].reshape(width, hidden),
         wide[third:],
     )
-
-
-def hidden_term(source, target, proj_turned, proj_bias, weight, denom):
-    source_low = source.astype(jnp.bfloat16)
-    mapped = back_product(source_low, proj_turned) + proj_bias
-    spread = mapped - target
-    d_mapped = (2.0 * weight * spread / denom).astype(jnp.bfloat16)
-    return (
-        jnp.sum(weight * spread * spread) / denom,
-        outer_product(d_mapped, source_low),
-        jnp.sum(d_mapped.astype(jnp.float32), 0),
-        jnp.dot(d_mapped, proj_turned, preferred_element_type=jnp.float32),
-    )
-
-
-def own_parts_of(value):
-    parts = value.reshape(2, 2, -1, value.shape[1])
-    return jnp.where(lax.axis_index("dp") % 2 == 0, parts[:, 0], parts[:, 1])
-
-
-def sum_along_x(parts):
-    first = lax.axis_index("dp") // 2 == 0
-    given = jnp.where(first, parts[1], parts[0])
-    kept = jnp.where(first, parts[0], parts[1])
-    return kept + lax.ppermute(given, "dp", [(0, 2), (2, 0), (1, 3), (3, 1)])
 
 
 def adam_update(value, first, second, grad):
@@ -669,8 +637,14 @@
 CHUNK = 96
 
 
-def teacher_kernel(x_ref, w_ref, vec_ref, mask_ref, y_ref, s_ref, qkv_ref, up_ref, context_ref):
+def teacher_kernel(
+    denom, x_ref, w_ref, vec_ref, mask_ref, zero_ref, last_ref, proj_ref, bias_ref, weight_ref, pick_ref,
+    s_ref, back_zero, back_last, proj_out, bias_out, loss_ref, picked_ref, t_picked_ref,
+    low_ref, qkv_ref, up_ref, context_ref,
+):
     size = DT // HT
+    for ref in (proj_out, bias_out, loss_ref):
+        ref[...] = jnp.zeros_like(ref)
     for index in range(3 * DT // CHUNK):
         made = regroup(w_ref[index], 3)
         for part in range(3):
@@ -736,26 +710,57 @@
             outer = outer + jnp.dot(
                 gelu(inner).astype(jnp.bfloat16), w_down, preferred_element_type=jnp.float32
             )
-        y_ref[at, :] = norm_forward(
+        made = norm_forward(
             middle + outer + vector(6 + many), vector(7 + many), vector(8 + many)
         )[0]
+        low_ref[at, :] = made.astype(jnp.bfloat16)
+        pairs = ((zero_ref, x_low.astype(jnp.float32), back_zero), (last_ref, made, back_last))
+        for source_ref, target, back_ref in pairs:
+            source = source_ref[at, :].astype(jnp.bfloat16)
+            spread = back_product(source, proj_ref[...]) + bias_ref[...] - target
+            weighted = spread * weight_ref[at, :]
+            loss_ref[...] += jnp.sum(weighted * spread, 0, keepdims=True)
+            d_mapped = (weighted * (2.0 / denom)).astype(jnp.bfloat16)
+            back_ref[at, :] = jnp.dot(d_mapped, proj_ref[...], preferred_element_type=jnp.float32)
+            proj_out[...] += outer_product(d_mapped, source)
+            bias_out[...] += jnp.sum(d_mapped.astype(jnp.float32), 0, keepdims=True)
         return carry
 
-    lax.fori_loop(0, x_ref.shape[0] // TILE, tile, 0)
-
-
-def teacher_forward(x_low, blocks, vectors, mask):
+    tokens = x_ref.shape[0]
+    lax.fori_loop(0, tokens // TILE, tile, 0)
+    line = lax.broadcasted_iota(jnp.int32, (pick_ref.shape[0], tokens), 1)
+    marks = jnp.where(pick_ref[...] == line, 1.0, 0.0).astype(jnp.bfloat16)
+    picked_ref[...] = jnp.dot(
+        marks, last_ref[...].astype(jnp.bfloat16), preferred_element_type=jnp.float32
+    ).astype(jnp.bfloat16)
+    t_picked_ref[...] = jnp.dot(
+        marks, low_ref[...], preferred_element_type=jnp.float32
+    ).astype(jnp.bfloat16)
+
+
+def teacher_forward(x_low, blocks, vectors, mask, embedded, last, proj, bias, weight, picks, denom):
     tokens, length = mask.shape
-    vmem = pl.BlockSpec(memory_space=pltpu.VMEM)
+    full = partial(jax.ShapeDtypeStruct, dtype=jnp.float32)
+    low = partial(jax.ShapeDtypeStruct, dtype=jnp.bfloat16)
+    amount = picks.shape[0]
+    made = (
+        full((tokens, HT * length)),
+        full((tokens, DS)),
+        full((tokens, DS)),
+        full((DT, DS)),
+        full((1, DT)),
+        full((1, DT)),
+        low((amount, DS)),
+        low((amount, DT)),
+    )
+    given = (x_low, blocks, vectors, mask, embedded, last, proj, bias, weight, picks)
     return pl.pallas_call(
-        teacher_kernel,
-        out_shape=(
-            jax.ShapeDtypeStruct((tokens, DT), jnp.float32),
-            jax.ShapeDtypeStruct((tokens, HT * length), jnp.float32),
-        ),
-        in_specs=[vmem] * 4,
-        out_specs=(vmem, vmem),
+        partial(teacher_kernel, denom),
+        out_shape=made,
+        in_specs=[VMEM_SPEC] * len(given),
+        out_specs=(VMEM_SPEC,) * len(made),
         scratch_shapes=[
+            pltpu.VMEM((tokens, DT), jnp.bfloat16),
             pltpu.VMEM((3, DT, DT), jnp.bfloat16),
             pltpu.VMEM((FT // DT, DT, DT), jnp.bfloat16),
             pltpu.VMEM((TILE, DT), jnp.bfloat16),
@@ -764,11 +769,10 @@
         cost_estimate=pl.CostEstimate(
             flops=20 * 10**9, bytes_accessed=25 * 10**6, transcendentals=5 * 10**6
         ),
-    )(x_low, blocks, vectors, mask)
+    )(*given)
 
 
 WIDER = -(-FS // 128) * 128
-VMEM_SPEC = pl.BlockSpec(memory_space=pltpu.VMEM)
 
 
 def refold(source, target, source_width, target_width):
@@ -971,9 +975,11 @@
 
 
 def back_kernel(
-    last, grad_ref, vec_ref, bias_ref, mask_ref, qkv_w, out_w, up_w, down_w,
+    last, first_layer, grad_ref, vec_ref, bias_ref, mask_ref, qkv_w, out_w, up_w, down_w,
     low_ref, qkv_ref, context_ref, one_ref, one_inv, two_ref, two_inv, *refs,
 ):
+    if first_layer:
+        (more_ref, zero_ref, zero_inv, evec_ref), refs = refs[:4], refs[4:]
     if last:
         score_ref, count_ref, refs = refs[0], refs[1], refs[2:]
     hidden_ref, *weight_refs, vec_out, bias_out, refs = (*refs[:9], refs[9:])
@@ -981,6 +987,10 @@
     if last:
         loss_ref, refs = refs[0], refs[1:]
         loss_ref[...] = jnp.zeros_like(loss_ref)
+    if first_layer:
+        (place_ref, edge_ref), refs = refs[:2], refs[2:]
+        place_ref[...] = jnp.zeros_like(place_ref)
+        edge_ref[...] = jnp.zeros_like(edge_ref)
     outer_s, attended_s, q_s, k_s, v_s, middle_s, active_s, inner_s, unfolded, folded = refs
     length = mask_ref.shape[1]
     size = DS // HS
@@ -991,13 +1001,13 @@
     def vector(index):
         return vec_ref[index : index + 1, :]
 
-    def note(index, value):
-        vec_out[index : index + 1, :] += jnp.sum(value.astype(jnp.float32), 0, keepdims=True)
-
-    def norm_back(grad, normed, inverse, gain, index):
+    def note(index, value, to=vec_out):
+        to[index : index + 1, :] += jnp.sum(value.astype(jnp.float32), 0, keepdims=True)
+
+    def norm_back(grad, normed, inverse, gain, index, to=vec_out):
         d_normed = grad * gain
-        note(index, grad * normed)
-        note(index + 1, grad)
+        note(index, grad * normed, to)
+        note(index + 1, grad, to)
         return inverse * (
             d_normed
             - jnp.mean(d_normed, -1, keepdims=True)
@@ -1072,6 +1082,17 @@
             if part != 1:
                 note(part // 2, d_part)
             d_hidden = d_hidden + back_product(d_part, qkv_w[part])
+        if first_layer:
+            d_hidden = norm_back(
+                d_hidden + more_ref[at, :],
+                zero_ref[at, :],
+                zero_inv[at, :],
+                evec_ref[0:1, :],
+                0,
+                edge_ref,
+            )
+            for row in range(TILE // length):
+                place_ref[...] += d_hidden[row * length : (row + 1) * length]
         hidden_ref[at, :] = d_hidden
         return carry
 
@@ -1094,7 +1115,7 @@
         du_ref[:, 128 * tile_at : 128 * tile_at + lanes] = folded[tile_at, :, :lanes]
 
 
-def student_backward(grad, vectors, biases, mask, matrices, saved, last):
+def student_backward(grad, vectors, biases, mask, matrices, saved, last, first_layer):
     tokens, length = mask.shape
     full = partial(jax.ShapeDtypeStruct, dtype=jnp.float32)
     made = [
@@ -1106,12 +1127,15 @@
         full((1, WIDER)),
     ]
     given = [grad, vectors, biases, mask, *matrices, *saved]
+    given += first_layer
     if last:
         given += last
         made.append(full((1, length)))
+    if first_layer:
+        made += [full((length, DS)), full((8, DS))]
     low = partial(pltpu.VMEM, dtype=jnp.bfloat16)
     return pl.pallas_call(
-        partial(back_kernel, bool(last)),
+        partial(back_kernel, bool(last), bool(first_layer)),
         out_shape=tuple(made),
         in_specs=[VMEM_SPEC] * len(given),
         out_specs=(VMEM_SPEC,) * len(made),
@@ -1135,10 +1159,9 @@
 def head_kernel(
     groups, pair, denom, p_ref, t_ref, table_ref, head_ref, d_ref, own_ref, w_ref, *refs
 ):
-    inbox_ref, refs = (refs[0], refs[1:]) if pair else (None, refs)
     (
-        p_all, t_all, p_turned, t_turned, s_logits, t_logits, stats, rows_of, low_grads, tiles, total,
-        send, recv, stat_send, stat_recv, d_send, d_recv, tile_sem, pair_send, pair_recv,
+        p_all, t_all, p_turned, t_turned, s_logits, t_logits, stats, rows_of, inbox, total,
+        send, recv, stat_send, stat_recv, d_send, d_recv, pair_send, pair_recv, out_sem,
     ) = refs
     amount, width = p_ref.shape
     vocab = table_ref.shape[0]
@@ -1149,14 +1172,16 @@
     dp, me = lax.axis_index("dp"), lax.axis_index("fsdp")
     z, y = me // side, me % side
     sibling = (dp // 2 * 2 + 1 - dp % 2, me)
+    beside = ((dp + 2) % lax.axis_size("dp"), me)
     barrier = pltpu.get_barrier_semaphore()
     for step in range(1, groups):
         pl.semaphore_signal(
             barrier, inc=1, device_id=(dp, (me + step) % groups), device_id_type=MESH
         )
     if pair:
-        pl.semaphore_signal(barrier, inc=1, device_id=sibling, device_id_type=MESH)
-    pl.semaphore_wait(barrier, groups - 1 + (1 if pair else 0))
+        for other in (sibling, beside):
+            pl.semaphore_signal(barrier, inc=1, device_id=other, device_id_type=MESH)
+    pl.semaphore_wait(barrier, groups - 1 + (2 if pair else 0))
 
     def both(at, rank, target, own=False):
         return [
@@ -1304,34 +1329,62 @@
         rows_of[back, 3:4, :] = cross / t_sum
         total[back] = jnp.zeros((half, across), jnp.float32)
     own_ref[...] = rows_of[0]
-    narrow = next(size for size in (384, 320, 128) if vocab % size == 0)
-    outs = []
-    for index in range(vocab // narrow):
-        lines = slice(index * narrow, (index + 1) * narrow)
-        table = table_ref[lines, :]
-
-        def differ(back, carry, lines=lines, table=table):
-            row = rows_of[back]
-            made = 2.0 * jnp.exp(s_logits[back, lines, :] - row[0:1])
-            made = made - jnp.exp(t_logits[back, lines, :] - row[1:2]) * row[2:3]
-            low = (made * (1.0 / denom)).astype(jnp.bfloat16)
-            low_grads[back] = low
-            total[back, :width, :] += outer_product(table, low)
+    narrow = next(size for size in (320, 128) if vocab % size == 0)
+    part = vocab // 4 if pair else vocab
+
+    def rows_at(start, amount):
+        return t_logits.at[0, pl.ds(pl.multiple_of(start, 64), amount), 0:half]
+
+    def grade(first):
+        def chunk(index, carry):
+            lines = pl.ds(pl.multiple_of(first + index * narrow, 64), narrow)
+            table = table_ref[lines, :]
+            made = jnp.zeros((narrow, width), jnp.float32)
+            for back in range(side):
+                row = rows_of[back]
+                grads = 2.0 * jnp.exp(s_logits[back, lines, :] - row[0:1])
+                grads = grads - jnp.exp(t_logits[back, lines, :] - row[1:2]) * row[2:3]
+                low = (grads * (1.0 / denom)).astype(jnp.bfloat16)
+                total[back, :width, :] += outer_product(table, low)
+                at_y = (y + side - back) % side
+                states = jnp.concatenate([p_all[line * side + at_y] for line in range(z_size)])
+                made = made + jnp.dot(low, states, preferred_element_type=jnp.float32)
+            t_logits[0, lines, 0:width] = made
             return carry
 
-        lax.fori_loop(0, side, differ, 0)
-        if index >= 2:
-            outs[index - 2].wait()
-        made = jnp.zeros((narrow, width), jnp.float32)
-        for back in range(side):
-            at_y = (y + side - back) % side
-            states = jnp.concatenate([p_all[line * side + at_y] for line in range(z_size)])
-            made = made + jnp.dot(low_grads[back], states, preferred_element_type=jnp.float32)
-        tiles[index % 2] = made
-        outs.append(
-            pltpu.make_async_copy(tiles.at[index % 2], w_ref.at[lines, :], tile_sem.at[index % 2])
-        )
-        outs[-1].start()
+        lax.fori_loop(0, part // narrow, chunk, 0)
+
+    def pair_copy(index, source, target):
+        return pltpu.make_async_remote_copy(
+            source,
+            inbox.at[index],
+            pair_send.at[index],
+            pair_recv.at[index],
+            device_id=target,
+            device_id_type=MESH,
+        )
+
+    given = []
+    if pair:
+        x, core = dp // 2, dp % 2
+        far, near = 1 - x, x
+
+        def start_of(along, other):
+            return (2 * along + (core + other) % 2) * part
+
+        for index, (along, other) in enumerate(((far, 1), (far, 0), (near, 1), (near, 0))):
+            grade(start_of(along, other))
+            if other:
+                given.append(pair_copy(index // 2, rows_at(start_of(along, other), part), sibling))
+                given[-1].start()
+            elif along is far:
+                given[0].wait_recv()
+                lines = pl.ds(pl.multiple_of(start_of(far, 0), 64), part)
+                t_logits[0, lines, 0:half] += inbox[0]
+                given.append(pair_copy(2, rows_at(start_of(far, 0), part), beside))
+                given[-1].start()
+    else:
+        grade(0)
     for back in range(side):
         turned = total[back].T.astype(jnp.bfloat16)
         for line in range(z_size):
@@ -1351,34 +1404,27 @@
 
     for step in range(1, groups):
         d_copy(step).start()
-    for out in outs[-2:]:
-        out.wait()
-    given = []
-    if pair:
-        part = vocab // 4
-        for index in range(2):
-            start = pl.multiple_of((2 * index + 1 - dp % 2) * part, 8)
-            given.append(
-                pltpu.make_async_remote_copy(
-                    w_ref.at[pl.ds(start, part), :],
-                    inbox_ref.at[index],
-                    pair_send.at[index],
-                    pair_recv.at[index],
-                    device_id=sibling,
-                    device_id_type=MESH,
-                )
-            )
-            given[-1].start()
     made = t_all[me, :, half : 2 * half].astype(jnp.float32)
     for step in range(1, groups):
         d_copy(step).wait_recv()
         made = made + t_all[(me + groups - step) % groups, :, 0:half].astype(jnp.float32)
     d_ref[...] = made
+    kept = 0
+    if pair:
+        kept = start_of(near, 0)
+        lines = pl.ds(pl.multiple_of(kept, 64), part)
+        given[2].wait_recv()
+        t_logits[0, lines, 0:half] += inbox[1]
+        given[1].wait_recv()
+        t_logits[0, lines, 0:half] += inbox[2]
+    out = pltpu.make_async_copy(rows_at(kept, part), w_ref, out_sem)
+    out.start()
     for step in range(1, groups):
         stat_copy(step).wait_send()
         d_copy(step).wait_send()
     for copy in given:
-        copy.wait()
+        copy.wait_send()
+    out.wait()
 
 
 def head(picked, t_picked, table, teacher_head, denom, number):
@@ -1390,17 +1436,14 @@
     side, across = groups // z_size, z_size * amount
     half = d_all_width(width)
     assert 2 * half <= DT
-    narrow = next(size for size in (384, 320, 128) if vocab % size == 0)
     full, low = jnp.float32, jnp.bfloat16
     anywhere = pl.BlockSpec(memory_space=pl.ANY)
     dma = pltpu.SemaphoreType.DMA
     made = [
         jax.ShapeDtypeStruct((amount, half), full),
         jax.ShapeDtypeStruct((8, across), full),
-        jax.ShapeDtypeStruct((vocab, width), full),
+        jax.ShapeDtypeStruct((vocab // 4 if pair else vocab, half), full),
     ]
-    if pair:
-        made.append(jax.ShapeDtypeStruct((2, vocab // 4, width), full))
     return pl.pallas_call(
         partial(head_kernel, groups, pair, denom),
         out_shape=tuple(made),
@@ -1415,15 +1458,15 @@
             pltpu.VMEM((side, vocab, across), full),
             pltpu.VMEM((groups, side, 8, across), full),
             pltpu.VMEM((side, 8, across), full),
-            pltpu.VMEM((side, narrow, across), low),
-            pltpu.VMEM((2, narrow, width), full),
+            pltpu.VMEM((3, vocab // 4, half) if pair else (1, 8, 128), full),
             pltpu.VMEM((side, half, across), full),
             *[dma((2 * (2 * z_size + (side - 1) * z_size),))] * 2,
             *[dma((groups,))] * 4,
-            *[dma((2,))] * 3,
+            *[dma((3,))] * 2,
+            dma,
         ],
         compiler_params=pltpu.CompilerParams(
-            collective_id=number, has_side_effects=True, vmem_limit_bytes=60 * 1024 * 1024
+            collective_id=number, has_side_effects=True, vmem_limit_bytes=61 * 1024 * 1024
         ),
     )(picked, t_picked, table, teacher_head)
 
@@ -1614,9 +1657,6 @@
         start += pos_local * DS
         proj_all = flat_all[:, start : start + proj_local * DS].reshape(DT, DS)
 
-    slice_part = lax.optimization_barrier((slice_part, teacher_all))[0]
-    slice_table = lax.all_gather(slice_part, "dp", axis=0, tiled=True)
-
     proj_bias = misc_vec[2 * DS :]
     evec = misc_vec[: 2 * DS].reshape(2, DS)
     cut = 5 * DS
@@ -1629,33 +1669,33 @@
     embedded, normed_zero, inverse_zero, hidden, *saved = student_forward(
         token_rows, places_all, evec, vectors, biases, mask, matrices
     )
-    t_input = teacher_in.reshape(tokens, DT).astype(jnp.float32)
-    t_out, t_scores = teacher_forward(
-        teacher_in.reshape(tokens, DT), teacher_all, teacher_vec.astype(jnp.float32)[None], mask
-    )
-    weight = valid_mask.reshape(tokens, 1).astype(jnp.float32)
-    loss_zero, proj_zero, bias_zero, back_zero = hidden_term(
-        embedded, t_input, proj_all, proj_bias, weight, hidden_denom
-    )
-    loss_last, proj_last, bias_last, back_last = hidden_term(
-        hidden, t_out, proj_all, proj_bias, weight, hidden_denom
-    )
-    hidden_sum = loss_zero + loss_last
-    grad_proj = proj_zero + proj_last
+    slice_part = lax.optimization_barrier((slice_part, teacher_all, hidden))[0]
+    slice_table = lax.all_gather(slice_part, "dp", axis=0, tiled=True)
 
     flat_pick = (
         jnp.arange(rows, dtype=jnp.int32)[:, None] * length + mask_pos.reshape(rows, picks)
     ).reshape(-1)
+    weight = valid_mask.reshape(tokens, 1).astype(jnp.float32)
+    t_scores, back_zero, back_last, grad_proj, grad_bias, squares_of, picked, t_picked = (
+        teacher_forward(
+            teacher_in.reshape(tokens, DT),
+            teacher_all,
+            teacher_vec.astype(jnp.float32)[None],
+            mask,
+            embedded,
+            hidden,
+            proj_all,
+            proj_bias[None],
+            weight,
+            flat_pick[:, None],
+            hidden_denom,
+        )
+    )
+    hidden_sum = jnp.sum(squares_of) / hidden_denom
     pick_marks = (flat_pick[:, None] == lax.broadcasted_iota(jnp.int32, (1, tokens), 1)).astype(
         jnp.bfloat16
     )
-    picked = jnp.dot(
-        pick_marks, hidden.astype(jnp.bfloat16), preferred_element_type=jnp.float32
-    ).astype(jnp.bfloat16)
-    t_picked = jnp.dot(
-        pick_marks, t_out.astype(jnp.bfloat16), preferred_element_type=jnp.float32
-    ).astype(jnp.bfloat16)
-    d_picked, own_stats, head_grad, *inbox = head(
+    d_picked, own_stats, head_grad = head(
         picked, t_picked, slice_table, teacher_head, predict_denom, 4
     )
     own_z = place // (groups // z_size_of(groups))
@@ -1668,9 +1708,7 @@
     d_picked = d_picked[:, :width] - label_rows / predict_denom
     d_hidden = pick_exact(pick_marks, d_picked, True) + back_last
 
-    if inbox:
-        head_grad = sum_along_x(own_parts_of(head_grad) + inbox[0])
-    else:
+    if n_dp != 4:
         head_grad = lax.psum_scatter(head_grad, "dp", scatter_dimension=0, tiled=True)
 
     matrix_grads = [None] * layers
@@ -1686,20 +1724,19 @@
             matrices[4 * layer_index : 4 * layer_index + 4],
             saved[7 * layer_index : 7 * layer_index + 7],
             [t_scores, count.reshape(1, 1)] if layer_index == layers - 1 else [],
+            [] if layer_index else [back_zero, normed_zero, inverse_zero, evec],
         )
         matrix_grads[layer_index] = others[:6]
-        d_vectors, d_bias_up, square = others[6], others[7], others[8:]
+        d_vectors, d_bias_up, more = others[6], others[7], others[8:]
         d_vectors = d_vectors.reshape(-1)
         vector_grads[layer_index] = jnp.concatenate(
             [d_vectors[:cut], d_bias_up[0, :FS], d_vectors[cut:]]
         )
-        if square:
-            attention_sum = jnp.sum(square[0]) / count
+        if layer_index == layers - 1:
+            attention_sum = jnp.sum(more.pop(0)) / count
     d_hidden, head_grad = lax.optimization_barrier((d_hidden, head_grad))
-    d_token, d_gain, d_bias = norm_backward(
-        d_hidden + back_zero, normed_zero, inverse_zero, misc_vec[:DS]
-    )
-    grad_places = jnp.sum(d_token.reshape(rows, length, width), 0)
+    head_grad = head_grad[:, :width]
+    d_token, (grad_places, d_edge) = d_hidden, more
 
     row_grads = jnp.concatenate([d_token, -picked_wide / predict_denom])
     def more_grads(state):
@@ -1710,7 +1747,7 @@
             so_far + give_back(marks_now, wanted_now, row_grads, local_rows, devices),
         )
 
-    grad_small = jnp.concatenate(vector_grads + [d_gain, d_bias, bias_zero + bias_last])
+    grad_small = jnp.concatenate(vector_grads + [d_edge[0], d_edge[1], grad_bias[0]])
     small_local = -(-grad_small.shape[0] // devices)
     small_local = -(-small_local // DS) * DS
     small_padded = jnp.pad(grad_small, (0, devices * small_local - grad_small.shape[0]))

time: 678 us -> 649 us (0.957)
  matrix products: 37.9 us -> 12.4 us
  Pallas kernels: 457 us -> 479 us
  other arithmetic: 56.9 us -> 44.2 us
  waiting for transfers between devices: 10.8 us -> 0.08 us
    dot_general x6 -> x0, matrix products: 21 us -> none  [the longest x2 9.28 us: back_product(): lax.dot_general(grad, weight, (((1,), (1,)), ((), ())), preferred_element...]
    unnamed x132 -> x111, local copies, waits for them, and re-layouts: 10.4 us -> 25.4 us
    pallas_call x1, Pallas kernels: 98.9 us -> 110 us  [head(): pl.pallas_call(partial(head_kernel, groups, pair, denom), out_shape=tuple...]
    ppermute x1 -> x0, waiting for transfers between devices: 10.7 us -> none  [sum_along_x(): return kept + lax.ppermute(given, 'dp', [(0, 2), (2, 0), (1, 3), (3, 1)])]
    pallas_call x3, Pallas kernels: 108 us -> 117 us  [the longest x2 76.1 us: student_backward(): pl.pallas_call(partial(back_kernel, bool(last), bool(first_layer)), out_s...]
  transfers between devices with their start and end apart: 5 -> 4, of which waited for: 1 -> 0; matrix products, arithmetic and copies ran while one was open for 10% -> 8% of each run, Pallas kernels for 34% -> 37%
where the time goes in v3:
time: 649 us; the launch traced here: 640 us
  Pallas kernels  479 us (74%)
  local copies, waits for them, and re-layouts  59.4 us (9%)
  other arithmetic  44.2 us (7%)
  between operations  27.5 us (4%)
  starting transfers between devices  14.6 us (2%)
  matrix products  12.4 us (2%)
    pallas_call x1, Pallas kernels, reduce(): pl.pallas_call(partial(reduce_kernel, plan, len(parts)), out_shape=(jax.S...  121 us
    pallas_call x1, Pallas kernels, head(): pl.pallas_call(partial(head_kernel, groups, pair, denom), out_shape=tuple...  110 us
    pallas_call x2, Pallas kernels, student_backward(): pl.pallas_call(partial(back_kernel, bool(last), bool(first_layer)), out_s...  76.1 us
    pallas_call x1, Pallas kernels, entry(): pl.pallas_call(entry_kernel, out_shape=(jax.ShapeDtypeStruct(asked.shape,...  74 us
    pallas_call x1, Pallas kernels, teacher_forward(): pl.pallas_call(partial(teacher_kernel, denom), out_shape=made, in_specs=[...  41.4 us
    pallas_call x1, Pallas kernels, student_forward(): pl.pallas_call(partial(student_kernel, layers), out_shape=made, in_specs=...  39.1 us
    unnamed x111, local copies, waits for them, and re-layouts  25.4 us
  transfers between devices with their start and end apart: 4, of which 0 were waited for; matrix products, arithmetic and copies ran while one was open for 8% of the time, Pallas kernels for 37%

profile of v3, /device:TPU:0, one launch (start us, length us, event | category | flops | bytes accessed | tf_op | source)
XLA Modules:
  0.0 639.8 jit_solution(14819484668324640165)
XLA Ops:
  7.3 2.2 reshape.583
  13.5 2.4 convert_reduce_fusion
  16.5 2.1 select_reduce_fusion.2
  24.6 74.0 %shard_map.418 = (s32[32,1,128]{2,1,0:T(1,128)S(1)}, bf16[32,256,312]{2,1,0:T(8,128)(2,1)S(1)}, bf16[32,48,312]{2,1,0:T(8,128)(2,1)S(1)}) custom-call(s32[32,1,128]{2,1,0:T(1,128)S(1)} %add_add_fusion.2.ask_ref, bf16[256,312]{1,0:T(8,128)(2,1)S(1)} %maximum_bitcast_fusion.w_ref, bf16[960,312]{1,0:T(8,128)(2,1)S(1)} %convert_element_type.60.table_ref), custom_call_target="tpu_custom_call" | custom-call | tf_op jit(solution)/shard_map/pallas_call | solution.py:298
  98.6 3.9 copy-done
  108.5 3.0 fusion.21
  116.9 7.8 %shard_map.419 = (bf16[3,312,312]{2,1,0:T(8,128)(2,1)S(1)}, bf16[312,312]{1,0:T(8,128)(2,1)S(1)}, bf16[312,1280]{1,0:T(8,128)(2,1)S(1)}, bf16[1280,312]{1,0:T(8,...) custom-call(bf16[32,256,312]{2,1,0:T(8,128)(2,1)} %copy-done), custom_call_target="tpu_custom_call" | custom-call | bytes 20000000 | tf_op jit(solution)/shard_map/pallas_call | solution.py:836
  133.4 39.1 %shard_map.420 = (f32[1024,312]{1,0:T(8,128)}, f32[1024,312]{1,0:T(8,128)}, f32[1024,1]{1,0:T(8,128)}, f32[1024,312]{1,0:T(8,128)}, bf16[1024,312]{1,0:T(8,128)(...) custom-call(f32[1024,312]{1,0:T(8,128)} %slice.296.token_ref, ...), custom_call_target="tpu_custom_call" | custom-call | flops 8000000000 | bytes 40000000 | tf_op jit(solution)/shard_map/pallas_call | solution.py:965
  179.3 2.9 copy.194
  182.2 3.0 copy.193
  185.8 41.4 %shard_map.421 = (f32[1024,1536]{1,0:T(8,128)}, f32[1024,312]{1,0:T(8,128)}, f32[1024,312]{1,0:T(8,128)}, f32[768,312]{1,0:T(8,128)}, f32[1,768]{1,0:T(1,128)}, ...) custom-call(bf16[1024,768]{1,0:T(8,128)(2,1)} %bitcast.147, bf16[96,96,768]{2,1,0:T(8,128)(2,1)} %bitcast.146, ...), custom_call_target="tpu_custom_call" | custom-call | flops 20000000000 | bytes 25000000 | tf_op jit(solution)/shard_map/pallas_call | solution.py:757
  230.7 4.5 copy.182
  235.3 110.1 %shard_map.422 = (f32[160,384]{1,0:T(8,128)}, f32[8,640]{1,0:T(8,128)}, f32[960,384]{1,0:T(8,128)}) custom-call(bf16[160,312]{1,0:T(8,128)(2,1)} %get-tuple-element.267.p_ref, bf16[160,768]{1,0:T(8,128)(2,1)} %get-tuple-element.268.t_ref, bf16[3840,312]{1,0:T(8,128)(2,1)} %bitcast.118, bf16[3840,768]{1,0:T(8,128)(2,1)} %head_ref.1), custom_call_target="tpu_custom_call" | custom-call | tf_op jit(solution)/shard_map/pallas_call | solution.py:1447
  345.4 12.6 %collective-permute-start.1 = (f32[960,384]{1,0:T(8,128)}, f32[960,384]{1,0:T(8,128)}, u32[]{:S(2)}, u32[]{:S(2)}) collective-permute-start(f32[960,384]{1,0:T(8,128)} %get-tuple-element.313), channel_id=1, source_target_pairs={{0,0},{1,4},{2,8},{3,12},{4,16},{5,20},{6,24},{7,28},{8,1},{9,5},{... | collective-permute-start | bytes 4423688 | tf_op jit(solution)/shard_map/ppermute | solution.py:1717
  362.6 38.8 %shard_map.423 = (f32[1024,312]{1,0:T(8,128)}, f32[312,312]{1,0:T(8,128)}, f32[312,312]{1,0:T(8,128)}, f32[312,312]{1,0:T(8,128)}, f32[312,312]{1,0:T(8,128)}, /...) custom-call(f32[1024,312]{1,0:T(8,128)} %fusion.35.grad_ref, ...), custom_call_target="tpu_custom_call" | custom-call | flops 1000000000 | bytes 4000000 | tf_op jit(solution)/shard_map/pallas_call | solution.py:1137
  401.4 37.3 %shard_map.424 = (f32[1024,312]{1,0:T(8,128)}, f32[312,312]{1,0:T(8,128)}, f32[312,312]{1,0:T(8,128)}, f32[312,312]{1,0:T(8,128)}, f32[312,312]{1,0:T(8,128)}, /...) custom-call(f32[1024,312]{1,0:T(8,128)} %get-tuple-element.281.grad_, ...), custom_call_target="tpu_custom_call" | custom-call | flops 1000000000 | bytes 4000000 | tf_op jit(solution)/shard_map/pallas_call | solution.py:1137
  449.3 4.3 fusion.20
  456.1 121.0 %shard_map.425 = (f32[264,312]{1,0:T(8,128)}, f32[32,48,312]{2,1,0:T(8,128)}) custom-call(f32[312,312]{1,0:T(8,128)} %get-tuple-element.292.refs_0_, f32[312,312]{1,0:T(8,128)} %get-tuple-element.293.refs_1_, f32[312,312]{1,0:T(8,128)} %get-tuple-element.294.refs_2_, f32[312,312]{1,0:T(8,128)} %get-tuple-element.295.refs_3_, ...), custom_call_target="tpu_custom_call" | custom-call | tf_op jit(solution)/shard_map/pallas_call | solution.py:491
  583.8 2.2 reduce-precision_convert_fusion.3
  586.0 4.2 fusion.23
  594.5 2.4 multiply_reduce_fusion
  601.7 9.8 %shard_map.426 = f32[32,1,384]{2,1,0:T(1,128)} custom-call(f32[1,384]{1,0:T(1,128)} %reshape.609.x_ref), custom_call_target="tpu_custom_call" | custom-call | tf_op jit(solution)/shard_map/pallas_call | solution.py:96
  613.7 5.5 multiply_subtract_fusion
  619.2 3.0 copy.197
  (251 shorter events, 74.9 us)
Async XLA Ops:
  7.2 5.1 copy-start.48
  7.2 5.2 copy-start.42
  7.2 12.2 %copy-start.41 = (s32[2,4,128]{2,1,0:T(4,128)S(1)}, s32[2,4,128]{2,1,0:T(4,128)}, u32[]{:S(2)}) copy-start(s32[2,4,128]{2,1,0:T(4,128)} %param.32) | copy-start | bytes 12292
  7.2 12.2 %copy-start.29 = (s32[2,4,128]{2,1,0:T(4,128)S(1)}, s32[2,4,128]{2,1,0:T(4,128)}, u32[]{:S(2)}) copy-start(s32[2,4,128]{2,1,0:T(4,128)} %param.33) | copy-start | bytes 12292
  7.2 165.4 %all-gather.4.cloned.1.call-start = ((), (), s32[]{:S(2)}) async-start(), calls=%async_computation | async-start | bytes 14598144 | tf_op jit(solution)/shard_map/all_gather | solution.py:1604
  9.5 13.4 %copy-start.16 = (f32[960,312]{0,1:T(8,128)S(1)}, f32[960,312]{0,1:T(8,128)}, u32[]{:S(2)}) copy-start(f32[960,312]{0,1:T(8,128)} %param.40) | copy-start | bytes 3594244
  9.5 221.2 %all-gather.6.cloned.1.call-start = ((), (), s32[]{:S(2)}) async-start(), calls=%async_computation.1 | async-start | bytes 3194880 | tf_op jit(solution)/shard_map/all_gather | solution.py:1673
  23.6 84.7 %copy-start.27 = (f32[2,3696]{1,0:T(2,128)S(1)}, f32[2,3696]{1,0:T(2,128)}, u32[]{:S(2)}) copy-start(f32[2,3696]{1,0:T(2,128)} %param.52) | copy-start | bytes 88708
  103.6 69.0 %collective-permute-start = (bf16[960,312]{0,1:T(8,128)(2,1)}, bf16[960,312]{0,1:T(8,128)(2,1)S(1)}, u32[]{:S(2)}, u32[]{:S(2)}) collective-permute-start(bf16[960,312]{0,1:T(8,128)(2,1)} %copy.181), channel_id=1, source_target_pairs={{0,0},{4,1},{8,2},{12,3},{16,4},{20,5},{24,6},{28,7},{1,8},{5,9},{... | collective-permute-start | bytes 1797128 | tf_op jit(solution)/shard_map/ppermute | solution.py:1622
  116.9 13.3 %slice-start = ((f32[1392]{0:T(1024)}), f32[624]{0:T(1024)S(1)}, s32[]{:S(2)}) async-start(f32[1392]{0:T(1024)} %param.55), calls=%async_computation.2 | async-start | bytes 8192 | tf_op jit(solution)/shard_map/slice | solution.py:1661
  133.4 40.0 %copy-start.32 = (f32[1392]{0:T(1024)S(1)}, f32[1392]{0:T(1024)}, u32[]{:S(2)}) copy-start(f32[1392]{0:T(1024)} %param.55) | copy-start | bytes 16708
  133.4 40.4 %copy-start.40 = (s32[2,4,20]{2,1,0:T(4,128)S(1)}, s32[2,4,20]{2,1,0:T(4,128)}, u32[]{:S(2)}) copy-start(s32[2,4,20]{2,1,0:T(4,128)} %param.34) | copy-start | bytes 1924
  133.4 40.5 %copy-start.39 = (bf16[9984]{0:T(1024)(128)(2,1)S(1)}, bf16[9984]{0:T(1024)(128)(2,1)}, u32[]{:S(2)}) copy-start(bf16[9984]{0:T(1024)(128)(2,1)} %param.38) | copy-start | bytes 59908
  235.3 122.8 %copy-start.18 = (bf16[160,312]{1,0:T(8,128)(2,1)S(1)}, bf16[160,312]{1,0:T(8,128)(2,1)}, u32[]{:S(2)}) copy-start(bf16[160,312]{1,0:T(8,128)(2,1)} %get-tuple-element.267.p_ref) | copy-start | bytes 299524
  345.4 100.8 %collective-permute-start.1 = (f32[960,384]{1,0:T(8,128)}, f32[960,384]{1,0:T(8,128)}, u32[]{:S(2)}, u32[]{:S(2)}) collective-permute-start(f32[960,384]{1,0:T(8,128)} %get-tuple-element.313), channel_id=1, source_target_pairs={{0,0},{1,4},{2,8},{3,12},{4,16},{5,20},{6,24},{7,28},{8,1},{9,5},{... | collective-permute-start | bytes 4423688 | tf_op jit(solution)/shard_map/ppermute | solution.py:1717
  401.4 38.9 %copy-start.36 = (f32[8,312]{1,0:T(8,128)S(1)}, f32[8,312]{1,0:T(8,128)}, u32[]{:S(2)}) copy-start(f32[8,312]{1,0:T(8,128)} %get-tuple-element.308) | copy-start | bytes 29956
  401.4 39.8 %copy-start.47 = (f32[1,1280]{1,0:T(1,128)S(1)}, f32[1,1280]{1,0:T(1,128)}, u32[]{:S(2)}) copy-start(f32[1,1280]{1,0:T(1,128)} %get-tuple-element.309) | copy-start | bytes 15364
  401.4 41.4 %copy-start.49 = (f32[1,128]{1,0:T(1,128)S(1)}, f32[1,128]{1,0:T(1,128)}, u32[]{:S(2)}) copy-start(f32[1,128]{1,0:T(1,128)} %get-tuple-element.316) | copy-start | bytes 1540
  593.9 19.8 %copy-start.14 = (f32[1,35568]{1,0:T(1,128)}, f32[1,35568]{1,0:T(1,128)S(1)}, u32[]{:S(2)}) copy-start(f32[1,35568]{1,0:T(1,128)S(1)} %stack_reshape.6) | copy-start | bytes 426820
  623.7 4.5 copy-start.24
  623.8 4.5 copy-start.30
  623.8 4.5 copy-start.31
  625.3 4.3 copy-start.28
  625.3 4.3 copy-start.34
  (33 other events, 61.9 us)
Sparse Core Ops, SparseCore 0:
  11.0 159.5 all-gather.3
  173.6 27.1 all-gather.5

commit v4 on v3

--- a/solution.py
+++ b/solution.py
@@ -352,6 +352,7 @@
         row_copy(step).wait()
         return carry
 
+    lax.fori_loop(1, devices, row_start, 0)
     started = []
 
     def push(source, target, index, where):
@@ -418,7 +419,7 @@
                 total = total + from_second[step, z][0][...]
         return total
 
-    for number, key in enumerate(order):
+    for key in order:
         third, second, z = key
         if third == 0 and second == 0:
             continue
@@ -428,8 +429,6 @@
         else:
             target, where = from_second[second, z], (0, second, 0, 0)
         push(held.at[rank[key]], target[0], target[1], where)
-        if number == 0:
-            lax.fori_loop(1, devices, row_start, 0)
 
     def behind(way):
         return (grid.z > 0) if way > 0 else (grid.z < z_size - 1)
@@ -640,9 +639,32 @@
 def teacher_kernel(
     denom, x_ref, w_ref, vec_ref, mask_ref, zero_ref, last_ref, proj_ref, bias_ref, weight_ref, pick_ref,
     s_ref, back_zero, back_last, proj_out, bias_out, loss_ref, picked_ref, t_picked_ref,
-    low_ref, qkv_ref, up_ref, context_ref,
+    low_ref, qkv_ref, up_ref, context_ref, sent, send, recv,
 ):
     size = DT // HT
+    tokens = x_ref.shape[0]
+    line = lax.broadcasted_iota(jnp.int32, (pick_ref.shape[0], tokens), 1)
+    marks = jnp.where(pick_ref[...] == line, 1.0, 0.0).astype(jnp.bfloat16)
+    me, groups = lax.axis_index("fsdp"), lax.axis_size("fsdp")
+    own = jnp.dot(
+        marks, last_ref[...].astype(jnp.bfloat16), preferred_element_type=jnp.float32
+    ).astype(jnp.bfloat16)
+    sent[...] = own
+    picked_ref[me] = own
+    greet(groups, me, False)
+
+    def copy(step):
+        return pltpu.make_async_remote_copy(
+            sent,
+            picked_ref.at[me],
+            send.at[step],
+            recv.at[step],
+            device_id=member((me + step) % groups, False),
+            device_id_type=MESH,
+        )
+
+    for step in range(1, groups):
+        copy(step).start()
     for ref in (proj_out, bias_out, loss_ref):
         ref[...] = jnp.zeros_like(ref)
     for index in range(3 * DT // CHUNK):
@@ -726,23 +748,19 @@
             bias_out[...] += jnp.sum(d_mapped.astype(jnp.float32), 0, keepdims=True)
         return carry
 
-    tokens = x_ref.shape[0]
     lax.fori_loop(0, tokens // TILE, tile, 0)
-    line = lax.broadcasted_iota(jnp.int32, (pick_ref.shape[0], tokens), 1)
-    marks = jnp.where(pick_ref[...] == line, 1.0, 0.0).astype(jnp.bfloat16)
-    picked_ref[...] = jnp.dot(
-        marks, last_ref[...].astype(jnp.bfloat16), preferred_element_type=jnp.float32
-    ).astype(jnp.bfloat16)
     t_picked_ref[...] = jnp.dot(
         marks, low_ref[...], preferred_element_type=jnp.float32
     ).astype(jnp.bfloat16)
+    for step in range(1, groups):
+        copy(step).wait()
 
 
 def teacher_forward(x_low, blocks, vectors, mask, embedded, last, proj, bias, weight, picks, denom):
     tokens, length = mask.shape
     full = partial(jax.ShapeDtypeStruct, dtype=jnp.float32)
     low = partial(jax.ShapeDtypeStruct, dtype=jnp.bfloat16)
-    amount = picks.shape[0]
+    amount, groups = picks.shape[0], lax.axis_size("fsdp")
     made = (
         full((tokens, HT * length)),
         full((tokens, DS)),
@@ -750,7 +768,7 @@
         full((DT, DS)),
         full((1, DT)),
         full((1, DT)),
-        low((amount, DS)),
+        low((groups, amount, DS)),
         low((amount, DT)),
     )
     given = (x_low, blocks, vectors, mask, embedded, last, proj, bias, weight, picks)
@@ -764,8 +782,12 @@
             pltpu.VMEM((3, DT, DT), jnp.bfloat16),
             pltpu.VMEM((FT // DT, DT, DT), jnp.bfloat16),
             pltpu.VMEM((TILE, DT), jnp.bfloat16),
+            pltpu.VMEM((amount, DS), jnp.bfloat16),
+            *[pltpu.SemaphoreType.DMA((groups,))] * 2,
         ],
-        compiler_params=pltpu.CompilerParams(vmem_limit_bytes=58 * 1024 * 1024),
+        compiler_params=pltpu.CompilerParams(
+            collective_id=5, has_side_effects=True, vmem_limit_bytes=58 * 1024 * 1024
+        ),
         cost_estimate=pl.CostEstimate(
             flops=20 * 10**9, bytes_accessed=25 * 10**6, transcendentals=5 * 10**6
         ),
@@ -797,7 +819,7 @@
             target[tile, pl.ds(row, groups, stride=step_out), :] = made
 
 
-def unpack_kernel(plan, layers, w_ref, *refs):
+def unpack_into(plan, layers, w_ref, *refs):
     place_ref, proj_ref, square, wide, folded, unfolded, small = refs[4 * layers :]
     for layer in range(layers):
         qkv_ref, out_ref, up_ref, down_ref = refs[4 * layer : 4 * layer + 4]
@@ -830,28 +852,13 @@
     proj_ref[...] = small[1].astype(jnp.bfloat16)
 
 
-def unpack(blocks, plan, layers, length):
+def unpack_shapes(layers, length):
     low = partial(jax.ShapeDtypeStruct, dtype=jnp.bfloat16)
-    full = jnp.float32
-    return pl.pallas_call(
-        partial(unpack_kernel, plan, layers),
-        out_shape=(
-            *[low((3, DS, DS)), low((DS, DS)), low((DS, WIDER)), low((WIDER, DS))] * layers,
-            low((length, DS)),
-            low((DT, DS)),
-        ),
-        in_specs=[VMEM_SPEC],
-        out_specs=(VMEM_SPEC,) * (4 * layers + 2),
-        scratch_shapes=[
-            pltpu.VMEM((4, DS, DS), full),
-            pltpu.VMEM((FS, DS), full),
-            pltpu.VMEM((-(-DS // 128), FS, 128), full),
-            pltpu.VMEM((WIDER // 128, DS, 128), full),
-            pltpu.VMEM((2, DT, DS), full),
-        ],
-        compiler_params=pltpu.CompilerParams(vmem_limit_bytes=50 * 1024 * 1024),
-        cost_estimate=pl.CostEstimate(flops=0, bytes_accessed=20 * 10**6, transcendentals=0),
-    )(blocks)
+    return (
+        *[low((3, DS, DS)), low((DS, DS)), low((DS, WIDER)), low((WIDER, DS))] * layers,
+        low((length, DS)),
+        low((DT, DS)),
+    )
 
 
 def by_heads(value, heads):
@@ -868,10 +875,13 @@
 
 
 def student_kernel(
-    layers, token_ref, place_ref, evec_ref, vec_ref, bias_ref, mask_ref,
-    *refs,
+    plan, layers, token_ref, evec_ref, vec_ref, bias_ref, mask_ref, *refs,
 ):
-    matrices, refs = refs[: 4 * layers], refs[4 * layers :]
+    ready = 4 * layers + 2
+    if plan:
+        w_ref, *refs = refs
+        unpack_into(plan, layers, w_ref, *refs[:ready], *refs[-5:])
+    matrices, place_ref, refs = refs[: 4 * layers], refs[4 * layers], refs[ready:]
     emb_ref, zero_ref, zero_inv, last_ref = refs[:4]
     length = mask_ref.shape[1]
     size = DS // HS
@@ -941,12 +951,15 @@
     lax.fori_loop(0, token_ref.shape[0] // TILE, tile, 0)
 
 
-def student_forward(token_rows, places, evec, vectors, biases, mask, matrices):
+def student_forward(token_rows, evec, vectors, biases, mask, plan, blocks, matrices):
     tokens = token_rows.shape[0]
     layers = vectors.shape[0]
     full = partial(jax.ShapeDtypeStruct, dtype=jnp.float32)
     low = partial(jax.ShapeDtypeStruct, dtype=jnp.bfloat16)
+    length = mask.shape[1]
+    shapes = () if matrices else unpack_shapes(layers, length)
     made = (
+        *shapes,
         full((tokens, DS)),
         full((tokens, DS)),
         full((tokens, 1)),
@@ -962,16 +975,29 @@
         ]
         * layers,
     )
-    return pl.pallas_call(
-        partial(student_kernel, layers),
+    given = (token_rows, evec, vectors, biases, mask, *(matrices or [blocks]))
+    all_of = pl.pallas_call(
+        partial(student_kernel, plan, layers),
         out_shape=made,
-        in_specs=[VMEM_SPEC] * (6 + len(matrices)),
+        in_specs=[VMEM_SPEC] * len(given),
         out_specs=(VMEM_SPEC,) * len(made),
+        scratch_shapes=(
+            []
+            if matrices
+            else [
+                pltpu.VMEM((4, DS, DS), jnp.float32),
+                pltpu.VMEM((FS, DS), jnp.float32),
+                pltpu.VMEM((-(-DS // 128), FS, 128), jnp.float32),
+                pltpu.VMEM((WIDER // 128, DS, 128), jnp.float32),
+                pltpu.VMEM((2, DT, DS), jnp.float32),
+            ]
+        ),
         compiler_params=pltpu.CompilerParams(vmem_limit_bytes=58 * 1024 * 1024),
         cost_estimate=pl.CostEstimate(
             flops=8 * 10**9, bytes_accessed=40 * 10**6, transcendentals=6 * 10**6
         ),
-    )(token_rows, places, evec, vectors, biases, mask, *matrices)
+    )(*given)
+    return list(all_of[: len(shapes)] or matrices), all_of[len(shapes) :]
 
 
 def back_kernel(
@@ -1157,13 +1183,13 @@
 
 
 def head_kernel(
-    groups, pair, denom, p_ref, t_ref, table_ref, head_ref, d_ref, own_ref, w_ref, *refs
+    groups, pair, denom, p_all, t_ref, table_ref, head_ref, d_ref, own_ref, w_ref, *refs
 ):
     (
-        p_all, t_all, p_turned, t_turned, s_logits, t_logits, stats, rows_of, inbox, total,
+        t_all, p_turned, t_turned, s_logits, t_logits, stats, rows_of, inbox, total,
         send, recv, stat_send, stat_recv, d_send, d_recv, pair_send, pair_recv, out_sem,
     ) = refs
-    amount, width = p_ref.shape
+    amount, width = p_all.shape[1:]
     vocab = table_ref.shape[0]
     z_size = z_size_of(groups)
     side = groups // z_size
@@ -1186,14 +1212,13 @@
     def both(at, rank, target, own=False):
         return [
             pltpu.make_async_remote_copy(
-                given if own else held.at[at],
-                held.at[at],
-                send.at[2 * rank + index],
-                recv.at[2 * rank + index],
+                t_ref if own else t_all.at[at],
+                t_all.at[at],
+                send.at[rank],
+                recv.at[rank],
                 device_id=(dp, target),
                 device_id_type=MESH,
             )
-            for index, (given, held) in enumerate(((p_ref, p_all), (t_ref, t_all)))
         ]
 
     def begin(copies):
@@ -1262,7 +1287,6 @@
         for index, value in enumerate(made):
             stats[me, at_y, index : index + 1, :] = value
 
-    p_all[me] = p_ref[...]
     t_all[me] = t_ref[...]
     for way in (1, -1):
         made, wanted = z_copies(0, way, False)
@@ -1430,7 +1454,7 @@
 def head(picked, t_picked, table, teacher_head, denom, number):
     groups, n_dp = lax.axis_size("fsdp"), lax.axis_size("dp")
     pair = n_dp == 4
-    amount, width = picked.shape
+    amount, width = picked.shape[1:]
     vocab = table.shape[0]
     z_size = z_size_of(groups)
     side, across = groups // z_size, z_size * amount
@@ -1450,7 +1474,6 @@
         in_specs=[VMEM_SPEC] * 4,
         out_specs=(VMEM_SPEC, VMEM_SPEC) + (anywhere,) * (len(made) - 2),
         scratch_shapes=[
-            pltpu.VMEM((groups, amount, width), low),
             pltpu.VMEM((groups, amount, DT), low),
             pltpu.VMEM((width, across), low),
             pltpu.VMEM((DT, across), low),
@@ -1460,7 +1483,7 @@
             pltpu.VMEM((side, 8, across), full),
             pltpu.VMEM((3, vocab // 4, half) if pair else (1, 8, 128), full),
             pltpu.VMEM((side, half, across), full),
-            *[dma((2 * (2 * z_size + (side - 1) * z_size),))] * 2,
+            *[dma((2 * z_size + (side - 1) * z_size,))] * 2,
             *[dma((groups,))] * 4,
             *[dma((3,))] * 2,
             dma,
@@ -1541,6 +1564,74 @@
     sent = pick_exact(marks, grads)
     got = exchange(sent.reshape(devices, SLOTS, -1), 2)
     return pick_exact(wanted_marks(wanted, local_rows), got.reshape(devices * SLOTS, -1), True)
+
+
+def finish_kernel(
+    at, rows_ref, wanted_ref, more_ref, head_ref, reduced_ref, note_ref, g_ref, notes_ref, sent, send, recv
+):
+    count, me = notes_ref.shape[0], place_of()
+    greet(count, me, True)
+    value = rows_ref[...]
+    width = value.shape[1]
+    high = value.astype(jnp.bfloat16)
+    rest = value - high.astype(jnp.float32)
+    middle = rest.astype(jnp.bfloat16)
+    low = (rest - middle.astype(jnp.float32)).astype(jnp.bfloat16)
+    rows = g_ref.shape[0]
+    step = next(size for size in (192, 120, 8) if rows % size == 0)
+    squares = jnp.sum(reduced_ref[...] * reduced_ref[...], 0, keepdims=True)
+    squares = jnp.sum(squares, 1, keepdims=True)
+    line = lax.broadcasted_iota(jnp.int32, (step, value.shape[0]), 0)
+    for first in range(0, rows, step):
+        marks = jnp.where(line + first == wanted_ref[...], 1.0, 0.0).astype(jnp.bfloat16)
+        made = more_ref[first : first + step, :] + head_ref[first : first + step, :width]
+        for term in (high, middle, low):
+            made = made + jnp.dot(marks, term, preferred_element_type=jnp.float32)
+        g_ref[first : first + step, :] = made
+        squares = squares + jnp.sum(jnp.sum(made * made, 0, keepdims=True), 1, keepdims=True)
+    lane = lax.broadcasted_iota(jnp.int32, sent.shape, 1)
+    note = jnp.where(lane == at, squares, note_ref[...])
+    sent[...] = note
+    notes_ref[me] = note
+
+    def copy(step):
+        return pltpu.make_async_remote_copy(
+            sent,
+            notes_ref.at[me],
+            send.at[step],
+            recv.at[step],
+            device_id=member((me + step) % count, True),
+            device_id_type=MESH,
+        )
+
+    def start(step, carry):
+        copy(step).start()
+        return carry
+
+    def finish(step, carry):
+        copy(step).wait()
+        return carry
+
+    lax.fori_loop(1, count, start, 0)
+    lax.fori_loop(1, count, finish, 0)
+
+
+def finish(row_blocks, wanted, more, head_grad, reduced, note, at, number):
+    count = lax.axis_size("dp") * lax.axis_size("fsdp")
+    dma = pltpu.SemaphoreType.DMA
+    return pl.pallas_call(
+        partial(finish_kernel, at),
+        out_shape=(
+            jax.ShapeDtypeStruct(more.shape, more.dtype),
+            jax.ShapeDtypeStruct((count,) + note.shape, note.dtype),
+        ),
+        in_specs=[VMEM_SPEC] * 6,
+        out_specs=(VMEM_SPEC,) * 2,
+        scratch_shapes=[pltpu.VMEM(note.shape, note.dtype), dma((count,)), dma((count,))],
+        compiler_params=pltpu.CompilerParams(
+            collective_id=number, has_side_effects=True, vmem_limit_bytes=40 * 1024 * 1024
+        ),
+    )(row_blocks, wanted[None], more, head_grad, reduced, note)
 
 
 def local(
@@ -1635,9 +1726,9 @@
     token_rows, label_rows = (all_rows[:tokens], all_rows[tokens:])
     pos_local, proj_local = pos_table.shape[0], proj_weight.shape[1]
     if by_rows:
-        where = block_plan(devices, chunk, layers, (pos_local, proj_local))
-        *matrices, places_all, proj_all = unpack(weights_all, where, layers, length)
+        where, matrices = block_plan(devices, chunk, layers, (pos_local, proj_local)), []
     else:
+        where = ()
         flat_all = weights_all.reshape(devices, -1)
         split = []
         for index in range(layers):
@@ -1655,7 +1746,7 @@
         start = layers * flat_local
         places_all = flat_all[:, start : start + pos_local * DS].reshape(length, DS)
         start += pos_local * DS
-        proj_all = flat_all[:, start : start + proj_local * DS].reshape(DT, DS)
+        matrices += [places_all, flat_all[:, start : start + proj_local * DS].reshape(DT, DS)]
 
     proj_bias = misc_vec[2 * DS :]
     evec = misc_vec[: 2 * DS].reshape(2, DS)
@@ -1666,9 +1757,11 @@
     biases = jnp.pad(layer_vec[:, cut : cut + FS], ((0, 0), (0, WIDER - FS)))[:, None]
 
     mask = jnp.where(pair_mask, 2.0, jnp.where(allowed, 1.0, 0.0)).reshape(tokens, length)
-    embedded, normed_zero, inverse_zero, hidden, *saved = student_forward(
-        token_rows, places_all, evec, vectors, biases, mask, matrices
-    )
+    matrices, made = student_forward(
+        token_rows, evec, vectors, biases, mask, where, weights_all, matrices
+    )
+    embedded, normed_zero, inverse_zero, hidden, *saved = made
+    proj_all = matrices[-1]
     slice_part = lax.optimization_barrier((slice_part, teacher_all, hidden))[0]
     slice_table = lax.all_gather(slice_part, "dp", axis=0, tiled=True)
 
@@ -1676,7 +1769,7 @@
         jnp.arange(rows, dtype=jnp.int32)[:, None] * length + mask_pos.reshape(rows, picks)
     ).reshape(-1)
     weight = valid_mask.reshape(tokens, 1).astype(jnp.float32)
-    t_scores, back_zero, back_last, grad_proj, grad_bias, squares_of, picked, t_picked = (
+    t_scores, back_zero, back_last, grad_proj, grad_bias, squares_of, picked_all, t_picked = (
         teacher_forward(
             teacher_in.reshape(tokens, DT),
             teacher_all,
@@ -1695,8 +1788,9 @@
     pick_marks = (flat_pick[:, None] == lax.broadcasted_iota(jnp.int32, (1, tokens), 1)).astype(
         jnp.bfloat16
     )
+    picked = lax.dynamic_index_in_dim(picked_all, place, 0, False)
     d_picked, own_stats, head_grad = head(
-        picked, t_picked, slice_table, teacher_head, predict_denom, 4
+        picked_all, t_picked, slice_table, teacher_head, predict_denom, 4
     )
     own_z = place // (groups // z_size_of(groups))
     own_stats = lax.dynamic_slice_in_dim(own_stats, own_z * rows * picks, rows * picks, 1)
@@ -1735,7 +1829,6 @@
         if layer_index == layers - 1:
             attention_sum = jnp.sum(more.pop(0)) / count
     d_hidden, head_grad = lax.optimization_barrier((d_hidden, head_grad))
-    head_grad = head_grad[:, :width]
     d_token, (grad_places, d_edge) = d_hidden, more
 
     row_grads = jnp.concatenate([d_token, -picked_wide / predict_denom])
@@ -1768,11 +1861,8 @@
         grad_parts = [pack([part.reshape(devices, -1) for part in wides + rest], *block[::-1])]
         block_rows_of = ()
     reduced, row_blocks = reduce(grad_parts, block_rows_of, block, sent, 7)
-    g_table = pick_exact(
-        wanted_marks(wanted, local_rows), row_blocks.reshape(devices * SLOTS, width), True
-    )
-    g_table = lax.while_loop(lambda state: state[0] < rounds, more_grads, (1, g_table))[1]
-    g_table = g_table + head_grad
+    more = jnp.zeros((local_rows, width), jnp.float32)
+    more = lax.while_loop(lambda state: state[0] < rounds, more_grads, (1, more))[1]
     if by_rows:
         pieces = []
         start = 0
@@ -1787,18 +1877,21 @@
     g_places = pieces[layers].reshape(pos_local, DS)
     g_proj = pieces[layers + 1].reshape(proj_local, DS).T
     small_part = pieces[layers + 2].reshape(-1)
-    squares = (
-        jnp.sum(g_table * g_table)
-        + jnp.sum(g_places * g_places)
-        + jnp.sum(g_proj * g_proj)
-        + jnp.sum(layer_acc * layer_acc)
-        + jnp.sum(small_part * small_part)
-    )
     note = jnp.concatenate(
-        [small_part, jnp.stack([attention_sum + hidden_sum + predict_sum, squares])]
-    )
-    note = jnp.pad(note, (0, -(-note.shape[0] // 128) * 128 - note.shape[0])).reshape(1, -1)
-    notes_all = exchange(note, 8, spread=True)[:, 0]
+        [small_part, (attention_sum + hidden_sum + predict_sum).reshape(1)]
+    )
+    note = jnp.pad(note, (0, -(-(small_local + 2) // 128) * 128 - note.shape[0])).reshape(1, -1)
+    g_table, notes_all = finish(
+        row_blocks.reshape(devices * SLOTS, width),
+        wanted,
+        more,
+        head_grad,
+        reduced,
+        note,
+        small_local + 1,
+        8,
+    )
+    notes_all = notes_all[:, 0]
     small = notes_all[:, :small_local].reshape(-1)
     loss = jnp.sum(notes_all[:, small_local])
     norm = jnp.sqrt(jnp.sum(notes_all[:, small_local + 1]))

time: 649 us -> 623 us (0.960)
  starting transfers between devices: 14.6 us -> 4.02 us
  other arithmetic: 44.2 us -> 34.5 us
    ppermute x1, starting transfers between devices: 12.6 us -> 2.03 us  [local(): head_grad = lax.ppermute(head_grad, BOTH, to_owner)]
    pallas_call x1, Pallas kernels: 110 us -> 99.6 us  [head(): pl.pallas_call(partial(head_kernel, groups, pair, denom), out_shape=tuple...]
    unnamed x111 -> x95, local copies, waits for them, and re-layouts: 25.4 us -> 19.1 us
    pallas_call x3 -> x2, Pallas kernels: 56.7 us -> 59.8 us  [the longest x1 45.1 us: student_forward(): pl.pallas_call(partial(student_kernel, plan, layers), out_shape=made, in_...]
  transfers between devices with their start and end apart: 4 -> 4, of which waited for: 0 -> 1; matrix products, arithmetic and copies ran while one was open for 8% -> 8% of each run, Pallas kernels for 37% -> 39%
where the time goes in v4:
time: 623 us; the launch traced here: 615 us
  Pallas kernels  479 us (77%)
  local copies, waits for them, and re-layouts  57.1 us (9%)
  other arithmetic  34.5 us (6%)
  between operations  24.3 us (4%)
  matrix products  8.27 us (1%)
    pallas_call x1, Pallas kernels, reduce(): pl.pallas_call(partial(reduce_kernel, plan, len(parts)), out_shape=(jax.S...  125 us
    pallas_call x1, Pallas kernels, head(): pl.pallas_call(partial(head_kernel, groups, pair, denom), out_shape=tuple...  99.6 us
    pallas_call x2, Pallas kernels, student_backward(): pl.pallas_call(partial(back_kernel, bool(last), bool(first_layer)), out_s...  76.1 us
    pallas_call x1, Pallas kernels, entry(): pl.pallas_call(entry_kernel, out_shape=(jax.ShapeDtypeStruct(asked.shape,...  74.2 us
    pallas_call x1, Pallas kernels, student_forward(): pl.pallas_call(partial(student_kernel, plan, layers), out_shape=made, in_...  45.1 us
    pallas_call x1, Pallas kernels, teacher_forward(): pl.pallas_call(partial(teacher_kernel, denom), out_shape=made, in_specs=[...  45 us
    unnamed x95, local copies, waits for them, and re-layouts  19.1 us
    pallas_call x1, Pallas kernels, finish(): pl.pallas_call(partial(finish_kernel, at), out_shape=(jax.ShapeDtypeStruc...  14.8 us
  transfers between devices with their start and end apart: 4, of which 1 were waited for; matrix products, arithmetic and copies ran while one was open for 8% of the time, Pallas kernels for 39%

profile of v4, /device:TPU:0, one launch (start us, length us, event | category | flops | bytes accessed | tf_op | source)
XLA Modules:
  0.0 614.9 jit_solution(7724577279519820624)
XLA Ops:
  7.3 2.2 reshape.587
  13.5 2.4 convert_reduce_fusion
  16.5 2.1 select_reduce_fusion.2
  24.6 74.2 %shard_map.418 = (s32[32,1,128]{2,1,0:T(1,128)S(1)}, bf16[32,256,312]{2,1,0:T(8,128)(2,1)S(1)}, bf16[32,48,312]{2,1,0:T(8,128)(2,1)S(1)}) custom-call(s32[32,1,128]{2,1,0:T(1,128)S(1)} %add_add_fusion.2.ask_ref, bf16[256,312]{1,0:T(8,128)(2,1)S(1)} %maximum_bitcast_fusion.w_ref, bf16[960,312]{1,0:T(8,128)(2,1)S(1)} %convert_element_type.61.table_ref), custom_call_target="tpu_custom_call" | custom-call | tf_op jit(solution)/shard_map/pallas_call | solution.py:298
  98.7 4.0 copy-done.3
  108.7 3.0 fusion.21
  111.7 2.0 while.22
  113.8 2.1 copy.177
  120.5 45.1 %shard_map.419 = (bf16[3,312,312]{2,1,0:T(8,128)(2,1)}, bf16[312,312]{1,0:T(8,128)(2,1)}, bf16[312,1280]{1,0:T(8,128)(2,1)}, bf16[1280,312]{1,0:T(8,128)(2,1)}, ...) custom-call(f32[1024,312]{1,0:T(8,128)} %slice.280.token_ref, ...), custom_call_target="tpu_custom_call" | custom-call | flops 8000000000 | bytes 40000000 | tf_op jit(solution)/shard_map/pallas_call | solution.py:979
  165.6 4.9 all-gather.4.cloned.1.call-done
  180.2 45.0 %shard_map.420 = (f32[1024,1536]{1,0:T(8,128)}, f32[1024,312]{1,0:T(8,128)}, f32[1024,312]{1,0:T(8,128)}, f32[768,312]{1,0:T(8,128)}, f32[1,768]{1,0:T(1,128)}, ...) custom-call(bf16[1024,768]{1,0:T(8,128)(2,1)} %bitcast.145, ...), custom_call_target="tpu_custom_call" | custom-call | flops 20000000000 | bytes 25000000 | tf_op jit(solution)/shard_map/pallas_call | solution.py:775
  228.8 4.9 copy.182
  233.7 99.6 %shard_map.421 = (f32[160,384]{1,0:T(8,128)}, f32[8,640]{1,0:T(8,128)}, f32[960,384]{1,0:T(8,128)}) custom-call(bf16[8,160,312]{2,1,0:T(8,128)(2,1)} %get-tuple-element.259.p_all, bf16[160,768]{1,0:T(8,128)(2,1)} %get-tuple-element.260.t_ref, bf16[3840,312]{1,0:T(8,128)(2,1)} %bitcast.116, bf16[3840,768]{1,0:T(8,128)(2,1)} %head_ref.1), custom_call_target="tpu_custom_call" | custom-call | tf_op jit(solution)/shard_map/pallas_call | solution.py:1471
  333.3 2.0 collective-permute-start.1
  338.1 2.0 fusion.27.grad_ref
  340.1 38.8 %shard_map.422 = (f32[1024,312]{1,0:T(8,128)}, f32[312,312]{1,0:T(8,128)}, f32[312,312]{1,0:T(8,128)}, f32[312,312]{1,0:T(8,128)}, f32[312,312]{1,0:T(8,128)}, /...) custom-call(f32[1024,312]{1,0:T(8,128)} %fusion.27.grad_ref, ...), custom_call_target="tpu_custom_call" | custom-call | flops 1000000000 | bytes 4000000 | tf_op jit(solution)/shard_map/pallas_call | solution.py:1163
  379.0 37.3 %shard_map.423 = (f32[1024,312]{1,0:T(8,128)}, f32[312,312]{1,0:T(8,128)}, f32[312,312]{1,0:T(8,128)}, f32[312,312]{1,0:T(8,128)}, f32[312,312]{1,0:T(8,128)}, /...) custom-call(f32[1024,312]{1,0:T(8,128)} %get-tuple-element.277.grad_, ...), custom_call_target="tpu_custom_call" | custom-call | flops 1000000000 | bytes 4000000 | tf_op jit(solution)/shard_map/pallas_call | solution.py:1163
  426.8 4.3 fusion.20
  432.9 3.0 copy.187
  435.9 124.8 %shard_map.424 = (f32[264,312]{1,0:T(8,128)}, f32[32,48,312]{2,1,0:T(8,128)}) custom-call(f32[312,312]{1,0:T(8,128)} %get-tuple-element.292.refs_0_, f32[312,312]{1,0:T(8,128)} %get-tuple-element.293.refs_1_, f32[312,312]{1,0:T(8,128)} %get-tuple-element.294.refs_2_, f32[312,312]{1,0:T(8,128)} %get-tuple-element.295.refs_3_, ...), custom_call_target="tpu_custom_call" | custom-call | tf_op jit(solution)/shard_map/pallas_call | solution.py:490
  570.6 14.8 %shard_map.425 = (f32[960,312]{1,0:T(8,128)S(1)}, f32[32,1,384]{2,1,0:T(1,128)S(1)}) custom-call(f32[1536,312]{1,0:T(8,128)S(1)} %bitcast.111, s32[1,1536]{1,0:T(1,128)S(1)} %broadcast_in_dim_reshape_squeeze.3.wanted_ref, f32[960,312]{1,0:T(8,128)S(1)} %copy.188.more_ref, f32[960,384]{1,0:T(8,128)S(1)} %collective-permute-done.1.head_ref, ...), custom_call_target="tpu_custom_call" | custom-call | tf_op jit(solution)/shard_map/pallas_call | solution.py:1622
  587.9 5.0 multiply_subtract_fusion
  592.9 2.9 copy.197
  603.3 2.0 multiply_subtract_fusion.1
  (228 shorter events, 62.2 us)
Async XLA Ops:
  7.2 5.1 copy-start.42
  7.2 5.2 copy-start.36
  7.2 12.2 %copy-start.35 = (s32[2,4,128]{2,1,0:T(4,128)S(1)}, s32[2,4,128]{2,1,0:T(4,128)}, u32[]{:S(2)}) copy-start(s32[2,4,128]{2,1,0:T(4,128)} %param.32) | copy-start | bytes 12292
  7.2 12.2 %copy-start.23 = (s32[2,4,128]{2,1,0:T(4,128)S(1)}, s32[2,4,128]{2,1,0:T(4,128)}, u32[]{:S(2)}) copy-start(s32[2,4,128]{2,1,0:T(4,128)} %param.33) | copy-start | bytes 12292
  7.2 163.3 %all-gather.4.cloned.1.call-start = ((), (), s32[]{:S(2)}) async-start(), calls=%async_computation | async-start | bytes 14598144 | tf_op jit(solution)/shard_map/all_gather | solution.py:1695
  9.5 13.4 %copy-start.9 = (f32[960,312]{0,1:T(8,128)S(1)}, f32[960,312]{0,1:T(8,128)}, u32[]{:S(2)}) copy-start(f32[960,312]{0,1:T(8,128)} %param.40) | copy-start | bytes 3594244
  9.5 219.3 %all-gather.6.cloned.1.call-start = ((), (), s32[]{:S(2)}) async-start(), calls=%async_computation.1 | async-start | bytes 3194880 | tf_op jit(solution)/shard_map/all_gather | solution.py:1766
  23.6 84.9 %copy-start.21 = (f32[2,3696]{1,0:T(2,128)S(1)}, f32[2,3696]{1,0:T(2,128)}, u32[]{:S(2)}) copy-start(f32[2,3696]{1,0:T(2,128)} %param.52) | copy-start | bytes 88708
  103.9 61.7 %collective-permute-start = (bf16[960,312]{0,1:T(8,128)(2,1)}, bf16[960,312]{0,1:T(8,128)(2,1)S(1)}, u32[]{:S(2)}, u32[]{:S(2)}) collective-permute-start(bf16[960,312]{0,1:T(8,128)(2,1)} %copy.181), channel_id=1, source_target_pairs={{0,0},{4,1},{8,2},{12,3},{16,4},{20,5},{24,6},{28,7},{1,8},{5,9},{... | collective-permute-start | bytes 1797128 | tf_op jit(solution)/shard_map/ppermute | solution.py:1713
  115.8 4.7 copy-start.6
  120.5 50.1 %copy-start.26 = (f32[1392]{0:T(1024)S(1)}, f32[1392]{0:T(1024)}, u32[]{:S(2)}) copy-start(f32[1392]{0:T(1024)} %param.55) | copy-start | bytes 16708
  120.5 50.4 %copy-start.34 = (s32[2,4,20]{2,1,0:T(4,128)S(1)}, s32[2,4,20]{2,1,0:T(4,128)}, u32[]{:S(2)}) copy-start(s32[2,4,20]{2,1,0:T(4,128)} %param.34) | copy-start | bytes 1924
  120.5 50.6 %copy-start.33 = (bf16[9984]{0:T(1024)(128)(2,1)S(1)}, bf16[9984]{0:T(1024)(128)(2,1)}, u32[]{:S(2)}) copy-start(bf16[9984]{0:T(1024)(128)(2,1)} %param.38) | copy-start | bytes 59908
  165.6 10.8 %copy-start.10 = (f32[960,312]{0,1:T(8,128)S(1)}, f32[960,312]{0,1:T(8,128)}, u32[]{:S(2)}) copy-start(f32[960,312]{0,1:T(8,128)} %param.42) | copy-start | bytes 3594244
  165.6 4.9 copy-start.14
  171.1 7.0 %copy-start.11 = (f32[960,312]{0,1:T(8,128)S(1)}, f32[960,312]{0,1:T(8,128)}, u32[]{:S(2)}) copy-start(f32[960,312]{0,1:T(8,128)} %param.41) | copy-start | bytes 3594244
  333.3 90.5 %collective-permute-start.1 = (f32[960,384]{1,0:T(8,128)}, f32[960,384]{1,0:T(8,128)S(1)}, u32[]{:S(2)}, u32[]{:S(2)}) collective-permute-start(f32[960,384]{1,0:T(8,128)} %get-tuple-element.313), channel_id=1, source_target_pairs={{0,0},{1,4},{2,8},{3,12},{4,16},{5,20},{6,24},{7,28},{8,1},{9,5},{... | collective-permute-start | bytes 4423688 | tf_op jit(solution)/shard_map/ppermute | solution.py:1811
  378.9 38.9 %copy-start.30 = (f32[8,312]{1,0:T(8,128)S(1)}, f32[8,312]{1,0:T(8,128)}, u32[]{:S(2)}) copy-start(f32[8,312]{1,0:T(8,128)} %get-tuple-element.308) | copy-start | bytes 29956
  379.0 39.8 %copy-start.41 = (f32[1,1280]{1,0:T(1,128)S(1)}, f32[1,1280]{1,0:T(1,128)}, u32[]{:S(2)}) copy-start(f32[1,1280]{1,0:T(1,128)} %get-tuple-element.309) | copy-start | bytes 15364
  379.0 41.4 %copy-start.43 = (f32[1,128]{1,0:T(1,128)S(1)}, f32[1,128]{1,0:T(1,128)}, u32[]{:S(2)}) copy-start(f32[1,128]{1,0:T(1,128)} %get-tuple-element.319) | copy-start | bytes 1540
  426.8 4.3 copy-start.7
  599.3 4.1 copy-start.12
  599.3 4.0 copy-start.17
  599.3 4.0 copy-start.18
  (25 other events, 48.2 us)
Sparse Core Ops, SparseCore 0:
  11.0 159.5 all-gather.3
  172.1 24.1 all-gather.5

commit v5 on v4

--- a/solution.py
+++ b/solution.py
@@ -1267,7 +1267,7 @@
             s_top, s_sum, t_top, t_sum, cross = carry
             lines = pl.ds(pl.multiple_of(index * wide, 64), wide)
             t_now = jnp.dot(head_ref[lines, :], t_turned[...], preferred_element_type=jnp.float32)
-            s_now = jnp.dot(table_ref[lines, :], p_turned[...], preferred_element_type=jnp.float32)
+            s_now = jnp.dot(table_ref[lines, 0:width], p_turned[...], preferred_element_type=jnp.float32)
             t_logits[back, lines, :] = t_now
             s_logits[back, lines, :] = s_now
             s_next = jnp.maximum(s_top, jnp.max(s_now, 0, keepdims=True))
@@ -1362,7 +1362,7 @@
     def grade(first):
         def chunk(index, carry):
             lines = pl.ds(pl.multiple_of(first + index * narrow, 64), narrow)
-            table = table_ref[lines, :]
+            table = table_ref[lines, 0:width]
             made = jnp.zeros((narrow, width), jnp.float32)
             for back in range(side):
                 row = rows_of[back]
@@ -1577,17 +1577,17 @@
     rest = value - high.astype(jnp.float32)
     middle = rest.astype(jnp.bfloat16)
     low = (rest - middle.astype(jnp.float32)).astype(jnp.bfloat16)
-    rows = g_ref.shape[0]
-    step = next(size for size in (192, 120, 8) if rows % size == 0)
+    rows = more_ref.shape[0]
     squares = jnp.sum(reduced_ref[...] * reduced_ref[...], 0, keepdims=True)
     squares = jnp.sum(squares, 1, keepdims=True)
-    line = lax.broadcasted_iota(jnp.int32, (step, value.shape[0]), 0)
-    for first in range(0, rows, step):
+    for first in range(0, rows, 384):
+        step = min(384, rows - first)
+        line = lax.broadcasted_iota(jnp.int32, (step, value.shape[0]), 0)
         marks = jnp.where(line + first == wanted_ref[...], 1.0, 0.0).astype(jnp.bfloat16)
         made = more_ref[first : first + step, :] + head_ref[first : first + step, :width]
         for term in (high, middle, low):
             made = made + jnp.dot(marks, term, preferred_element_type=jnp.float32)
-        g_ref[first : first + step, :] = made
+        g_ref[:, first : first + step] = made.T
         squares = squares + jnp.sum(jnp.sum(made * made, 0, keepdims=True), 1, keepdims=True)
     lane = lax.broadcasted_iota(jnp.int32, sent.shape, 1)
     note = jnp.where(lane == at, squares, note_ref[...])
@@ -1622,7 +1622,7 @@
     return pl.pallas_call(
         partial(finish_kernel, at),
         out_shape=(
-            jax.ShapeDtypeStruct(more.shape, more.dtype),
+            jax.ShapeDtypeStruct(more.shape[::-1], more.dtype),
             jax.ShapeDtypeStruct((count,) + note.shape, note.dtype),
         ),
         in_specs=[VMEM_SPEC] * 6,
@@ -1710,6 +1710,7 @@
     marks, asked = question(plan, 0, devices, extra)
     got, weights_all, token_blocks = entry(asked, pack(own_parts, line, block_rows)[0], table_low, 3)
     table_then = lax.optimization_barrier((table_low, got))[0]
+    table_then = jnp.pad(table_then, ((0, 0), (0, d_all_width(width) - width)))
     slice_part = lax.ppermute(table_then, BOTH, from_owner)
     wanted = got[:, 0, :SLOTS].reshape(-1)
     notes = got[:, 0, SLOTS : SLOTS + 2]
@@ -1891,7 +1892,7 @@
         small_local + 1,
         8,
     )
-    notes_all = notes_all[:, 0]
+    g_table, notes_all = g_table.T, notes_all[:, 0]
     small = notes_all[:, :small_local].reshape(-1)
     loss = jnp.sum(notes_all[:, small_local])
     norm = jnp.sqrt(jnp.sum(notes_all[:, small_local + 1]))

time: 623 us -> 622 us (level)
  local copies, waits for them, and re-layouts: 57.1 us -> 47.2 us
    unnamed x95 -> x100, local copies, waits for them, and re-layouts: 19.1 us -> 9.39 us
  transfers between devices with their start and end apart: 4 -> 4, of which waited for: 1 -> 1; matrix products, arithmetic and copies ran while one was open for 8% -> 7% of each run, Pallas kernels for 39% -> 39%
where the time goes in v5:
time: 622 us; the launch traced here: 613 us
  Pallas kernels  481 us (77%)
  local copies, waits for them, and re-layouts  47.2 us (8%)
  other arithmetic  37.7 us (6%)
  between operations  24.2 us (4%)
  starting transfers between devices  9.56 us (2%)
  matrix products  7.77 us (1%)
    pallas_call x1, Pallas kernels, reduce(): pl.pallas_call(partial(reduce_kernel, plan, len(parts)), out_shape=(jax.S...  127 us
    pallas_call x1, Pallas kernels, head(): pl.pallas_call(partial(head_kernel, groups, pair, denom), out_shape=tuple...  98.1 us
    pallas_call x2, Pallas kernels, student_backward(): pl.pallas_call(partial(back_kernel, bool(last), bool(first_layer)), out_s...  76.2 us
    pallas_call x1, Pallas kernels, entry(): pl.pallas_call(entry_kernel, out_shape=(jax.ShapeDtypeStruct(asked.shape,...  74.4 us
    pallas_call x1, Pallas kernels, teacher_forward(): pl.pallas_call(partial(teacher_kernel, denom), out_shape=made, in_specs=[...  45.8 us
    pallas_call x1, Pallas kernels, student_forward(): pl.pallas_call(partial(student_kernel, plan, layers), out_shape=made, in_...  45.3 us
    pallas_call x1, Pallas kernels, finish(): pl.pallas_call(partial(finish_kernel, at), out_shape=(jax.ShapeDtypeStruc...  14.8 us
  transfers between devices with their start and end apart: 4, of which 1 were waited for; matrix products, arithmetic and copies ran while one was open for 7% of the time, Pallas kernels for 39%

profile of v5, /device:TPU:0, one launch (start us, length us, event | category | flops | bytes accessed | tf_op | source)
XLA Modules:
  0.0 613.1 jit_solution(9639757964776510296)
XLA Ops:
  7.3 2.2 reshape.587
  13.5 2.4 convert_reduce_fusion
  16.5 2.1 select_reduce_fusion.2
  24.1 74.4 %shard_map.418 = (s32[32,1,128]{2,1,0:T(1,128)S(1)}, bf16[32,256,312]{2,1,0:T(8,128)(2,1)S(1)}, bf16[32,48,312]{2,1,0:T(8,128)(2,1)S(1)}) custom-call(s32[32,1,128]{2,1,0:T(1,128)S(1)} %add_add_fusion.2.ask_ref, bf16[256,312]{1,0:T(8,128)(2,1)S(1)} %maximum_bitcast_fusion.w_ref, bf16[960,312]{1,0:T(8,128)(2,1)S(1)} %copy.120.table_ref), custom_call_target="tpu_custom_call" | custom-call | tf_op jit(solution)/shard_map/pallas_call | solution.py:298
  98.6 3.5 copy-done.4
  103.0 7.4 %collective-permute-start = (bf16[960,384]{1,0:T(8,128)(2,1)}, bf16[960,384]{1,0:T(8,128)(2,1)}, u32[]{:S(2)}, u32[]{:S(2)}) collective-permute-start(bf16[960,384]{1,0:T(8,128)(2,1)} %pad.17), channel_id=1, source_target_pairs={{0,0},{4,1},{8,2},{12,3},{16,4},{20,5},{24,6},{28,7},{1,8},{5,9},{... | collective-permute-start | bytes 2211848 | tf_op jit(solution)/shard_map/ppermute | solution.py:1714
  114.6 2.5 fusion.21
  117.1 2.0 while.22
  124.8 45.3 %shard_map.419 = (bf16[3,312,312]{2,1,0:T(8,128)(2,1)}, bf16[312,312]{1,0:T(8,128)(2,1)}, bf16[312,1280]{1,0:T(8,128)(2,1)}, bf16[1280,312]{1,0:T(8,128)(2,1)}, ...) custom-call(f32[1024,312]{1,0:T(8,128)} %slice.280.token_ref, ...), custom_call_target="tpu_custom_call" | custom-call | flops 8000000000 | bytes 40000000 | tf_op jit(solution)/shard_map/pallas_call | solution.py:979
  170.0 3.1 all-gather.3.cloned.1.call-done
  179.5 45.8 %shard_map.420 = (f32[1024,1536]{1,0:T(8,128)}, f32[1024,312]{1,0:T(8,128)}, f32[1024,312]{1,0:T(8,128)}, f32[768,312]{1,0:T(8,128)}, f32[1,768]{1,0:T(1,128)}, ...) custom-call(bf16[1024,768]{1,0:T(8,128)(2,1)} %bitcast.148, ...), custom_call_target="tpu_custom_call" | custom-call | flops 20000000000 | bytes 25000000 | tf_op jit(solution)/shard_map/pallas_call | solution.py:775
  229.0 98.1 %shard_map.421 = (f32[160,384]{1,0:T(8,128)}, f32[8,640]{1,0:T(8,128)}, f32[960,384]{1,0:T(8,128)}) custom-call(bf16[8,160,312]{2,1,0:T(8,128)(2,1)} %get-tuple-element.259.p_all, bf16[160,768]{1,0:T(8,128)(2,1)} %get-tuple-element.260.t_ref, bf16[3840,384]{1,0:T(8,128)(2,1)} %all-gather.5.cloned.1.call-done.table_ref, bf16[3840,768]{1,0:T(8,128)(2,1)} %head_ref.1), custom_call_target="tpu_custom_call" | custom-call | tf_op jit(solution)/shard_map/pallas_call | solution.py:1471
  327.1 2.0 collective-permute-start.1
  331.8 2.0 fusion.27.grad_ref
  333.9 38.9 %shard_map.422 = (f32[1024,312]{1,0:T(8,128)}, f32[312,312]{1,0:T(8,128)}, f32[312,312]{1,0:T(8,128)}, f32[312,312]{1,0:T(8,128)}, f32[312,312]{1,0:T(8,128)}, /...) custom-call(f32[1024,312]{1,0:T(8,128)} %fusion.27.grad_ref, ...), custom_call_target="tpu_custom_call" | custom-call | flops 1000000000 | bytes 4000000 | tf_op jit(solution)/shard_map/pallas_call | solution.py:1163
  372.8 37.3 %shard_map.423 = (f32[1024,312]{1,0:T(8,128)}, f32[312,312]{1,0:T(8,128)}, f32[312,312]{1,0:T(8,128)}, f32[312,312]{1,0:T(8,128)}, f32[312,312]{1,0:T(8,128)}, /...) custom-call(f32[1024,312]{1,0:T(8,128)} %get-tuple-element.277.grad_, ...), custom_call_target="tpu_custom_call" | custom-call | flops 1000000000 | bytes 4000000 | tf_op jit(solution)/shard_map/pallas_call | solution.py:1163
  417.6 1.9 reduce-precision_convert_fusion.3
  420.7 4.3 fusion.20
  426.8 3.0 copy.130
  429.8 126.8 %shard_map.424 = (f32[264,312]{1,0:T(8,128)}, f32[32,48,312]{2,1,0:T(8,128)}) custom-call(f32[312,312]{1,0:T(8,128)} %get-tuple-element.292.refs_0_, f32[312,312]{1,0:T(8,128)} %get-tuple-element.293.refs_1_, f32[312,312]{1,0:T(8,128)} %get-tuple-element.294.refs_2_, f32[312,312]{1,0:T(8,128)} %get-tuple-element.295.refs_3_, ...), custom_call_target="tpu_custom_call" | custom-call | tf_op jit(solution)/shard_map/pallas_call | solution.py:490
  562.9 1.8 copy.131.more_ref
  566.5 14.8 %shard_map.425 = (f32[312,960]{1,0:T(8,128)S(1)}, f32[32,1,384]{2,1,0:T(1,128)S(1)}) custom-call(f32[1536,312]{1,0:T(8,128)S(1)} %bitcast.116, s32[1,1536]{1,0:T(1,128)S(1)} %broadcast_in_dim_reshape_squeeze.3.wanted_ref, f32[960,312]{1,0:T(8,128)S(1)} %copy.131.more_ref, f32[960,384]{1,0:T(8,128)S(1)} %collective-permute-done.1.head_ref, ...), custom_call_target="tpu_custom_call" | custom-call | tf_op jit(solution)/shard_map/pallas_call | solution.py:1622
  596.7 4.4 multiply_subtract_fusion
  601.8 2.0 multiply_subtract_fusion.1
  (231 shorter events, 61.0 us)
Async XLA Ops:
  7.2 5.2 copy-start.36
  7.2 12.2 %copy-start.34 = (s32[2,4,128]{2,1,0:T(4,128)S(1)}, s32[2,4,128]{2,1,0:T(4,128)}, u32[]{:S(2)}) copy-start(s32[2,4,128]{2,1,0:T(4,128)} %param.32) | copy-start | bytes 12292
  7.2 12.2 %copy-start.21 = (s32[2,4,128]{2,1,0:T(4,128)S(1)}, s32[2,4,128]{2,1,0:T(4,128)}, u32[]{:S(2)}) copy-start(s32[2,4,128]{2,1,0:T(4,128)} %param.33) | copy-start | bytes 12292
  7.2 165.9 %all-gather.3.cloned.1.call-start = ((), (), s32[]{:S(2)}) async-start(), calls=%async_computation | async-start | bytes 14598144 | tf_op jit(solution)/shard_map/all_gather | solution.py:1695
  9.5 14.0 %copy-start.7 = (f32[960,312]{0,1:T(8,128)S(1)}, f32[960,312]{0,1:T(8,128)}, u32[]{:S(2)}) copy-start(f32[960,312]{0,1:T(8,128)} %param.40) | copy-start | bytes 3594244
  9.5 219.5 %all-gather.5.cloned.1.call-start = ((), (), s32[]{:S(2)}) async-start(), calls=%async_computation.1 | async-start | bytes 3686400 | tf_op jit(solution)/shard_map/all_gather | solution.py:1767
  13.5 7.7 %copy-start.38 = (pred[1184]{0:T(1024)(128)(4,1)}, pred[1184]{0:T(1024)(128)(4,1)S(1)}, u32[]{:S(2)}) copy-start(pred[1184]{0:T(1024)(128)(4,1)S(1)} %iota_compare_fusion.19) | copy-start | bytes 3556
  23.9 89.3 %copy-start.17 = (f32[2,3696]{1,0:T(2,128)S(1)}, f32[2,3696]{1,0:T(2,128)}, u32[]{:S(2)}) copy-start(f32[2,3696]{1,0:T(2,128)} %param.52) | copy-start | bytes 88708
  103.0 67.0 %collective-permute-start = (bf16[960,384]{1,0:T(8,128)(2,1)}, bf16[960,384]{1,0:T(8,128)(2,1)}, u32[]{:S(2)}, u32[]{:S(2)}) collective-permute-start(bf16[960,384]{1,0:T(8,128)(2,1)} %pad.17), channel_id=1, source_target_pairs={{0,0},{4,1},{8,2},{12,3},{16,4},{20,5},{24,6},{28,7},{1,8},{5,9},{... | collective-permute-start | bytes 2211848 | tf_op jit(solution)/shard_map/ppermute | solution.py:1714
  124.7 48.4 %copy-start.23 = (f32[1392]{0:T(1024)S(1)}, f32[1392]{0:T(1024)}, u32[]{:S(2)}) copy-start(f32[1392]{0:T(1024)} %param.55) | copy-start | bytes 16708
  124.7 48.5 %copy-start.35 = (s32[2,4,128]{2,1,0:T(4,128)S(1)}, s32[2,4,128]{2,1,0:T(4,128)}, u32[]{:S(2)}) copy-start(s32[2,4,128]{2,1,0:T(4,128)} %param.32) | copy-start | bytes 12292
  124.7 48.7 %copy-start.33 = (s32[2,4,20]{2,1,0:T(4,128)S(1)}, s32[2,4,20]{2,1,0:T(4,128)}, u32[]{:S(2)}) copy-start(s32[2,4,20]{2,1,0:T(4,128)} %param.34) | copy-start | bytes 1924
  124.7 48.9 %copy-start.32 = (bf16[9984]{0:T(1024)(128)(2,1)S(1)}, bf16[9984]{0:T(1024)(128)(2,1)}, u32[]{:S(2)}) copy-start(bf16[9984]{0:T(1024)(128)(2,1)} %param.38) | copy-start | bytes 59908
  327.1 90.5 %collective-permute-start.1 = (f32[960,384]{1,0:T(8,128)}, f32[960,384]{1,0:T(8,128)S(1)}, u32[]{:S(2)}, u32[]{:S(2)}) collective-permute-start(f32[960,384]{1,0:T(8,128)} %get-tuple-element.313), channel_id=1, source_target_pairs={{0,0},{1,4},{2,8},{3,12},{4,16},{5,20},{6,24},{7,28},{8,1},{9,5},{... | collective-permute-start | bytes 4423688 | tf_op jit(solution)/shard_map/ppermute | solution.py:1812
  372.8 38.9 %copy-start.27 = (f32[8,312]{1,0:T(8,128)S(1)}, f32[8,312]{1,0:T(8,128)}, u32[]{:S(2)}) copy-start(f32[8,312]{1,0:T(8,128)} %get-tuple-element.308) | copy-start | bytes 29956
  372.8 39.8 %copy-start.44 = (f32[1,1280]{1,0:T(1,128)S(1)}, f32[1,1280]{1,0:T(1,128)}, u32[]{:S(2)}) copy-start(f32[1,1280]{1,0:T(1,128)} %get-tuple-element.309) | copy-start | bytes 15364
  372.8 41.4 %copy-start.46 = (f32[1,128]{1,0:T(1,128)S(1)}, f32[1,128]{1,0:T(1,128)}, u32[]{:S(2)}) copy-start(f32[1,128]{1,0:T(1,128)} %get-tuple-element.319) | copy-start | bytes 1540
  586.2 6.1 %copy-start.31 = (f32[4,312]{1,0:T(4,128)S(1)}, f32[4,312]{1,0:T(4,128)}, u32[]{:S(2)}) copy-start(f32[4,312]{1,0:T(4,128)} %param.43) | copy-start | bytes 14980
  587.2 8.0 %copy-start.24 = (f32[1392]{0:T(1024)S(1)}, f32[1392]{0:T(1024)}, u32[]{:S(2)}) copy-start(f32[1392]{0:T(1024)} %param.55) | copy-start | bytes 16708
  587.2 8.0 %copy-start.37 = (f32[1392]{0:T(1024)S(1)}, f32[1392]{0:T(1024)}, u32[]{:S(2)}) copy-start(f32[1392]{0:T(1024)} %param.57) | copy-start | bytes 16708
  587.2 9.4 %copy-start.3 = (f32[312,960]{1,0:T(8,128)S(1)}, f32[312,960]{1,0:T(8,128)}, u32[]{:S(2)}) copy-start(f32[312,960]{1,0:T(8,128)} %copy-done.2) | copy-start | bytes 3594244
  587.3 9.3 %copy-start.8 = (f32[960,312]{0,1:T(8,128)S(1)}, f32[960,312]{0,1:T(8,128)}, u32[]{:S(2)}) copy-start(f32[960,312]{0,1:T(8,128)} %param.40) | copy-start | bytes 3594244
  596.6 5.2 copy-start.11
  596.6 5.2 copy-start.14
  (30 other events, 93.4 us)
Sparse Core Ops, SparseCore 0:
  11.0 162.0 all-gather.2
  174.7 27.1 all-gather.4

commit v6 on v5

--- a/solution.py
+++ b/solution.py
@@ -1287,6 +1287,18 @@
         for index, value in enumerate(made):
             stats[me, at_y, index : index + 1, :] = value
 
+    def stat_copy(step, back):
+        at_y = (y + side - back) % side
+        rank = back * groups + step
+        return pltpu.make_async_remote_copy(
+            stats.at[me, at_y],
+            stats.at[me, at_y],
+            stat_send.at[rank],
+            stat_recv.at[rank],
+            device_id=(dp, (me + step) % groups),
+            device_id_type=MESH,
+        )
+
     t_all[me] = t_ref[...]
     for way in (1, -1):
         made, wanted = z_copies(0, way, False)
@@ -1312,6 +1324,9 @@
             for step in range(z_size):
                 received(y_copies(back, step, step * side + (y + side - back) % side))
         measure(back)
+        if back < side - 1:
+            for step in range(1, groups):
+                stat_copy(step, back).start()
     for step in range(z_size - 1):
         for way in (1, -1):
             made, wanted = z_copies(step, way, False)
@@ -1320,20 +1335,11 @@
         for step in range(z_size):
             sent(y_copies(back, step, step * side + y))
 
-    def stat_copy(step):
-        return pltpu.make_async_remote_copy(
-            stats.at[me],
-            stats.at[me],
-            stat_send.at[step],
-            stat_recv.at[step],
-            device_id=(dp, (me + step) % groups),
-            device_id_type=MESH,
-        )
-
     for step in range(1, groups):
-        stat_copy(step).start()
+        stat_copy(step, side - 1).start()
     for step in range(1, groups):
-        stat_copy(step).wait_recv()
+        for back in range(side):
+            stat_copy(step, back).wait_recv()
     for back in range(side):
         at_y = (y + side - back) % side
         parts = [stats[other, at_y] for other in range(groups)]
@@ -1444,7 +1450,8 @@
     out = pltpu.make_async_copy(rows_at(kept, part), w_ref, out_sem)
     out.start()
     for step in range(1, groups):
-        stat_copy(step).wait_send()
+        for back in range(side):
+            stat_copy(step, back).wait_send()
         d_copy(step).wait_send()
     for copy in given:
         copy.wait_send()
@@ -1484,7 +1491,8 @@
             pltpu.VMEM((3, vocab // 4, half) if pair else (1, 8, 128), full),
             pltpu.VMEM((side, half, across), full),
             *[dma((2 * z_size + (side - 1) * z_size,))] * 2,
-            *[dma((groups,))] * 4,
+            *[dma((side * groups,))] * 2,
+            *[dma((groups,))] * 2,
             *[dma((3,))] * 2,
             dma,
         ],

time: 622 us -> 621 us (level)
  no operation moved by 1% of the time
where the time goes in v6:
time: 621 us; the launch traced here: 612 us
  Pallas kernels  480 us (77%)
  local copies, waits for them, and re-layouts  47.1 us (8%)
  other arithmetic  37.7 us (6%)
  between operations  24.2 us (4%)
  starting transfers between devices  9.56 us (2%)
  matrix products  7.78 us (1%)
    pallas_call x1, Pallas kernels, reduce(): pl.pallas_call(partial(reduce_kernel, plan, len(parts)), out_shape=(jax.S...  126 us
    pallas_call x1, Pallas kernels, head(): pl.pallas_call(partial(head_kernel, groups, pair, denom), out_shape=tuple...  97.8 us
    pallas_call x2, Pallas kernels, student_backward(): pl.pallas_call(partial(back_kernel, bool(last), bool(first_layer)), out_s...  76.2 us
    pallas_call x1, Pallas kernels, entry(): pl.pallas_call(entry_kernel, out_shape=(jax.ShapeDtypeStruct(asked.shape,...  74.4 us
    pallas_call x1, Pallas kernels, teacher_forward(): pl.pallas_call(partial(teacher_kernel, denom), out_shape=made, in_specs=[...  45.8 us
    pallas_call x1, Pallas kernels, student_forward(): pl.pallas_call(partial(student_kernel, plan, layers), out_shape=made, in_...  45.3 us
    pallas_call x1, Pallas kernels, finish(): pl.pallas_call(partial(finish_kernel, at), out_shape=(jax.ShapeDtypeStruc...  14.8 us
  transfers between devices with their start and end apart: 4, of which 1 were waited for; matrix products, arithmetic and copies ran while one was open for 7% of the time, Pallas kernels for 39%

profile of v6, /device:TPU:0, one launch (start us, length us, event | category | flops | bytes accessed | tf_op | source)
XLA Modules:
  0.0 612.0 jit_solution(3408708006529843785)
XLA Ops:
  7.3 2.2 reshape.587
  13.5 2.4 convert_reduce_fusion
  16.5 2.1 select_reduce_fusion.2
  24.1 74.4 %shard_map.418 = (s32[32,1,128]{2,1,0:T(1,128)S(1)}, bf16[32,256,312]{2,1,0:T(8,128)(2,1)S(1)}, bf16[32,48,312]{2,1,0:T(8,128)(2,1)S(1)}) custom-call(s32[32,1,128]{2,1,0:T(1,128)S(1)} %add_add_fusion.2.ask_ref, bf16[256,312]{1,0:T(8,128)(2,1)S(1)} %maximum_bitcast_fusion.w_ref, bf16[960,312]{1,0:T(8,128)(2,1)S(1)} %copy.120.table_ref), custom_call_target="tpu_custom_call" | custom-call | tf_op jit(solution)/shard_map/pallas_call | solution.py:298
  98.6 3.5 copy-done.4
  103.0 7.4 %collective-permute-start = (bf16[960,384]{1,0:T(8,128)(2,1)}, bf16[960,384]{1,0:T(8,128)(2,1)}, u32[]{:S(2)}, u32[]{:S(2)}) collective-permute-start(bf16[960,384]{1,0:T(8,128)(2,1)} %pad.17), channel_id=1, source_target_pairs={{0,0},{4,1},{8,2},{12,3},{16,4},{20,5},{24,6},{28,7},{1,8},{5,9},{... | collective-permute-start | bytes 2211848 | tf_op jit(solution)/shard_map/ppermute | solution.py:1722
  114.6 2.5 fusion.21
  117.1 2.0 while.22
  124.8 45.3 %shard_map.419 = (bf16[3,312,312]{2,1,0:T(8,128)(2,1)}, bf16[312,312]{1,0:T(8,128)(2,1)}, bf16[312,1280]{1,0:T(8,128)(2,1)}, bf16[1280,312]{1,0:T(8,128)(2,1)}, ...) custom-call(f32[1024,312]{1,0:T(8,128)} %slice.280.token_ref, ...), custom_call_target="tpu_custom_call" | custom-call | flops 8000000000 | bytes 40000000 | tf_op jit(solution)/shard_map/pallas_call | solution.py:979
  170.0 3.1 all-gather.3.cloned.1.call-done
  179.5 45.8 %shard_map.420 = (f32[1024,1536]{1,0:T(8,128)}, f32[1024,312]{1,0:T(8,128)}, f32[1024,312]{1,0:T(8,128)}, f32[768,312]{1,0:T(8,128)}, f32[1,768]{1,0:T(1,128)}, ...) custom-call(bf16[1024,768]{1,0:T(8,128)(2,1)} %bitcast.148, ...), custom_call_target="tpu_custom_call" | custom-call | flops 20000000000 | bytes 25000000 | tf_op jit(solution)/shard_map/pallas_call | solution.py:775
  229.0 97.8 %shard_map.421 = (f32[160,384]{1,0:T(8,128)}, f32[8,640]{1,0:T(8,128)}, f32[960,384]{1,0:T(8,128)}) custom-call(bf16[8,160,312]{2,1,0:T(8,128)(2,1)} %get-tuple-element.259.p_all, bf16[160,768]{1,0:T(8,128)(2,1)} %get-tuple-element.260.t_ref, bf16[3840,384]{1,0:T(8,128)(2,1)} %all-gather.5.cloned.1.call-done.table_ref, bf16[3840,768]{1,0:T(8,128)(2,1)} %head_ref.1), custom_call_target="tpu_custom_call" | custom-call | tf_op jit(solution)/shard_map/pallas_call | solution.py:1478
  326.8 2.0 collective-permute-start.1
  331.5 2.0 fusion.27.grad_ref
  333.6 38.9 %shard_map.422 = (f32[1024,312]{1,0:T(8,128)}, f32[312,312]{1,0:T(8,128)}, f32[312,312]{1,0:T(8,128)}, f32[312,312]{1,0:T(8,128)}, f32[312,312]{1,0:T(8,128)}, /...) custom-call(f32[1024,312]{1,0:T(8,128)} %fusion.27.grad_ref, ...), custom_call_target="tpu_custom_call" | custom-call | flops 1000000000 | bytes 4000000 | tf_op jit(solution)/shard_map/pallas_call | solution.py:1163
  372.6 37.3 %shard_map.423 = (f32[1024,312]{1,0:T(8,128)}, f32[312,312]{1,0:T(8,128)}, f32[312,312]{1,0:T(8,128)}, f32[312,312]{1,0:T(8,128)}, f32[312,312]{1,0:T(8,128)}, /...) custom-call(f32[1024,312]{1,0:T(8,128)} %get-tuple-element.277.grad_, ...), custom_call_target="tpu_custom_call" | custom-call | flops 1000000000 | bytes 4000000 | tf_op jit(solution)/shard_map/pallas_call | solution.py:1163
  417.4 1.9 reduce-precision_convert_fusion.3
  420.4 4.3 fusion.20
  426.5 3.0 copy.130
  429.5 125.9 %shard_map.424 = (f32[264,312]{1,0:T(8,128)}, f32[32,48,312]{2,1,0:T(8,128)}) custom-call(f32[312,312]{1,0:T(8,128)} %get-tuple-element.292.refs_0_, f32[312,312]{1,0:T(8,128)} %get-tuple-element.293.refs_1_, f32[312,312]{1,0:T(8,128)} %get-tuple-element.294.refs_2_, f32[312,312]{1,0:T(8,128)} %get-tuple-element.295.refs_3_, ...), custom_call_target="tpu_custom_call" | custom-call | tf_op jit(solution)/shard_map/pallas_call | solution.py:490
  561.8 1.8 copy.131.more_ref
  565.4 14.8 %shard_map.425 = (f32[312,960]{1,0:T(8,128)S(1)}, f32[32,1,384]{2,1,0:T(1,128)S(1)}) custom-call(f32[1536,312]{1,0:T(8,128)S(1)} %bitcast.116, s32[1,1536]{1,0:T(1,128)S(1)} %broadcast_in_dim_reshape_squeeze.3.wanted_ref, f32[960,312]{1,0:T(8,128)S(1)} %copy.131.more_ref, f32[960,384]{1,0:T(8,128)S(1)} %collective-permute-done.1.head_ref, ...), custom_call_target="tpu_custom_call" | custom-call | tf_op jit(solution)/shard_map/pallas_call | solution.py:1630
  595.5 4.4 multiply_subtract_fusion
  600.6 2.0 multiply_subtract_fusion.1
  (231 shorter events, 61.0 us)
Async XLA Ops:
  7.2 5.2 copy-start.36
  7.2 12.2 %copy-start.34 = (s32[2,4,128]{2,1,0:T(4,128)S(1)}, s32[2,4,128]{2,1,0:T(4,128)}, u32[]{:S(2)}) copy-start(s32[2,4,128]{2,1,0:T(4,128)} %param.32) | copy-start | bytes 12292
  7.2 12.2 %copy-start.21 = (s32[2,4,128]{2,1,0:T(4,128)S(1)}, s32[2,4,128]{2,1,0:T(4,128)}, u32[]{:S(2)}) copy-start(s32[2,4,128]{2,1,0:T(4,128)} %param.33) | copy-start | bytes 12292
  7.2 165.9 %all-gather.3.cloned.1.call-start = ((), (), s32[]{:S(2)}) async-start(), calls=%async_computation | async-start | bytes 14598144 | tf_op jit(solution)/shard_map/all_gather | solution.py:1703
  9.5 14.0 %copy-start.7 = (f32[960,312]{0,1:T(8,128)S(1)}, f32[960,312]{0,1:T(8,128)}, u32[]{:S(2)}) copy-start(f32[960,312]{0,1:T(8,128)} %param.40) | copy-start | bytes 3594244
  9.5 219.5 %all-gather.5.cloned.1.call-start = ((), (), s32[]{:S(2)}) async-start(), calls=%async_computation.1 | async-start | bytes 3686400 | tf_op jit(solution)/shard_map/all_gather | solution.py:1775
  13.5 7.7 %copy-start.38 = (pred[1184]{0:T(1024)(128)(4,1)}, pred[1184]{0:T(1024)(128)(4,1)S(1)}, u32[]{:S(2)}) copy-start(pred[1184]{0:T(1024)(128)(4,1)S(1)} %iota_compare_fusion.19) | copy-start | bytes 3556
  23.9 89.3 %copy-start.17 = (f32[2,3696]{1,0:T(2,128)S(1)}, f32[2,3696]{1,0:T(2,128)}, u32[]{:S(2)}) copy-start(f32[2,3696]{1,0:T(2,128)} %param.52) | copy-start | bytes 88708
  103.0 67.0 %collective-permute-start = (bf16[960,384]{1,0:T(8,128)(2,1)}, bf16[960,384]{1,0:T(8,128)(2,1)}, u32[]{:S(2)}, u32[]{:S(2)}) collective-permute-start(bf16[960,384]{1,0:T(8,128)(2,1)} %pad.17), channel_id=1, source_target_pairs={{0,0},{4,1},{8,2},{12,3},{16,4},{20,5},{24,6},{28,7},{1,8},{5,9},{... | collective-permute-start | bytes 2211848 | tf_op jit(solution)/shard_map/ppermute | solution.py:1722
  124.7 48.4 %copy-start.23 = (f32[1392]{0:T(1024)S(1)}, f32[1392]{0:T(1024)}, u32[]{:S(2)}) copy-start(f32[1392]{0:T(1024)} %param.55) | copy-start | bytes 16708
  124.7 48.5 %copy-start.35 = (s32[2,4,128]{2,1,0:T(4,128)S(1)}, s32[2,4,128]{2,1,0:T(4,128)}, u32[]{:S(2)}) copy-start(s32[2,4,128]{2,1,0:T(4,128)} %param.32) | copy-start | bytes 12292
  124.7 48.7 %copy-start.33 = (s32[2,4,20]{2,1,0:T(4,128)S(1)}, s32[2,4,20]{2,1,0:T(4,128)}, u32[]{:S(2)}) copy-start(s32[2,4,20]{2,1,0:T(4,128)} %param.34) | copy-start | bytes 1924
  124.7 48.9 %copy-start.32 = (bf16[9984]{0:T(1024)(128)(2,1)S(1)}, bf16[9984]{0:T(1024)(128)(2,1)}, u32[]{:S(2)}) copy-start(bf16[9984]{0:T(1024)(128)(2,1)} %param.38) | copy-start | bytes 59908
  326.8 90.6 %collective-permute-start.1 = (f32[960,384]{1,0:T(8,128)}, f32[960,384]{1,0:T(8,128)S(1)}, u32[]{:S(2)}, u32[]{:S(2)}) collective-permute-start(f32[960,384]{1,0:T(8,128)} %get-tuple-element.313), channel_id=1, source_target_pairs={{0,0},{1,4},{2,8},{3,12},{4,16},{5,20},{6,24},{7,28},{8,1},{9,5},{... | collective-permute-start | bytes 4423688 | tf_op jit(solution)/shard_map/ppermute | solution.py:1820
  372.5 38.9 %copy-start.27 = (f32[8,312]{1,0:T(8,128)S(1)}, f32[8,312]{1,0:T(8,128)}, u32[]{:S(2)}) copy-start(f32[8,312]{1,0:T(8,128)} %get-tuple-element.308) | copy-start | bytes 29956
  372.5 39.8 %copy-start.44 = (f32[1,1280]{1,0:T(1,128)S(1)}, f32[1,1280]{1,0:T(1,128)}, u32[]{:S(2)}) copy-start(f32[1,1280]{1,0:T(1,128)} %get-tuple-element.309) | copy-start | bytes 15364
  372.5 41.4 %copy-start.46 = (f32[1,128]{1,0:T(1,128)S(1)}, f32[1,128]{1,0:T(1,128)}, u32[]{:S(2)}) copy-start(f32[1,128]{1,0:T(1,128)} %get-tuple-element.319) | copy-start | bytes 1540
  585.1 6.1 %copy-start.31 = (f32[4,312]{1,0:T(4,128)S(1)}, f32[4,312]{1,0:T(4,128)}, u32[]{:S(2)}) copy-start(f32[4,312]{1,0:T(4,128)} %param.43) | copy-start | bytes 14980
  586.1 8.0 %copy-start.24 = (f32[1392]{0:T(1024)S(1)}, f32[1392]{0:T(1024)}, u32[]{:S(2)}) copy-start(f32[1392]{0:T(1024)} %param.55) | copy-start | bytes 16708
  586.1 8.0 %copy-start.37 = (f32[1392]{0:T(1024)S(1)}, f32[1392]{0:T(1024)}, u32[]{:S(2)}) copy-start(f32[1392]{0:T(1024)} %param.57) | copy-start | bytes 16708
  586.1 9.4 %copy-start.3 = (f32[312,960]{1,0:T(8,128)S(1)}, f32[312,960]{1,0:T(8,128)}, u32[]{:S(2)}) copy-start(f32[312,960]{1,0:T(8,128)} %copy-done.2) | copy-start | bytes 3594244
  586.1 9.3 %copy-start.8 = (f32[960,312]{0,1:T(8,128)S(1)}, f32[960,312]{0,1:T(8,128)}, u32[]{:S(2)}) copy-start(f32[960,312]{0,1:T(8,128)} %param.40) | copy-start | bytes 3594244
  595.5 5.2 copy-start.11
  595.5 5.2 copy-start.14
  (30 other events, 93.4 us)
Sparse Core Ops, SparseCore 0:
  11.0 162.0 all-gather.2
  174.7 27.1 all-gather.4
